TPU v7x, 128 devices: a whole 4x4x4 slice. The times are simulated.
128 devices in a mesh: dom: 128 (over y, z, x, core).
Axes of the slice: x: 4, y: 4, z: 4, core: 2. Of those that a mesh axis runs over, the one named last changes fastest.
Arguments:
- residual_in: bfloat16 [1024, 32, 1024], P('dom'), may hold values from -6 to 6
- local_inverse: bfloat16 [1024, 1024, 1024], P('dom'), may hold values from -1 to 3, as said below
- coarse_basis: bfloat16 [1024, 16, 1024], P('dom'), may hold values from -0.25 to 0.25
- coarse_inverse: float32 [8192, 8192], P('dom'), may hold values from -1 to 3, as said below
- multiplicity: int32 [1024, 1024], P('dom'), may hold values from 1 to 2, as said below
- iface_len: int32 [1024], P('dom'), may hold values from 1 to 256, as said below
- iface_dof: int32 [1024, 256], P('dom'), may hold values from 0 to 131071, as said below
- coarse_map: int32 [1024, 16], P('dom'), may hold values from 0 to 8191
Outputs:
- first_apply: float32 [1024, 32, 1024], P('dom')
- second_apply: float32 [1024, 32, 1024], P('dom')
Inputs may be any that keep to these rules, and one draw needn't show every extreme that they name: `coarse_inverse`: symmetric; diagonal entries dominate. `local_inverse`: diagonal entries dominate. `iface_dof`: subdomain i lies on device i // 8. The live entries of a row are distinct and each is owned (index // 1024) by the row's own device or by the device before it, cyclically; every live index is named by exactly two rows. Dead entries name an index owned by the row's own device. `multiplicity`: 2 on the first iface_len[i] entries of row i, 1 on the others. `iface_len`: the busiest devices carry about twice the mean.
All inputs are finite; a program needn't handle non-finite values.
Results may differ from a plain program's by a relative error of at most 0.00083.
Values sent between devices are 32-bit elements; how exact they have to be, the bound alone decides.
No kernel may reach another device: no remote copies, remote signals or barrier semaphores. Data moves between devices by JAX's collectives and lax.ppermute only.
A program may use at most 128 MiB of HBM per device.

v0:
```python
import jax
import jax.numpy as jnp
from jax import lax
from jax.sharding import PartitionSpec as P


def from_behind(value, axis, steps):
    count = lax.axis_size(axis)
    pairs = [(source, (source + steps) % count) for source in range(count)]
    return lax.ppermute(value, axis, pairs)


def precondition(
    values, local_inverse, coarse_basis, coarse_rows, weights, live, iface_dof, coarse_map
):
    sub_count = values.shape[0]
    cases = values.shape[1]
    coarse_order = coarse_rows.shape[1]
    scaled = (values * weights[:, None, :]).astype(jnp.bfloat16)
    coarse_part = jnp.einsum(
        "srl,skl->srk", scaled, coarse_basis, preferred_element_type=jnp.float32
    )
    flat_part = jnp.transpose(coarse_part, (1, 0, 2)).reshape(cases, -1)
    one_hot = (
        coarse_map.reshape(-1)[:, None] == jnp.arange(coarse_order, dtype=jnp.int32)[None, :]
    ).astype(jnp.float32)
    local_rhs = jnp.dot(flat_part, one_hot, precision=lax.Precision.HIGHEST)
    coarse_rhs = lax.psum(local_rhs, "dom")
    own_sol = jnp.dot(coarse_rhs, coarse_rows.T, precision=lax.Precision.HIGHEST)
    coarse_sol = lax.all_gather(own_sol, "dom", axis=1, tiled=True)
    looked = jnp.dot(coarse_sol, one_hot.T, precision=lax.Precision.HIGHEST).reshape(
        cases, sub_count, -1
    )
    correction = jnp.einsum(
        "rsk,skl->srl", looked, coarse_basis.astype(jnp.float32), precision=lax.Precision.HIGHEST
    )
    combined = (
        jnp.einsum("srl,slm->srm", scaled, local_inverse, preferred_element_type=jnp.float32)
        + correction
    )
    iface_width = iface_dof.shape[1]
    contrib = combined[:, :, :iface_width] * weights[:, None, :iface_width] * live[:, None, :]
    flat_contrib = jnp.transpose(contrib, (1, 0, 2)).reshape(cases, -1)
    own_width = sub_count * iface_width // 2
    device = lax.axis_index("dom")
    owner = iface_dof // own_width
    outside = (owner != device).astype(jnp.int32)
    position = (outside * own_width + (iface_dof - owner * own_width)).reshape(-1)
    local_sum = jnp.zeros((cases, 2 * own_width), jnp.float32).at[:, position].add(flat_contrib)
    arrived = from_behind(local_sum[:, own_width:], "dom", -1)
    owned_sum = local_sum[:, :own_width] + arrived
    from_left = from_behind(owned_sum, "dom", 1)
    both = jnp.concatenate([owned_sum, from_left], axis=1)
    fetched = jnp.take(both, position, axis=1).reshape(cases, sub_count, iface_width)
    fetched = jnp.transpose(fetched, (1, 0, 2))
    head = jnp.where(live[:, None, :] > 0, fetched, combined[:, :, :iface_width])
    return jnp.concatenate([head, combined[:, :, iface_width:]], axis=2)


def local(
    residual_in,
    local_inverse,
    coarse_basis,
    coarse_inverse,
    multiplicity,
    iface_len,
    iface_dof,
    coarse_map,
):
    weights = 1.0 / multiplicity.astype(jnp.float32)
    iface_width = iface_dof.shape[1]
    live = (jnp.arange(iface_width, dtype=jnp.int32)[None, :] < iface_len[:, None]).astype(
        jnp.float32
    )
    first_apply = precondition(
        residual_in.astype(jnp.float32),
        local_inverse,
        coarse_basis,
        coarse_inverse,
        weights,
        live,
        iface_dof,
        coarse_map,
    )
    second_apply = precondition(
        first_apply,
        local_inverse,
        coarse_basis,
        coarse_inverse,
        weights,
        live,
        iface_dof,
        coarse_map,
    )
    return (first_apply, second_apply)


def solution(mesh):
    placed = (
        P("dom", None, None),
        P("dom", None, None),
        P("dom", None, None),
        P("dom", None),
        P("dom", None),
        P("dom"),
        P("dom", None),
        P("dom", None),
    )
    return jax.shard_map(
        local,
        mesh=mesh,
        in_specs=placed,
        out_specs=(P("dom", None, None), P("dom", None, None)),
        check_vma=False,
    )
```

profile of v0, /device:TPU:0, one launch (start us, length us, event | category | flops | bytes accessed | tf_op | source)
XLA Modules:
  0.0 582.8 jit_solution(8016925904154326362)
XLA Ops:
  7.3 0.9 eq.8
  8.2 0.8 convert_divide_fusion
  8.9 1.4 fusion.12
  10.3 2.6 fusion.3
  13.0 149.6 %all-reduce.3.cloned.1.call-done = f32[32,8192]{1,0:T(8,128)} async-done(((f32[32,8192]{1,0:T(8,128)}), f32[32,8192]{1,0:T(8,128)}) %all-reduce.3.cloned.1.call-update) | async-done | bytes 1048592 | tf_op jit(solution)/shard_map/psum | solution.py:28
  162.6 3.6 convolution_bitcast_fusion.1
  166.6 9.7 %fusion.13 = f32[8,32,1024]{2,1,0:T(8,128)} fusion(bf16[8,1024,1024]{2,1,0:T(8,128)(2,1)} %param.11, bf16[8,32,1024]{2,1,0:T(8,128)(2,1)S(1)} %copy-done.5, f32[8,1024]{1,0:T(8,128)S(1)} %convert_divide_fusion), kind=kOutput, calls=%fused_computation.32 | convolution fusion | flops 537657344 | bytes 18382848 | tf_op jit(solution)/shard_map/srl,slm->srm/dot_general | solution.py:38
  176.4 55.0 %all-gather.5.cloned.1.call-done = f32[128,64,32]{1,2,0:T(8,128)} async-done(((f32[1,64,32]{1,2,0:T(8,128)}), f32[128,64,32]{1,2,0:T(8,128)}) %all-gather.5.cloned.1.call-update) | async-done | bytes 1048592 | tf_op jit(solution)/shard_map/all_gather | solution.py:30
  231.3 4.1 copy.42
  235.5 2.1 reshape.148
  237.6 2.1 fusion.2
  239.7 1.9 convolution_add_fusion.1
  241.7 0.8 copy.60
  242.5 2.3 copy.45
  244.7 14.8 %scatter_custom_fusion = f32[32,2048]{0,1:T(8,128)} fusion(s32[2048]{0:T(1024)S(1)} %bitcast.78, f32[2048,32]{1,0:T(8,128)} %copy.45, f32[]{:T(128)} %constant.18.clone.1), kind=kCustom, calls=%fused_computation.29 | custom fusion | flops 65536 | bytes 262656 | tf_op jit(solution)/shard_map/scatter-add | solution.py:49
  259.5 1.1 slice.46
  260.6 3.0 collective-permute-start
  263.6 6.7 %collective-permute-done = f32[32,1024]{0,1:T(8,128)S(1)} collective-permute-done((f32[32,1024]{0,1:T(8,128)S(1)}, f32[32,1024]{0,1:T(8,128)S(1)}, u32[]{:S(2)}, u32[]{:S(2)}) %collective-permute-start) | collective-permute-done | bytes 131104 | tf_op jit(solution)/shard_map/ppermute | solution.py:10
  270.3 1.1 slice_add_fusion.1
  271.5 0.9 slice.47
  272.5 13.2 %collective-permute-done.1 = f32[32,1024]{0,1:T(8,128)S(1)} collective-permute-done((f32[32,1024]{0,1:T(8,128)S(1)}, f32[32,1024]{0,1:T(8,128)S(1)}, u32[]{:S(2)}, u32[]{:S(2)}) %collective-permute-start.1) | collective-permute-done | bytes 131104 | tf_op jit(solution)/shard_map/ppermute | solution.py:10
  285.8 7.6 %gather_fusion = f32[2048,32]{1,0:T(8,128)} fusion(f32[32,2048]{0,1:T(8,128)S(1)} %pad_maximum_fusion, s32[2048]{0:T(1024)S(1)} %fusion.19), kind=kCustom, calls=%fused_computation.clone | custom fusion | bytes 532480 | tf_op jit(solution)/shard_map/jit(_take)/gather | solution.py:54
  293.4 1.6 broadcast_select_fusion.1
  295.0 1.0 copy.47
  296.0 1.1 bitcast_select_fusion.1
  297.1 1.2 pad_maximum_fusion.1
  298.6 2.6 fusion.1
  301.2 0.3 all-gather.7.cloned.1.call-start
  301.4 139.9 %all-reduce.5.cloned.1.call-done = f32[32,8192]{1,0:T(8,128)} async-done(((f32[32,8192]{1,0:T(8,128)}), f32[32,8192]{1,0:T(8,128)}) %all-reduce.5.cloned.1.call-update) | async-done | bytes 1048592 | tf_op jit(solution)/shard_map/psum | solution.py:28
  441.4 3.6 convolution_bitcast_fusion
  445.0 9.7 %fusion.15 = f32[8,32,1024]{2,1,0:T(8,128)} fusion(bf16[8,1024,1024]{2,1,0:T(8,128)(2,1)} %param.11, f32[8,32,1024]{2,1,0:T(8,128)S(1)} %pad_maximum_fusion.1, f32[8,1024]{1,0:T(8,128)S(1)} %convert_divide_fusion), kind=kOutput, calls=%fused_computation.38 | convolution fusion | flops 537395200 | bytes 18907136 | tf_op jit(solution)/shard_map/srl,slm->srm/dot_general | solution.py:38
  454.7 55.0 %all-gather.7.cloned.1.call-done = f32[128,64,32]{1,2,0:T(8,128)} async-done(((f32[1,64,32]{1,2,0:T(8,128)}), f32[128,64,32]{1,2,0:T(8,128)}) %all-gather.7.cloned.1.call-update) | async-done | bytes 1048592 | tf_op jit(solution)/shard_map/all_gather | solution.py:30
  509.7 4.1 copy.48
  513.8 2.1 reshape.150
  516.0 2.1 fusion
  518.1 1.9 convolution_add_fusion
  520.0 1.3 copy.51
  521.3 14.8 %scatter_custom_fusion.1 = f32[32,2048]{0,1:T(8,128)} fusion(s32[2048]{0:T(1024)S(1)} %bitcast.79, f32[2048,32]{1,0:T(8,128)} %copy.51, f32[]{:T(128)} %constant.18.clone.1), kind=kCustom, calls=%fused_computation.27 | custom fusion | flops 65536 | bytes 262656 | tf_op jit(solution)/shard_map/scatter-add | solution.py:49
  536.1 1.1 slice.50
  537.2 3.0 collective-permute-start.2
  540.2 6.7 %collective-permute-done.2 = f32[32,1024]{0,1:T(8,128)S(1)} collective-permute-done((f32[32,1024]{0,1:T(8,128)S(1)}, f32[32,1024]{0,1:T(8,128)S(1)}, u32[]{:S(2)}, u32[]{:S(2)}) %collective-permute-start.2) | collective-permute-done | bytes 131104 | tf_op jit(solution)/shard_map/ppermute | solution.py:10
  546.9 1.1 slice_add_fusion
  548.1 14.2 %collective-permute-done.3 = f32[32,1024]{0,1:T(8,128)S(1)} collective-permute-done((f32[32,1024]{0,1:T(8,128)S(1)}, f32[32,1024]{0,1:T(8,128)S(1)}, u32[]{:S(2)}, u32[]{:S(2)}) %collective-permute-start.3) | collective-permute-done | bytes 131104 | tf_op jit(solution)/shard_map/ppermute | solution.py:10
  562.4 7.6 %gather_fusion.1 = f32[2048,32]{1,0:T(8,128)} fusion(f32[32,2048]{0,1:T(8,128)S(1)} %pad_maximum_fusion.2, s32[2048]{0:T(1024)S(1)} %fusion.19), kind=kCustom, calls=%fused_computation.1.clone | custom fusion | bytes 532480 | tf_op jit(solution)/shard_map/jit(_take)/gather | solution.py:54
  570.0 2.6 broadcast_select_fusion
  572.6 1.5 copy.53
  574.1 1.0 bitcast_select_fusion
  575.2 1.1 pad_maximum_fusion.3
  (41 shorter events, 1.2 us)
Async XLA Ops:
  7.2 155.4 %copy-start = (f32[64,8192]{1,0:T(8,128)S(1)}, f32[64,8192]{1,0:T(8,128)}, u32[]{:S(2)}) copy-start(f32[64,8192]{1,0:T(8,128)} %param.13) | copy-start | bytes 6291460
  7.2 159.4 %copy-start.5 = (bf16[8,32,1024]{2,1,0:T(8,128)(2,1)S(1)}, bf16[8,32,1024]{2,1,0:T(8,128)(2,1)}, u32[]{:S(2)}) copy-start(bf16[8,32,1024]{2,1,0:T(8,128)(2,1)} %param.10) | copy-start | bytes 1572868
  7.2 159.3 %copy-start.6 = (s32[8,256]{1,0:T(8,128)S(1)}, s32[8,256]{1,0:T(8,128)}, u32[]{:S(2)}) copy-start(s32[8,256]{1,0:T(8,128)} %param.16) | copy-start | bytes 24580
  7.2 159.3 %copy-start.7 = (s32[8]{0:T(128)S(1)}, s32[8]{0:T(128)}, u32[]{:S(2)}) copy-start(s32[8]{0:T(128)} %param.15) | copy-start | bytes 100
  7.2 155.4 %all-reduce.3.cloned.1.call-start = ((), (), s32[]{:S(2)}) async-start(), calls=%async_computation | async-start | bytes 2097152 | tf_op jit(solution)/shard_map/psum | solution.py:28
  12.9 218.4 %all-gather.5.cloned.1.call-start = ((), (), s32[]{:S(2)}) async-start(), calls=%async_computation.2 | async-start | bytes 2113536 | tf_op jit(solution)/shard_map/all_gather | solution.py:30
  166.2 275.2 %all-reduce.5.cloned.1.call-start = ((), (), s32[]{:S(2)}) async-start(), calls=%async_computation.1 | async-start | bytes 2097152 | tf_op jit(solution)/shard_map/psum | solution.py:28
  176.3 63.4 %copy-start.4 = (bf16[8,16,1024]{2,1,0:T(8,128)(2,1)S(1)}, bf16[8,16,1024]{2,1,0:T(8,128)(2,1)}, u32[]{:S(2)}) copy-start(bf16[8,16,1024]{2,1,0:T(8,128)(2,1)} %param.12) | copy-start | bytes 786436
  241.6 30.9 %copy-start.3 = (f32[8,32,1024]{2,1,0:T(8,128)}, f32[8,32,1024]{2,1,0:T(8,128)S(1)}, u32[]{:S(2)}) copy-start(f32[8,32,1024]{2,1,0:T(8,128)S(1)} %convolution_add_fusion.1) | copy-start | bytes 3145732
  260.6 9.7 %collective-permute-start = (f32[32,1024]{0,1:T(8,128)S(1)}, f32[32,1024]{0,1:T(8,128)S(1)}, u32[]{:S(2)}, u32[]{:S(2)}) collective-permute-start(f32[32,1024]{0,1:T(8,128)S(1)} %slice.46), channel_id=1, source_target_pairs={{0,127},{1,0},{2,1},{3,2},{4,3},{5,4},{6,5},{7,6},{8,7},{9,8},{10,... | collective-permute-start | bytes 393224 | tf_op jit(solution)/shard_map/ppermute | solution.py:10
  271.4 14.3 %collective-permute-start.1 = (f32[32,1024]{0,1:T(8,128)S(1)}, f32[32,1024]{0,1:T(8,128)S(1)}, u32[]{:S(2)}, u32[]{:S(2)}) collective-permute-start(f32[32,1024]{0,1:T(8,128)S(1)} %slice_add_fusion.1), channel_id=1, source_target_pairs={{0,1},{1,2},{2,3},{3,4},{4,5},{5,6},{6,7},{7,8},{8,9},{9,10},{10,1... | collective-permute-start | bytes 393224 | tf_op jit(solution)/shard_map/ppermute | solution.py:10
  298.3 156.4 %copy-start.1 = (f32[8,32,1024]{2,1,0:T(8,128)}, f32[8,32,1024]{2,1,0:T(8,128)S(1)}, u32[]{:S(2)}) copy-start(f32[8,32,1024]{2,1,0:T(8,128)S(1)} %pad_maximum_fusion.1) | copy-start | bytes 3145732
  301.2 208.5 %all-gather.7.cloned.1.call-start = ((), (), s32[]{:S(2)}) async-start(), calls=%async_computation.3 | async-start | bytes 2113536 | tf_op jit(solution)/shard_map/all_gather | solution.py:30
  519.9 28.2 %copy-start.2 = (f32[8,32,1024]{2,1,0:T(8,128)}, f32[8,32,1024]{2,1,0:T(8,128)S(1)}, u32[]{:S(2)}) copy-start(f32[8,32,1024]{2,1,0:T(8,128)S(1)} %convolution_add_fusion) | copy-start | bytes 3145732
  537.2 9.7 %collective-permute-start.2 = (f32[32,1024]{0,1:T(8,128)S(1)}, f32[32,1024]{0,1:T(8,128)S(1)}, u32[]{:S(2)}, u32[]{:S(2)}) collective-permute-start(f32[32,1024]{0,1:T(8,128)S(1)} %slice.50), channel_id=1, source_target_pairs={{0,127},{1,0},{2,1},{3,2},{4,3},{5,4},{6,5},{7,6},{8,7},{9,8},{10,... | collective-permute-start | bytes 393224 | tf_op jit(solution)/shard_map/ppermute | solution.py:10
  548.1 14.3 %collective-permute-start.3 = (f32[32,1024]{0,1:T(8,128)S(1)}, f32[32,1024]{0,1:T(8,128)S(1)}, u32[]{:S(2)}, u32[]{:S(2)}) collective-permute-start(f32[32,1024]{0,1:T(8,128)S(1)} %slice_add_fusion), channel_id=1, source_target_pairs={{0,1},{1,2},{2,3},{3,4},{4,5},{5,6},{6,7},{7,8},{8,9},{9,10},{10,1... | collective-permute-start | bytes 393224 | tf_op jit(solution)/shard_map/ppermute | solution.py:10
  570.0 5.1 slice-start
Sparse Core Ops, SparseCore 0:
  13.4 149.1 all-reduce.2
  166.8 64.5 all-gather.4
  301.3 140.0 all-reduce.4
  445.1 64.5 all-gather.6
where the time goes:
time: 584 us; the launch traced here: 583 us
  waiting for transfers between devices  440 us (75%)
  other arithmetic  41.4 us (7%)
  matrix products  41.3 us (7%)
  local copies, waits for them, and re-layouts  38.8 us (7%)
  between operations  14.1 us (2%)
  starting transfers between devices  6.79 us (1%)
    psum x2, waiting for transfers between devices, precondition(): coarse_rhs = lax.psum(local_rhs, 'dom')  290 us
    all_gather x2, waiting for transfers between devices, precondition(): coarse_sol = lax.all_gather(own_sol, 'dom', axis=1, tiled=True)  110 us
    ppermute x4, waiting for transfers between devices, from_behind(): return lax.ppermute(value, axis, pairs)  40.8 us
    scatter-add x2, other arithmetic, precondition(): jnp.zeros((cases, 2 * own_width), jnp.float32).at[:, position]  29.5 us
    dot_general x2, matrix products, precondition(): jnp.einsum('srl,slm->srm', scaled, local_inverse, preferred_element_type=...  19.5 us
    gather x2, local copies, waits for them, and re-layouts, precondition(): jnp.take(both, position, axis=1).reshape(cases, sub_count, iface_width)  15.2 us
  transfers between devices with their start and end apart: 8, of which 8 were waited for; matrix products, arithmetic and copies ran while one was open for 4% of the time, Pallas kernels for 0%

commit v1 on v0

v1 whole, which is shorter than its diff:
```python
import functools

import jax
import jax.numpy as jnp
from jax import lax
from jax.experimental import pallas as pl
from jax.experimental.pallas import tpu as pltpu
from jax.sharding import Mesh
from jax.sharding import PartitionSpec as P

CHIPS = ("y", "z", "x")
DOM = ("y", "z", "x", "c")
MIB = 2**20
VMEM = pl.BlockSpec(memory_space=pltpu.VMEM)
SMEM = pl.BlockSpec(memory_space=pltpu.SMEM)


def halves(value):
    high = value.astype(jnp.bfloat16)
    low = (value - high.astype(jnp.float32)).astype(jnp.bfloat16)
    return jnp.concatenate([high, low], axis=0)


def thirds(value):
    high = value.astype(jnp.bfloat16)
    rest = value - high.astype(jnp.float32)
    middle = rest.astype(jnp.bfloat16)
    low = (rest - middle.astype(jnp.float32)).astype(jnp.bfloat16)
    return jnp.concatenate([high, middle, low], axis=0)


def split_dot(value, parts, other, contract=0):
    rows = value.shape[0]
    pieces = halves(value) if parts == 2 else thirds(value)
    out = lax.dot_general(
        pieces, other, (((1,), (contract,)), ((), ())), preferred_element_type=jnp.float32
    )
    total = out[:rows]
    for part in range(1, parts):
        total = total + out[part * rows : (part + 1) * rows]
    return total


def call(kernel, out_shape, args, specs=None, mib=40, **more):
    return pl.pallas_call(
        kernel,
        out_shape=out_shape,
        in_specs=specs if specs is not None else [VMEM] * len(args),
        compiler_params=pltpu.CompilerParams(vmem_limit_bytes=mib * MIB),
        **more,
    )(*args)


def f32(*shape):
    return jax.ShapeDtypeStruct(shape, jnp.float32)


def bf16(*shape):
    return jax.ShapeDtypeStruct(shape, jnp.bfloat16)


def turn_kernel(core_ref, mine_ref, other_ref, out_ref):
    core = core_ref[0]
    for chunk in range(mine_ref.shape[1] // 128):
        columns = slice(chunk * 128, (chunk + 1) * 128)
        mine, other = mine_ref[:, columns], other_ref[:, columns]
        first = jnp.where(core == 0, mine, other)
        second = jnp.where(core == 0, other, mine)
        out_ref[columns, :] = jnp.concatenate([first, second], axis=0).T


def pick_kernel(index_ref, turned_ref, out_ref, rows_ref):
    count = rows_ref.shape[0]
    start = pl.program_id(0) * count

    def sixteen(group, carry):
        for row in range(16):
            place = group * 16 + row
            rows_ref[pl.ds(place, 1), :] = turned_ref[pl.ds(index_ref[start + place], 1), :]
        return carry

    lax.fori_loop(0, count // 16, sixteen, 0)
    rows = rows_ref[...]
    high = rows.astype(jnp.bfloat16)
    width = rows.shape[1]
    out_ref[:, :width] = high
    out_ref[:, width:] = (rows - high.astype(jnp.float32)).astype(jnp.bfloat16)


def pick(index, turned):
    count, block = index.shape[0], 1024
    order, width = turned.shape
    return pl.pallas_call(
        pick_kernel,
        out_shape=bf16(count, 2 * width),
        grid_spec=pltpu.PrefetchScalarGridSpec(
            num_scalar_prefetch=1,
            grid=(count // block,),
            in_specs=[
                pl.BlockSpec((order, width), lambda i, s: (0, 0), pipeline_mode=pl.Buffered(1))
            ],
            out_specs=pl.BlockSpec((block, 2 * width), lambda i, s: (i, 0)),
            scratch_shapes=[pltpu.VMEM((block, width), jnp.float32)],
        ),
        compiler_params=pltpu.CompilerParams(vmem_limit_bytes=24 * MIB),
        cost_estimate=pl.CostEstimate(flops=0, bytes_accessed=60 * MIB, transcendentals=0),
        name="pick",
    )(index, turned)


def solve_kernel(parts_ref, picked_ref, out_ref):
    cases = parts_ref.shape[1]
    width = out_ref.shape[2]
    total = jnp.zeros((2 * cases, 2 * width), jnp.float32)
    for pair in range(parts_ref.shape[0] // 2):
        value = jnp.concatenate([parts_ref[2 * pair], parts_ref[2 * pair + 1]], axis=1)
        wide = value.shape[1]
        total = total + jnp.dot(
            halves(value),
            picked_ref[pair * wide : (pair + 1) * wide, :],
            preferred_element_type=jnp.float32,
        )
    high, low = total[:cases], total[cases:]
    own = (high[:, :width] + high[:, width:]) + (low[:, :width] + low[:, width:])
    out_ref[...] = jnp.broadcast_to(own[None], out_ref.shape)


def local_kernel(scaled_ref, inverse_ref, slots_ref, mask_ref, local_ref, sums_ref):
    solved = jnp.dot(scaled_ref[0], inverse_ref[0], preferred_element_type=jnp.float32)
    local_ref[0] = solved
    width = slots_ref.shape[0]
    sums = split_dot(solved[:, :width] * mask_ref[0], 3, slots_ref[...])

    @pl.when(pl.program_id(0) == 0)
    def _():
        sums_ref[...] = sums

    @pl.when(pl.program_id(0) > 0)
    def _():
        sums_ref[...] += sums


def local_solve(scaled, inverse, slots, mask):
    subs, cases, length = scaled.shape
    width = slots.shape[0] // subs
    return pl.pallas_call(
        local_kernel,
        out_shape=(f32(subs, cases, length), f32(cases, slots.shape[1])),
        grid=(subs,),
        in_specs=[
            pl.BlockSpec((1, cases, length), lambda i: (i, 0, 0)),
            pl.BlockSpec((1, length, length), lambda i: (i, 0, 0)),
            pl.BlockSpec((width, slots.shape[1]), lambda i: (i, 0)),
            pl.BlockSpec((1, 1, width), lambda i: (i, 0, 0)),
        ],
        out_specs=(
            pl.BlockSpec((1, cases, length), lambda i: (i, 0, 0)),
            pl.BlockSpec((cases, slots.shape[1]), lambda i: (0, 0)),
        ),
        compiler_params=pltpu.CompilerParams(vmem_limit_bytes=24 * MIB),
        cost_estimate=pl.CostEstimate(
            flops=2 * subs * cases * length * length,
            bytes_accessed=36 * MIB,
            transcendentals=0,
        ),
        name="local_solve",
    )(scaled, inverse, slots, mask)


def base_kernel(local_ref, sums_ref, prev_ref, next_ref, slots_ref, live_ref, base_ref):
    half = prev_ref.shape[1]
    sums = sums_ref[...]
    sums = jnp.concatenate(
        [sums[:, :half] + next_ref[...], sums[:, half:] + prev_ref[...]], axis=1
    )
    width = live_ref.shape[2]
    for sub in range(local_ref.shape[0]):
        fetched = split_dot(sums, 3, slots_ref[sub * width : (sub + 1) * width, :], 1)
        base_ref[sub, :, :width] = jnp.where(
            live_ref[sub] > 0, fetched, local_ref[sub, :, :width]
        )
        base_ref[sub, :, width:] = local_ref[sub, :, width:]


def make_base(local, sums, behind, ahead, slots, live):
    return call(
        base_kernel,
        f32(*local.shape),
        (local, sums, behind, ahead, slots, live),
        cost_estimate=pl.CostEstimate(
            flops=2 * 3 * 32 * 2048 * 2048, bytes_accessed=14 * MIB, transcendentals=0
        ),
        name="make_base",
    )


def own_parts(scaled_of, basis_ref):
    total = None
    for sub in range(basis_ref.shape[0]):
        part = lax.dot_general(
            scaled_of(sub),
            basis_ref[sub],
            (((1,), (1,)), ((), ())),
            preferred_element_type=jnp.float32,
        )
        total = part if total is None else total + part
    return total


def spread(parts, out_ref):
    cases = out_ref.shape[1]
    for core in range(2):
        own = parts[core * cases : (core + 1) * cases]
        for chip in range(out_ref.shape[0] // 2):
            out_ref[2 * chip + core] = own


def first_kernel(values_ref, weights_ref, basis_ref, scaled_ref, parts_ref):
    for sub in range(values_ref.shape[0]):
        scaled = values_ref[sub].astype(jnp.float32) * weights_ref[sub]
        scaled_ref[sub] = scaled.astype(jnp.bfloat16)
    spread(own_parts(lambda sub: scaled_ref[sub], basis_ref), parts_ref)


def correct(core_ref, mine_ref, other_ref, hot_ref, shared_ref, basis_ref, base_ref, out_ref):
    subs, cases, _ = base_ref.shape
    width = shared_ref.shape[1] // subs
    chips, half, rows = mine_ref.shape
    looked = jnp.zeros((4 * half, hot_ref.shape[1]), jnp.float32)
    for pair in range(chips // 2):
        mine = jnp.concatenate([mine_ref[2 * pair], mine_ref[2 * pair + 1]], axis=1)
        other = jnp.concatenate([other_ref[2 * pair], other_ref[2 * pair + 1]], axis=1)
        both = jnp.concatenate([mine, other], axis=0)
        looked = looked + jnp.dot(
            halves(both),
            hot_ref[2 * pair * rows : 2 * (pair + 1) * rows, :],
            preferred_element_type=jnp.float32,
        )
    looked = looked[: 2 * half] + looked[2 * half :]
    turned = jnp.concatenate([looked[half:], looked[:half]], axis=0)
    looked = jnp.where(core_ref[0] == 0, looked, turned)
    own = looked.shape[1] // 3
    shared = split_dot(looked, 3, shared_ref[...])
    for sub in range(subs):
        inner = split_dot(looked[:, own : 2 * own], 3, basis_ref[sub, :, width:])
        out_ref[sub, :, :width] = (
            base_ref[sub, :, :width] + shared[:, sub * width : (sub + 1) * width]
        )
        out_ref[sub, :, width:] = base_ref[sub, :, width:] + inner


def last_kernel(core_ref, mine_ref, other_ref, hot_ref, shared_ref, basis_ref, base_ref, out_ref):
    correct(core_ref, mine_ref, other_ref, hot_ref, shared_ref, basis_ref, base_ref, out_ref)


def middle_kernel(
    core_ref,
    mine_ref,
    other_ref,
    hot_ref,
    shared_ref,
    basis_ref,
    base_ref,
    weights_ref,
    out_ref,
    scaled_ref,
    parts_ref,
):
    correct(core_ref, mine_ref, other_ref, hot_ref, shared_ref, basis_ref, base_ref, out_ref)
    for sub in range(base_ref.shape[0]):
        scaled_ref[sub] = (out_ref[sub] * weights_ref[sub]).astype(jnp.bfloat16)
    spread(own_parts(lambda sub: scaled_ref[sub], basis_ref), parts_ref)


def shift(value, steps):
    count = lax.axis_size(DOM)
    return lax.ppermute(value, DOM, [(s, (s + steps) % count) for s in range(count)])


def swap(value):
    return lax.ppermute(value, "c", [(0, 1), (1, 0)])


def local(
    residual_in,
    local_inverse,
    coarse_basis,
    coarse_inverse,
    multiplicity,
    iface_len,
    iface_dof,
    coarse_map,
):
    subs, cases, length = residual_in.shape
    coarse = coarse_basis.shape[1]
    width = iface_dof.shape[1]
    order = coarse_inverse.shape[1]
    count = lax.axis_size(DOM)
    chips = count // 2
    half_cases = cases // 2
    entries = subs * coarse
    spots = subs * width
    owned = spots // 2
    device = lax.axis_index(DOM)
    core = lax.axis_index("c").astype(jnp.int32).reshape(1)

    own_map = coarse_map.reshape(1, entries)
    maps = lax.all_to_all(jnp.broadcast_to(own_map, (count, entries)), DOM, 0, 0, tiled=True)
    turned = call(
        turn_kernel,
        f32(order, 2 * coarse_inverse.shape[0]),
        (core, coarse_inverse, swap(coarse_inverse)),
        [SMEM, VMEM, VMEM],
        mib=24,
        name="turn",
    )

    weights = 1.0 / multiplicity.astype(jnp.float32)
    weights3 = weights.reshape(subs, 1, length)
    same = (
        jnp.arange(subs, dtype=jnp.int32)[:, None] == jnp.arange(subs, dtype=jnp.int32)[None, :]
    )
    basis_pad = jnp.where(
        same[:, :, None, None], coarse_basis[:, None], jnp.zeros((), jnp.bfloat16)
    ).reshape(subs, entries, length)

    scaled, parts = call(
        first_kernel,
        (bf16(subs, cases, length), f32(count, half_cases, entries)),
        (residual_in, weights3, basis_pad),
        mib=24,
        name="first",
    )
    parts = lax.all_to_all(parts, DOM, 0, 0, tiled=True)

    live = jnp.arange(width, dtype=jnp.int32)[None, :] < iface_len[:, None]
    owner = iface_dof // owned
    slot = jnp.where(owner != device, owned, 0) + (iface_dof - owner * owned)
    slot = jnp.where(live, slot, -1).reshape(spots)
    slots = (slot[:, None] == jnp.arange(spots, dtype=jnp.int32)[None, :]).astype(jnp.bfloat16)
    live3 = live.astype(jnp.float32).reshape(subs, 1, width)
    mask = live3 * weights3[:, :, :width]

    def interface(scaled):
        solved, sums = local_solve(scaled, local_inverse, slots, mask)
        ahead = shift(sums[:, owned:], -1)
        behind = shift(sums[:, :owned], 1)
        return make_base(solved, sums, behind, ahead, slots, live3)

    base = interface(scaled)

    head = coarse_basis[:, :, :width].astype(jnp.float32)
    weighted = (head * mask).astype(jnp.bfloat16)
    compact = jnp.transpose(weighted, (1, 0, 2)).reshape(coarse, spots)
    row_of = jnp.broadcast_to(jnp.arange(subs, dtype=jnp.bfloat16)[:, None], (subs, width))
    block = jnp.where(
        same[:, None, :, None], weighted[:, :, None, :], jnp.zeros((), jnp.bfloat16)
    ).reshape(entries, spots)
    stacked = jnp.concatenate(
        [block, compact, row_of.reshape(1, spots), jnp.zeros((15, spots), jnp.bfloat16)], axis=0
    )
    by_slot = jnp.dot(stacked, slots, preferred_element_type=jnp.float32)
    compact = by_slot[entries : entries + 24]
    ahead = shift(compact[:, owned:], -1)
    behind = shift(compact[:, :owned], 1)

    def widened(arrived):
        row = arrived[coarse : coarse + 1]
        subs_of = jnp.arange(subs, dtype=jnp.float32)[:, None, None]
        return jnp.where(row[None] == subs_of, arrived[None, :coarse], 0.0).reshape(
            entries, owned
        )

    nothing = jnp.zeros((entries, owned), jnp.float32)
    by_slot = jnp.concatenate(
        [
            jnp.concatenate([nothing, widened(behind)], axis=1),
            by_slot[:entries],
            jnp.concatenate([widened(ahead), nothing], axis=1),
        ],
        axis=0,
    ).astype(jnp.bfloat16)
    shared = lax.dot_general(
        by_slot, slots, (((1,), (1,)), ((), ())), preferred_element_type=jnp.float32
    )
    dead = jnp.where(
        same[:, None, :, None] & ~live[None, None], head[:, :, None, :], 0.0
    ).reshape(entries, spots)
    shared = (
        (shared + jnp.concatenate([jnp.zeros_like(dead), dead, jnp.zeros_like(dead)], axis=0))
    ).astype(jnp.bfloat16)

    near = [
        lax.dynamic_slice_in_dim(maps, (device + step) % count, 1, axis=0)
        for step in (count - 1, 0, 1)
    ]
    near = jnp.concatenate(near, axis=1)
    hot = (jnp.arange(order, dtype=jnp.int32)[:, None] == near).astype(jnp.bfloat16)
    picked = pick(maps.reshape(count * entries), turned)

    def coarse_solve(parts):
        own = call(
            solve_kernel,
            f32(chips, half_cases, 2 * coarse_inverse.shape[0]),
            (parts, picked),
            name="solve",
        )
        mine = lax.all_to_all(own, CHIPS, 0, 0, tiled=True)
        return mine, swap(mine)

    specs = [SMEM] + [VMEM] * 6
    mine, other = coarse_solve(parts)
    first_apply, scaled, parts = call(
        middle_kernel,
        (
            f32(subs, cases, length),
            bf16(subs, cases, length),
            f32(count, half_cases, entries),
        ),
        (core, mine, other, hot, shared, basis_pad, base, weights3),
        specs + [VMEM],
        name="middle",
    )
    parts = lax.all_to_all(parts, DOM, 0, 0, tiled=True)
    base = interface(scaled)
    mine, other = coarse_solve(parts)
    second_apply = call(
        last_kernel,
        f32(subs, cases, length),
        (core, mine, other, hot, shared, basis_pad, base),
        specs,
        name="last",
    )
    return first_apply, second_apply


def solution(mesh):
    grid = Mesh(mesh.devices.reshape(4, 4, 4, 2), DOM)
    placed = (
        P(DOM, None, None),
        P(DOM, None, None),
        P(DOM, None, None),
        P(DOM, None),
        P(DOM, None),
        P(DOM),
        P(DOM, None),
        P(DOM, None),
    )
    return jax.shard_map(
        local,
        mesh=grid,
        in_specs=placed,
        out_specs=(P(DOM, None, None), P(DOM, None, None)),
        check_vma=False,
    )
```

time: 584 us -> 233 us (0.40)
  waiting for transfers between devices: 440 us -> 21.1 us
  Pallas kernels: 0 us -> 59 us
  blocking collectives: 0 us -> 41 us
  starting transfers between devices: 6.79 us -> 42.1 us
  matrix products: 41.3 us -> 9.25 us
  other arithmetic: 41.4 us -> 16.6 us
  between operations: 14.1 us -> 1.08 us
    psum x2 -> x0, waiting for transfers between devices: 290 us -> none  [precondition(): coarse_rhs = lax.psum(local_rhs, 'dom')]
    all_gather x2 -> x0, waiting for transfers between devices: 110 us -> none  [precondition(): coarse_sol = lax.all_gather(own_sol, 'dom', axis=1, tiled=True)]
    pallas_call x0 -> x11, Pallas kernels: none -> 59 us  [the longest x1 25.2 us: pick(): pl.pallas_call(pick_kernel, out_shape=bf16(count, 2 * width), grid_spec=p...]
    all_to_all x0 -> x2, blocking collectives: none -> 41 us  [the longest x1 23.3 us: local(): parts = lax.all_to_all(parts, DOM, 0, 0, tiled=True)]
    dot_general x12 -> x2, matrix products: 41.3 us -> 9.25 us  [the longest x1 5.55 us: local(): lax.dot_general(by_slot, slots, (((1,), (1,)), ((), ())), preferred_eleme...]
    ppermute x4 -> x9, waiting for transfers between devices: 40.8 us -> 9.88 us  [the longest x6 9.83 us: shift(): lax.ppermute(value, DOM, [(s, (s + steps) % count) for s in range(count)])]
    all_to_all x0 -> x3, starting transfers between devices: none -> 30.8 us  [the longest x1 11.1 us: local(): lax.all_to_all(jnp.broadcast_to(own_map, (count, entries)), DOM, 0, 0, ti...]
    unnamed x20 -> x42, local copies, waits for them, and re-layouts: 4.31 us -> 34.3 us
  transfers between devices with their start and end apart: 8 -> 12, of which waited for: 8 -> 3; matrix products, arithmetic and copies ran while one was open for 4% -> 15% of each run, Pallas kernels for 0% -> 22%
where the time goes in v1:
time: 233 us; the launch traced here: 232 us
  Pallas kernels  59 us (25%)
  local copies, waits for them, and re-layouts  42.2 us (18%)
  starting transfers between devices  42.1 us (18%)
  blocking collectives  41 us (18%)
  waiting for transfers between devices  21.1 us (9%)
  other arithmetic  16.6 us (7%)
  matrix products  9.25 us (4%)
    unnamed x42, local copies, waits for them, and re-layouts  34.3 us
    pallas_call x1, Pallas kernels, pick(): pl.pallas_call(pick_kernel, out_shape=bf16(count, 2 * width), grid_spec=p...  25.2 us
    all_to_all x1, blocking collectives, local(): parts = lax.all_to_all(parts, DOM, 0, 0, tiled=True)  23.3 us
    pallas_call x8, Pallas kernels, call(): pl.pallas_call(kernel, out_shape=out_shape, in_specs=specs if specs is no...  22.7 us
    all_to_all x1, blocking collectives, coarse_solve(): mine = lax.all_to_all(own, CHIPS, 0, 0, tiled=True)  17.6 us
    ppermute x6, starting transfers between devices, shift(): lax.ppermute(value, DOM, [(s, (s + steps) % count) for s in range(count)])  11.3 us
    all_to_all x1, waiting for transfers between devices, coarse_solve(): mine = lax.all_to_all(own, CHIPS, 0, 0, tiled=True)  11.2 us
    all_to_all x1, starting transfers between devices, local(): lax.all_to_all(jnp.broadcast_to(own_map, (count, entries)), DOM, 0, 0, ti...  11.1 us
  transfers between devices with their start and end apart: 12, of which 3 were waited for; matrix products, arithmetic and copies ran while one was open for 15% of the time, Pallas kernels for 22%

profile of v1, /device:TPU:0, one launch (start us, length us, event | category | flops | bytes accessed | tf_op | source)
XLA Modules:
  0.0 232.3 jit_solution(12533455324682828664)
XLA Ops:
  0.6 0.8 broadcast_in_dim.143
  2.1 11.1 %all-to-all-start.1 = ((s32[128,1,128]{2,1,0:T(1,128)}), s32[128,1,128]{2,1,0:T(1,128)S(1)}, u32[]{:S(2)}, u32[]{:S(2)}) async-start(s32[128,1,128]{2,1,0:T(1,128)} %broadcast_in_dim.144), calls=%async_computation.1 | async-start | bytes 131072 | tf_op jit(solution)/shard_map/all_to_all | solution.py:308
  13.2 0.8 convert_divide_fusion
  14.8 0.9 fusion.40
  15.7 0.9 multiply_convert_fusion
  16.6 0.8 select_bitcast_fusion
  17.7 3.7 %fusion.2 = f32[160,2048]{1,0:T(8,128)S(1)} fusion(s32[2048]{0:T(1024)S(1)} %bitcast.46, bf16[1,2048]{1,0:T(2,128)(2,1)S(1)} %bitcast.51, bf16[16,2048]{1,0:T(8,128)(2,1)S(1)} %bitcast.45, bf16[128,2048]{1,0:T(8,128)(2,1)S(1)} %bitcast.40, bf16[160]{0:T(256)(128)(2,1)S(1)} %pad.13.clone), kind=kOutput, calls=%fused_computation.3 | convolution fusion | flops 1348993024 | bytes 1913152 | tf_op jit(solution)/shard_map/dot_general | solution.py:362
  21.5 7.1 %collective-permute-start.3 = (f32[24,1024]{1,0:T(8,128)S(1)}, f32[24,1024]{1,0:T(8,128)}, u32[]{:S(2)}, u32[]{:S(2)}) collective-permute-start(f32[24,1024]{1,0:T(8,128)S(1)} %get-tuple-element.21), channel_id=1, source_target_pairs={{0,127},{1,0},{2,1},{3,2},{4,3},{5,4},{6,5},{7,6},{8,7},{9,8},{10,... | collective-permute-start | bytes 294920 | tf_op jit(solution)/shard_map/ppermute | solution.py:277
  28.6 4.7 %fusion.slots_ref = bf16[2048,2048]{1,0:T(8,128)(2,1)} fusion(s32[2048]{0:T(1024)S(1)} %bitcast.47), kind=kLoop, calls=%fused_computation.1 | loop fusion | flops 8388608 | bytes 8396800 | tf_op jit(solution)/shard_map/convert_element_type | solution.py:340
  33.7 1.9 first.1
  35.7 3.4 %copy-done = bf16[2048,2048]{1,0:T(8,128)(2,1)S(1)} copy-done((bf16[2048,2048]{1,0:T(8,128)(2,1)S(1)}, bf16[2048,2048]{1,0:T(8,128)(2,1)}, u32[]{:S(2)}) %copy-start) | copy-done | bytes 8388632
  39.0 5.8 %copy-done.4 = bf16[8,1024,1024]{2,1,0:T(8,128)(2,1)S(1)} copy-done((bf16[8,1024,1024]{2,1,0:T(8,128)(2,1)S(1)}, bf16[8,1024,1024]{2,1,0:T(8,128)(2,1)}, u32[]{:S(2)}) %copy-start.4) | copy-done | bytes 16777240
  44.8 5.6 %local_solve.2 = (f32[8,32,1024]{2,1,0:T(8,128)S(1)}, f32[32,2048]{1,0:T(8,128)S(1)}) custom-call(bf16[8,32,1024]{2,1,0:T(8,128)(2,1)S(1)} %get-tuple-element.12.scaled_ref, bf16[8,1024,1024]{2,1,0:T(8,128)(2,1)S(1)} %copy-done.4, bf16[2048,2048]{1,0:T(8,128)(2,1)S(1)} %copy-done, f32[8,1,256]{2,1,0:T(1,128)S(1)} %compare_select_fusion.mask_ref), custom_call_target="tpu_custom_call" | custom-call | flops 536870912 | bytes 37748736 | tf_op jit(solution)/shard_map/local_solve/pallas_call | solution.py:146
  50.4 1.1 copy-done.10
  52.2 2.0 collective-permute-start.5
  54.4 1.1 broadcast_select_fusion
  55.5 2.1 slice.69
  57.7 2.5 %copy.16 = f32[16,8,8,256]{3,1,2,0:T(8,128)} copy(f32[16,8,8,256]{3,2,1,0:T(8,128)} %bitcast.37) | data formatting | bytes 2097152
  60.2 9.8 %all-to-all-start = ((f32[128,16,128]{2,1,0:T(8,128)}), f32[128,16,128]{2,1,0:T(8,128)}, u32[]{:S(2)}, u32[]{:S(2)}) async-start(f32[128,16,128]{2,1,0:T(8,128)} %get-tuple-element.11), calls=%async_computation | async-start | bytes 2097152 | tf_op jit(solution)/shard_map/all_to_all | solution.py:334
  70.1 5.4 %fusion.3.hot_ref = bf16[8192,384]{1,0:T(8,128)(2,1)} fusion(s32[384]{0:T(512)S(1)} %add_reduce_fusion), kind=kLoop, calls=%fused_computation.5 | loop fusion | flops 6291456 | bytes 6292992 | tf_op jit(solution)/shard_map/convert_element_type | solution.py:398
  75.5 0.8 slice.58
  76.2 0.8 slice.62
  77.0 3.4 %turn.1.turned_ref = f32[8192,128]{1,0:T(8,128)S(1)} custom-call(s32[1]{0:T(128)} %bitcast.core_ref, f32[64,8192]{1,0:T(8,128)} %mine_ref.1, f32[64,8192]{1,0:T(8,128)} %collective-permute-done.other_ref), custom_call_target="tpu_custom_call" | custom-call | tf_op jit(solution)/shard_map/turn/pallas_call | solution.py:45
  80.4 25.2 %pick.1.picked_ref = bf16[16384,256]{1,0:T(8,128)(2,1)S(1)} custom-call(s32[16384]{0:T(1024)S(1)} %bitcast.36, f32[8192,128]{1,0:T(8,128)S(1)} %turn.1.turned_ref), custom_call_target="tpu_custom_call" | custom-call | bytes 62914560 | tf_op jit(solution)/shard_map/pick/pallas_call | solution.py:93
  105.6 3.2 %copy-done.1 = bf16[16384,256]{1,0:T(8,128)(2,1)} copy-done((bf16[16384,256]{1,0:T(8,128)(2,1)}, bf16[16384,256]{1,0:T(8,128)(2,1)S(1)}, u32[]{:S(2)}) %copy-start.1) | copy-done | bytes 8388632
  108.8 3.4 %copy-done.2 = bf16[16384,256]{1,0:T(8,128)(2,1)S(1)} copy-done((bf16[16384,256]{1,0:T(8,128)(2,1)S(1)}, bf16[16384,256]{1,0:T(8,128)(2,1)}, u32[]{:S(2)}) %copy-start.2) | copy-done | bytes 8388632
  112.2 3.6 %solve.2 = f32[64,16,128]{2,1,0:T(8,128)} custom-call(f32[128,16,128]{2,1,0:T(8,128)} %all-to-all-done.parts_ref, bf16[16384,256]{1,0:T(8,128)(2,1)S(1)} %copy-done.2), custom_call_target="tpu_custom_call" | custom-call | tf_op jit(solution)/shard_map/solve/pallas_call | solution.py:45
  115.8 9.9 %all-to-all-start.2 = ((f32[64,16,128]{2,1,0:T(8,128)}), f32[64,16,128]{2,1,0:T(8,128)S(1)}, u32[]{:S(2)}, u32[]{:S(2)}) async-start(f32[64,16,128]{2,1,0:T(8,128)} %solve.2), calls=%async_computation.2 | async-start | bytes 1048576 | tf_op jit(solution)/shard_map/all_to_all | solution.py:408
  125.7 0.8 slice.59
  126.6 0.8 slice.63
  127.5 0.8 select_convert_fusion.1
  128.2 11.2 %all-to-all-done.2.mine_ref = f32[64,16,128]{2,1,0:T(8,128)S(1)} async-done(((f32[64,16,128]{2,1,0:T(8,128)}), f32[64,16,128]{2,1,0:T(8,128)S(1)}, u32[]{:S(2)}, u32[]{:S(2)}) %all-to-all-start.2) | async-done | bytes 524320 | tf_op jit(solution)/shard_map/all_to_all | solution.py:408
  139.6 5.5 %fusion.6.shared_ref = bf16[384,2048]{1,0:T(8,128)(2,1)S(1)} fusion(f32[128,2048]{1,0:T(8,128)S(1)} %broadcast.142, f32[128,2048]{1,0:T(8,128)} %bitcast.39, s32[2048]{0:T(1024)S(1)} %bitcast.48, bf16[128,1024]{1,0:T(8,128)(2,1)S(1)} %bitcast.41, bf16[128,1024]{1,0:T(8,128)(2,1)} %bitcast.42, bf16[128,2048]{1,0:T(8,128)(2,1)} %slice.69), kind=kOutput, calls=%fused_computation.11 | convolution fusion | flops 3236429824 | bytes 4726784 | tf_op jit(solution)/shard_map/dot_general | solution.py:383
  145.2 2.7 %make_base.2.base_ref = f32[8,32,1024]{2,1,0:T(8,128)S(1)} custom-call(f32[8,32,1024]{2,1,0:T(8,128)S(1)} %copy-done.11, f32[32,2048]{1,0:T(8,128)S(1)} %get-tuple-element.14.sums_ref, f32[32,1024]{1,0:T(8,128)S(1)} %collective-permute-done.4.prev_ref, f32[32,1024]{1,0:T(8,128)S(1)} %collective-permute-done.5.next_ref, bf16[2048,2048]{1,0:T(8,128)(2,1)S(1)} %bitcast.35, ...), custom_call_target="tpu_custom_call" | custom-call | flops 805306368 | bytes 14680064 | tf_op jit(solution)/shard_map/make_base/pallas_call | solution.py:45
  147.9 2.8 %copy-done.6 = bf16[8192,384]{1,0:T(8,128)(2,1)S(1)} copy-done((bf16[8192,384]{1,0:T(8,128)(2,1)S(1)}, bf16[8192,384]{1,0:T(8,128)(2,1)}, u32[]{:S(2)}) %copy-start.6) | copy-done | bytes 6291480
  150.7 3.6 %middle.1 = (f32[8,32,1024]{2,1,0:T(8,128)}, bf16[8,32,1024]{2,1,0:T(8,128)(2,1)S(1)}, f32[128,16,128]{2,1,0:T(8,128)S(1)}) custom-call(s32[1]{0:T(128)} %bitcast.core_ref, f32[64,16,128]{2,1,0:T(8,128)S(1)} %all-to-all-done.2.mine_ref, f32[64,16,128]{2,1,0:T(8,128)S(1)} %collective-permute-done.1.other_ref, bf16[8192,384]{1,0:T(8,128)(2,1)S(1)} %copy-done.6, ...), custom_call_target="tpu_custom_call" | custom-call | tf_op jit(solution)/shard_map/middle/pallas_call | solution.py:45
  154.3 23.3 %all_to_all.26.parts_ref = f32[128,16,128]{2,1,0:T(8,128)S(1)} all-to-all(f32[128,16,128]{2,1,0:T(8,128)S(1)} %get-tuple-element.16), channel_id=1, replica_groups=mesh['y'=4,'z'=4,'x'=4,'c'=2] {'y','z','x','c'}, dimensions={0} | all-to-all | bytes 2097152 | tf_op jit(solution)/shard_map/all_to_all | solution.py:424
  177.6 3.4 %copy-done.3 = bf16[16384,256]{1,0:T(8,128)(2,1)S(1)} copy-done((bf16[16384,256]{1,0:T(8,128)(2,1)S(1)}, bf16[16384,256]{1,0:T(8,128)(2,1)}, u32[]{:S(2)}) %copy-start.3) | copy-done | bytes 8388632
  181.0 1.6 solve.3
  182.6 17.6 %all_to_all.27.mine_ref = f32[64,16,128]{2,1,0:T(8,128)S(1)} all-to-all(f32[64,16,128]{2,1,0:T(8,128)S(1)} %solve.3), channel_id=1, replica_groups=mesh['y'=4,'z'=4,'x'=4,'c'=2] {'y','z','x'}, dimensions={0} | all-to-all | bytes 1048576 | tf_op jit(solution)/shard_map/all_to_all | solution.py:408
  200.2 5.8 %copy-done.5 = bf16[8,1024,1024]{2,1,0:T(8,128)(2,1)S(1)} copy-done((bf16[8,1024,1024]{2,1,0:T(8,128)(2,1)S(1)}, bf16[8,1024,1024]{2,1,0:T(8,128)(2,1)}, u32[]{:S(2)}) %copy-start.5) | copy-done | bytes 16777240
  206.0 5.6 %local_solve.3 = (f32[8,32,1024]{2,1,0:T(8,128)S(1)}, f32[32,2048]{1,0:T(8,128)S(1)}) custom-call(bf16[8,32,1024]{2,1,0:T(8,128)(2,1)S(1)} %get-tuple-element.17.scaled_ref, bf16[8,1024,1024]{2,1,0:T(8,128)(2,1)S(1)} %copy-done.5, bf16[2048,2048]{1,0:T(8,128)(2,1)S(1)} %bitcast.35, f32[8,1,256]{2,1,0:T(1,128)S(1)} %compare_select_fusion.mask_ref), custom_call_target="tpu_custom_call" | custom-call | flops 536870912 | bytes 37748736 | tf_op jit(solution)/shard_map/local_solve/pallas_call | solution.py:146
  211.6 2.1 collective-permute-start.8
  213.7 2.5 %collective-permute-done.8.next_ref = f32[32,1024]{1,0:T(8,128)S(1)} collective-permute-done((f32[32,1024]{1,0:T(8,128)S(1)}, f32[32,1024]{1,0:T(8,128)S(1)}, u32[]{:S(2)}, u32[]{:S(2)}) %collective-permute-start.8) | collective-permute-done | bytes 131104 | tf_op jit(solution)/shard_map/ppermute | solution.py:277
  216.2 7.3 %collective-permute-done.7.prev_ref = f32[32,1024]{1,0:T(8,128)S(1)} collective-permute-done((f32[32,1024]{1,0:T(8,128)S(1)}, f32[32,1024]{1,0:T(8,128)S(1)}, u32[]{:S(2)}, u32[]{:S(2)}) %collective-permute-start.7) | collective-permute-done | bytes 131104 | tf_op jit(solution)/shard_map/ppermute | solution.py:277
  223.5 2.7 %make_base.3.base_ref = f32[8,32,1024]{2,1,0:T(8,128)S(1)} custom-call(f32[8,32,1024]{2,1,0:T(8,128)S(1)} %get-tuple-element.18.local_ref, f32[32,2048]{1,0:T(8,128)S(1)} %get-tuple-element.19.sums_ref, f32[32,1024]{1,0:T(8,128)S(1)} %collective-permute-done.7.prev_ref, f32[32,1024]{1,0:T(8,128)S(1)} %collective-permute-done.8.next_ref, ...), custom_call_target="tpu_custom_call" | custom-call | flops 805306368 | bytes 14680064 | tf_op jit(solution)/shard_map/make_base/pallas_call | solution.py:45
  226.2 2.8 %copy-done.7 = bf16[8192,384]{1,0:T(8,128)(2,1)S(1)} copy-done((bf16[8192,384]{1,0:T(8,128)(2,1)S(1)}, bf16[8192,384]{1,0:T(8,128)(2,1)}, u32[]{:S(2)}) %copy-start.7) | copy-done | bytes 6291480
  229.0 3.3 %last.1 = f32[8,32,1024]{2,1,0:T(8,128)} custom-call(s32[1]{0:T(128)} %bitcast.core_ref, f32[64,16,128]{2,1,0:T(8,128)S(1)} %all_to_all.27.mine_ref, f32[64,16,128]{2,1,0:T(8,128)S(1)} %collective-permute-done.6.other_ref, bf16[8192,384]{1,0:T(8,128)(2,1)S(1)} %copy-done.7, bf16[384,2048]{1,0:T(8,128)(2,1)S(1)} %copy-done.9, ...), custom_call_target="tpu_custom_call" | custom-call | tf_op jit(solution)/shard_map/last/pallas_call | solution.py:45
  (72 shorter events, 3.6 us)
Async XLA Ops:
  2.1 58.1 %all-to-all-start.1 = ((s32[128,1,128]{2,1,0:T(1,128)}), s32[128,1,128]{2,1,0:T(1,128)S(1)}, u32[]{:S(2)}, u32[]{:S(2)}) async-start(s32[128,1,128]{2,1,0:T(1,128)} %broadcast_in_dim.144), calls=%async_computation.1 | async-start | bytes 131072 | tf_op jit(solution)/shard_map/all_to_all | solution.py:308
  21.4 12.0 %copy-start.14 = (f32[160,2048]{1,0:T(8,128)}, f32[160,2048]{1,0:T(8,128)S(1)}, u32[]{:S(2)}) copy-start(f32[160,2048]{1,0:T(8,128)S(1)} %fusion.2) | copy-start | bytes 3932164
  21.4 54.1 %collective-permute-start.2 = (f32[24,1024]{1,0:T(8,128)S(1)}, f32[24,1024]{1,0:T(8,128)}, u32[]{:S(2)}, u32[]{:S(2)}) collective-permute-start(f32[24,1024]{1,0:T(8,128)S(1)} %get-tuple-element.20), channel_id=1, source_target_pairs={{0,1},{1,2},{2,3},{3,4},{4,5},{5,6},{6,7},{7,8},{8,9},{9,10},{10,1... | collective-permute-start | bytes 294920 | tf_op jit(solution)/shard_map/ppermute | solution.py:277
  21.5 12.0 %copy-start.13 = (bf16[8,16,1024]{2,1,0:T(8,128)(2,1)S(1)}, bf16[8,16,1024]{2,1,0:T(8,128)(2,1)}, u32[]{:S(2)}) copy-start(bf16[8,16,1024]{2,1,0:T(8,128)(2,1)} %param.10) | copy-start | bytes 786436
  21.5 12.2 %copy-start.12 = (bf16[8,32,1024]{2,1,0:T(8,128)(2,1)S(1)}, bf16[8,32,1024]{2,1,0:T(8,128)(2,1)}, u32[]{:S(2)}) copy-start(bf16[8,32,1024]{2,1,0:T(8,128)(2,1)} %values_ref.1) | copy-start | bytes 1572868
  21.5 54.7 %collective-permute-start.3 = (f32[24,1024]{1,0:T(8,128)S(1)}, f32[24,1024]{1,0:T(8,128)}, u32[]{:S(2)}, u32[]{:S(2)}) collective-permute-start(f32[24,1024]{1,0:T(8,128)S(1)} %get-tuple-element.21), channel_id=1, source_target_pairs={{0,127},{1,0},{2,1},{3,2},{4,3},{5,4},{6,5},{7,6},{8,7},{9,8},{10,... | collective-permute-start | bytes 294920 | tf_op jit(solution)/shard_map/ppermute | solution.py:277
  28.6 48.4 %collective-permute-start = (f32[64,8192]{1,0:T(8,128)}, f32[64,8192]{1,0:T(8,128)}, u32[]{:S(2)}, u32[]{:S(2)}) collective-permute-start(f32[64,8192]{1,0:T(8,128)} %mine_ref.1), channel_id=1, source_target_pairs={{0,1},{1,0},{2,3},{3,2},{4,5},{5,4},{6,7},{7,6},{8,9},{9,8},{10,11... | collective-permute-start | bytes 6291464 | tf_op jit(solution)/shard_map/ppermute | solution.py:281
  35.7 3.4 %copy-start = (bf16[2048,2048]{1,0:T(8,128)(2,1)S(1)}, bf16[2048,2048]{1,0:T(8,128)(2,1)}, u32[]{:S(2)}) copy-start(bf16[2048,2048]{1,0:T(8,128)(2,1)} %fusion.slots_ref) | copy-start | bytes 25165828
  39.0 5.8 %copy-start.4 = (bf16[8,1024,1024]{2,1,0:T(8,128)(2,1)S(1)}, bf16[8,1024,1024]{2,1,0:T(8,128)(2,1)}, u32[]{:S(2)}) copy-start(bf16[8,1024,1024]{2,1,0:T(8,128)(2,1)} %inverse_ref.3) | copy-start | bytes 50331652
  44.8 9.4 %copy-start.15 = (s32[8]{0:T(128)S(1)}, s32[8]{0:T(128)}, u32[]{:S(2)}) copy-start(s32[8]{0:T(128)} %param.13) | copy-start | bytes 100
  50.4 1.1 copy-start.10
  52.2 93.0 %collective-permute-start.5 = (f32[32,1024]{1,0:T(8,128)}, f32[32,1024]{1,0:T(8,128)S(1)}, u32[]{:S(2)}, u32[]{:S(2)}) collective-permute-start(f32[32,1024]{1,0:T(8,128)} %get-tuple-element.24), channel_id=1, source_target_pairs={{0,127},{1,0},{2,1},{3,2},{4,3},{5,4},{6,5},{7,6},{8,7},{9,8},{10,... | collective-permute-start | bytes 393224 | tf_op jit(solution)/shard_map/ppermute | solution.py:277
  54.2 91.0 %collective-permute-start.4 = (f32[32,1024]{1,0:T(8,128)}, f32[32,1024]{1,0:T(8,128)S(1)}, u32[]{:S(2)}, u32[]{:S(2)}) collective-permute-start(f32[32,1024]{1,0:T(8,128)} %get-tuple-element.25), channel_id=1, source_target_pairs={{0,1},{1,2},{2,3},{3,4},{4,5},{5,6},{6,7},{7,8},{8,9},{9,10},{10,1... | collective-permute-start | bytes 393224 | tf_op jit(solution)/shard_map/ppermute | solution.py:277
  60.2 48.6 %all-to-all-start = ((f32[128,16,128]{2,1,0:T(8,128)}), f32[128,16,128]{2,1,0:T(8,128)}, u32[]{:S(2)}, u32[]{:S(2)}) async-start(f32[128,16,128]{2,1,0:T(8,128)} %get-tuple-element.11), calls=%async_computation | async-start | bytes 2097152 | tf_op jit(solution)/shard_map/all_to_all | solution.py:334
  105.6 3.3 %copy-start.1 = (bf16[16384,256]{1,0:T(8,128)(2,1)}, bf16[16384,256]{1,0:T(8,128)(2,1)S(1)}, u32[]{:S(2)}) copy-start(bf16[16384,256]{1,0:T(8,128)(2,1)S(1)} %pick.1.picked_ref) | copy-start | bytes 25165828
  108.8 3.4 %copy-start.2 = (bf16[16384,256]{1,0:T(8,128)(2,1)S(1)}, bf16[16384,256]{1,0:T(8,128)(2,1)}, u32[]{:S(2)}) copy-start(bf16[16384,256]{1,0:T(8,128)(2,1)} %copy-done.1) | copy-start | bytes 25165828
  115.8 23.6 %all-to-all-start.2 = ((f32[64,16,128]{2,1,0:T(8,128)}), f32[64,16,128]{2,1,0:T(8,128)S(1)}, u32[]{:S(2)}, u32[]{:S(2)}) async-start(f32[64,16,128]{2,1,0:T(8,128)} %solve.2), calls=%async_computation.2 | async-start | bytes 1048576 | tf_op jit(solution)/shard_map/all_to_all | solution.py:408
  139.5 8.4 %collective-permute-start.1 = (f32[64,16,128]{2,1,0:T(8,128)S(1)}, f32[64,16,128]{2,1,0:T(8,128)S(1)}, u32[]{:S(2)}, u32[]{:S(2)}) collective-permute-start(f32[64,16,128]{2,1,0:T(8,128)S(1)} %all-to-all-done.2.mine_ref), channel_id=1, source_target_pairs={{0,1},{1,0},{2,3},{3,2},{4,5},{5,4},{6,7},{7,6},{8,9},{9,8},{10,11... | collective-permute-start | bytes 1572872 | tf_op jit(solution)/shard_map/ppermute | solution.py:281
  139.5 5.7 %slice-start = ((s8[8388608]{0:T(1024)(128)(4,1)}), s8[4194304]{0:T(1024)(128)(4,1)S(1)}, s32[]{:S(2)}) async-start(s8[8388608]{0:T(1024)(128)(4,1)} %bitcast.34), calls=%async_computation.5 | async-start | bytes 8388608
  139.6 5.6 %slice-start.1 = ((s8[8388608]{0:T(1024)(128)(4,1)}), s8[4194304]{0:T(1024)(128)(4,1)S(1)}, s32[]{:S(2)}) async-start(s8[8388608]{0:T(1024)(128)(4,1)} %bitcast.34), calls=%async_computation.6 | async-start | bytes 8388608
  139.6 5.6 %copy-start.11 = (f32[8,32,1024]{2,1,0:T(8,128)S(1)}, f32[8,32,1024]{2,1,0:T(8,128)}, u32[]{:S(2)}) copy-start(f32[8,32,1024]{2,1,0:T(8,128)} %copy-done.10) | copy-start | bytes 3145732
  145.1 2.8 %copy-start.8 = (bf16[384,2048]{1,0:T(8,128)(2,1)}, bf16[384,2048]{1,0:T(8,128)(2,1)S(1)}, u32[]{:S(2)}) copy-start(bf16[384,2048]{1,0:T(8,128)(2,1)S(1)} %fusion.6.shared_ref) | copy-start | bytes 4718596
  147.9 2.8 %copy-start.6 = (bf16[8192,384]{1,0:T(8,128)(2,1)S(1)}, bf16[8192,384]{1,0:T(8,128)(2,1)}, u32[]{:S(2)}) copy-start(bf16[8192,384]{1,0:T(8,128)(2,1)} %fusion.3.hot_ref) | copy-start | bytes 18874372
  177.6 3.4 %copy-start.3 = (bf16[16384,256]{1,0:T(8,128)(2,1)S(1)}, bf16[16384,256]{1,0:T(8,128)(2,1)}, u32[]{:S(2)}) copy-start(bf16[16384,256]{1,0:T(8,128)(2,1)} %copy-done.1) | copy-start | bytes 25165828
  200.2 25.9 %collective-permute-start.6 = (f32[64,16,128]{2,1,0:T(8,128)S(1)}, f32[64,16,128]{2,1,0:T(8,128)S(1)}, u32[]{:S(2)}, u32[]{:S(2)}) collective-permute-start(f32[64,16,128]{2,1,0:T(8,128)S(1)} %all_to_all.27.mine_ref), channel_id=1, source_target_pairs={{0,1},{1,0},{2,3},{3,2},{4,5},{5,4},{6,7},{7,6},{8,9},{9,8},{10,11... | collective-permute-start | bytes 1572872 | tf_op jit(solution)/shard_map/ppermute | solution.py:281
  200.2 5.8 %copy-start.5 = (bf16[8,1024,1024]{2,1,0:T(8,128)(2,1)S(1)}, bf16[8,1024,1024]{2,1,0:T(8,128)(2,1)}, u32[]{:S(2)}) copy-start(bf16[8,1024,1024]{2,1,0:T(8,128)(2,1)} %inverse_ref.3) | copy-start | bytes 50331652
  211.6 4.6 %collective-permute-start.8 = (f32[32,1024]{1,0:T(8,128)S(1)}, f32[32,1024]{1,0:T(8,128)S(1)}, u32[]{:S(2)}, u32[]{:S(2)}) collective-permute-start(f32[32,1024]{1,0:T(8,128)S(1)} %get-tuple-element.22), channel_id=1, source_target_pairs={{0,127},{1,0},{2,1},{3,2},{4,3},{5,4},{6,5},{7,6},{8,7},{9,8},{10,... | collective-permute-start | bytes 393224 | tf_op jit(solution)/shard_map/ppermute | solution.py:277
  213.7 9.8 %collective-permute-start.7 = (f32[32,1024]{1,0:T(8,128)S(1)}, f32[32,1024]{1,0:T(8,128)S(1)}, u32[]{:S(2)}, u32[]{:S(2)}) collective-permute-start(f32[32,1024]{1,0:T(8,128)S(1)} %get-tuple-element.23), channel_id=1, source_target_pairs={{0,1},{1,2},{2,3},{3,4},{4,5},{5,6},{6,7},{7,8},{8,9},{9,10},{10,1... | collective-permute-start | bytes 393224 | tf_op jit(solution)/shard_map/ppermute | solution.py:277
  223.5 2.7 %copy-start.9 = (bf16[384,2048]{1,0:T(8,128)(2,1)S(1)}, bf16[384,2048]{1,0:T(8,128)(2,1)}, u32[]{:S(2)}) copy-start(bf16[384,2048]{1,0:T(8,128)(2,1)} %copy-done.8) | copy-start | bytes 4718596
  226.2 2.8 %copy-start.7 = (bf16[8192,384]{1,0:T(8,128)(2,1)S(1)}, bf16[8192,384]{1,0:T(8,128)(2,1)}, u32[]{:S(2)}) copy-start(bf16[8192,384]{1,0:T(8,128)(2,1)} %fusion.3.hot_ref) | copy-start | bytes 18874372

commit v2 on v0

v2 whole, which is shorter than its diff:
```python
import jax
import jax.numpy as jnp
from jax import lax
from jax.experimental import pallas as pl
from jax.experimental.pallas import tpu as pltpu
from jax.sharding import Mesh
from jax.sharding import PartitionSpec as P

CHIPS = ("y", "z", "x")
DOM = ("y", "z", "x", "c")
MIB = 2**20
VMEM = pl.BlockSpec(memory_space=pltpu.VMEM)
SMEM = pl.BlockSpec(memory_space=pltpu.SMEM)
ANY = pl.BlockSpec(memory_space=pl.ANY)
HBM = pl.BlockSpec(memory_space=pltpu.HBM)
BY_ROW = (((1,), (1,)), ((), ()))


def halves(value):
    high = value.astype(jnp.bfloat16)
    low = (value - high.astype(jnp.float32)).astype(jnp.bfloat16)
    return jnp.concatenate([high, low], axis=0)


def thirds(value):
    high = value.astype(jnp.bfloat16)
    rest = value - high.astype(jnp.float32)
    middle = rest.astype(jnp.bfloat16)
    low = (rest - middle.astype(jnp.float32)).astype(jnp.bfloat16)
    return jnp.concatenate([high, middle, low], axis=0)


def folded(out, rows):
    total = out[:rows]
    for start in range(rows, out.shape[0], rows):
        total = total + out[start : start + rows]
    return total


def mul(left, right):
    return jnp.dot(left, right, preferred_element_type=jnp.float32)


def mul_rows(left, right):
    return lax.dot_general(left, right, BY_ROW, preferred_element_type=jnp.float32)


def call(kernel, name, out_shape, args, specs, flops=1e6, moved=MIB, mib=16, **more):
    return pl.pallas_call(
        kernel,
        out_shape=out_shape,
        in_specs=specs,
        compiler_params=pltpu.CompilerParams(vmem_limit_bytes=mib * MIB),
        cost_estimate=pl.CostEstimate(
            flops=int(flops), bytes_accessed=int(moved), transcendentals=0
        ),
        name=name,
        **more,
    )(*args)


def f32(*shape):
    return jax.ShapeDtypeStruct(shape, jnp.float32)


def bf16(*shape):
    return jax.ShapeDtypeStruct(shape, jnp.bfloat16)


def weights_of(multiplicity):
    return 1.0 / multiplicity.astype(jnp.float32)


def part_out(core_ref, scaled_ref, basis_ref, keep_ref, send_ref):
    parts = mul_rows(scaled_ref[0], basis_ref[0])
    for sub in range(1, basis_ref.shape[0]):
        parts = parts + mul_rows(scaled_ref[sub], basis_ref[sub])
    half = keep_ref.shape[0]
    first = core_ref[0] == 0
    keep_ref[...] = jnp.where(first, parts[:half], parts[half:])
    send_ref[...] = jnp.where(first, parts[half:], parts[:half])


def widen(basis_ref, wide_ref):
    subs, coarse, _ = basis_ref.shape
    for sub in range(subs):
        wide_ref[sub] = jnp.zeros_like(wide_ref[sub])
        wide_ref[sub, sub * coarse : (sub + 1) * coarse] = basis_ref[sub]


def first_kernel(
    core_ref, values_ref, mult_ref, basis_ref, scaled_ref, keep_ref, send_ref, wide_ref
):
    widen(basis_ref, wide_ref)
    for sub in range(values_ref.shape[0]):
        scaled = values_ref[sub].astype(jnp.float32) * weights_of(mult_ref[sub : sub + 1])
        scaled_ref[sub] = scaled.astype(jnp.bfloat16)
    part_out(core_ref, scaled_ref, wide_ref, keep_ref, send_ref)


def hot_pair(maps, pair):
    rows = lax.broadcasted_iota(jnp.int32, (256, maps.shape[1]), 0) + 256 * pair
    return jnp.where(rows == maps, 1.0, 0.0).astype(jnp.bfloat16)


def columns_of(rows):
    if rows.shape[0] == 1:
        rows = jnp.broadcast_to(rows, (8, rows.shape[1]))
    return rows.astype(jnp.float32).T


def dense_kernel(own_ref, mate_ref, keep_ref, got_ref, *refs):
    out_ref = refs[-1]
    cases, width = keep_ref.shape
    value = halves(jnp.concatenate([keep_ref[...], got_ref[...]], axis=1))
    maps = jnp.concatenate([own_ref[...], mate_ref[...]], axis=1)
    maps = columns_of(maps)[:, :1]
    wide = 2 * out_ref.shape[2]
    for pair in range(out_ref.shape[0] // 2):
        numbers = lax.broadcasted_iota(jnp.int32, (maps.shape[0], wide), 1) + wide * pair
        hot = jnp.where(numbers.astype(jnp.float32) == maps, 1.0, 0.0).astype(jnp.bfloat16)
        part = folded(mul(value, hot), cases)
        out_ref[2 * pair] = part[:, : wide // 2]
        out_ref[2 * pair + 1] = part[:, wide // 2 :]


def sum_kernel(parts_ref, *refs):
    out_ref = refs[-1]
    total = parts_ref[0]
    for chip in range(1, parts_ref.shape[0]):
        total = total + parts_ref[chip]
    for chip in range(out_ref.shape[0]):
        out_ref[chip] = total


def solve_kernel(core_ref, rhs_ref, mine_ref, other_ref, out_ref):
    cases, width = rhs_ref.shape[1:]
    total = jnp.zeros((2 * cases, 4 * mine_ref.shape[0]), jnp.float32)
    for pair in range(rhs_ref.shape[0] // 2):
        value = jnp.concatenate([rhs_ref[2 * pair], rhs_ref[2 * pair + 1]], axis=1)
        columns = slice(2 * pair * width, 2 * (pair + 1) * width)
        rows = jnp.concatenate([mine_ref[:, columns], other_ref[:, columns]], axis=0)
        total = total + mul_rows(halves(value), halves(rows))
    total = folded(total, cases)
    own = total[:, :width] + total[:, width:]
    half = width // 2
    turned = jnp.concatenate([own[:, half:], own[:, :half]], axis=1)
    own = jnp.where(core_ref[0] == 0, own, turned)
    for chip in range(out_ref.shape[0]):
        out_ref[chip] = own


def live_of(len_ref, sub, width):
    return lax.broadcasted_iota(jnp.int32, (1, width), 1) < len_ref[sub]


def slot_row(place_ref, len_ref, dof_ref, sub, spots):
    owned = spots // 2
    dof = dof_ref[sub : sub + 1]
    owner = lax.div(dof, owned)
    away = (owner != place_ref[0]).astype(jnp.int32)
    far = jnp.where(place_ref[1] == 0, away, 1 - away)
    live = live_of(len_ref, sub, dof.shape[1])
    return jnp.where(live, far * owned + (dof - owner * owned), -1)


def slots_of(place_ref, len_ref, dof_ref, sub, spots):
    slot = slot_row(place_ref, len_ref, dof_ref, sub, spots)
    rows = lax.broadcasted_iota(jnp.int32, (spots, slot.shape[1]), 0)
    return jnp.where(rows == slot, 1.0, 0.0).astype(jnp.bfloat16)


def column_copies(inverse_ref, buffer_ref, sems, start):
    copies = []
    for sub in range(inverse_ref.shape[0]):
        columns = pl.ds(start, buffer_ref.shape[2])
        copies.append(
            pltpu.make_async_copy(
                inverse_ref.at[sub, :, columns], buffer_ref.at[sub], sems.at[sub]
            )
        )
    for copy in copies:
        copy.start()
    return copies


def edge_kernel(place_ref, len_ref, scaled_ref, mult_ref, dof_ref, inverse_ref, *refs):
    *inputs, edge_ref, mate_ref, far_ref, buffer_ref, sems = refs
    subs, cases, _ = scaled_ref.shape
    width = dof_ref.shape[1]
    owned = mate_ref.shape[1]
    copies = column_copies(inverse_ref, buffer_ref, sems, 0)
    mate_ref[...] = jnp.zeros_like(mate_ref)
    far_ref[...] = jnp.zeros_like(far_ref)
    if inputs:
        basis_ref, map_ref, own_ref = inputs
        coarse = basis_ref.shape[1]
        for ref in (mate_ref, far_ref):
            ref[cases + coarse + 8 : cases + coarse + 9, : map_ref.shape[1]] = map_ref[
                ...
            ].astype(jnp.float32)
    slots = [slot_row(place_ref, len_ref, dof_ref, sub, 2 * owned) for sub in range(subs)]
    slots = columns_of(jnp.concatenate(slots, axis=0))
    numbers = lax.broadcasted_iota(jnp.int32, (width, 2 * owned), 1).astype(jnp.float32)
    for sub in range(subs):
        hot = jnp.where(numbers == slots[:, sub : sub + 1], 1.0, 0.0).astype(jnp.bfloat16)
        live = live_of(len_ref, sub, width)
        mask = jnp.where(live, weights_of(mult_ref[sub : sub + 1, :width]), 0.0)
        copies[sub].wait()
        solved = mul(scaled_ref[sub], buffer_ref[sub])
        edge_ref[:, sub * width : (sub + 1) * width] = solved
        pieces = [thirds(solved * mask)]
        if inputs:
            pieces.append((basis_ref[sub, :, :width].astype(jnp.float32) * mask).astype(jnp.bfloat16))
            number = jnp.where(live, float(sub), 0.0).astype(jnp.bfloat16)
            pieces.append(jnp.broadcast_to(number, (16, width)))
        out = mul(jnp.concatenate(pieces, axis=0), hot)
        moved = folded(out[: 3 * cases], cases)
        if inputs:
            rest = out[3 * cases : 3 * cases + coarse + 8]
            own_ref[sub * coarse : (sub + 1) * coarse, :] = rest[:coarse].astype(jnp.bfloat16)
            moved = jnp.concatenate([moved, rest], axis=0)
        mate_ref[: moved.shape[0]] += moved[:, :owned]
        far_ref[: moved.shape[0]] += moved[:, owned:]


def inner_kernel(scaled_ref, inverse_ref, after_ref, after_too_ref, inner_ref, buffer_ref, sems):
    copies = column_copies(
        inverse_ref, buffer_ref, sems, inverse_ref.shape[2] - buffer_ref.shape[2]
    )
    for sub in range(scaled_ref.shape[0]):
        copies[sub].wait()
        inner_ref[sub] = mul(scaled_ref[sub], buffer_ref[sub])


def head_kernel(
    place_ref,
    len_ref,
    edge_ref,
    mate_ref,
    far_ref,
    from_mate_ref,
    from_far_ref,
    dof_ref,
    after_ref,
    head_ref,
):
    subs, width = dof_ref.shape
    cases = edge_ref.shape[0]
    sums = thirds(
        jnp.concatenate(
            [
                mate_ref[:cases] + from_mate_ref[:cases],
                far_ref[:cases] + from_far_ref[:cases],
            ],
            axis=1,
        )
    )
    for sub in range(subs):
        columns = slice(sub * width, (sub + 1) * width)
        hot = slots_of(place_ref, len_ref, dof_ref, sub, sums.shape[1])
        fetched = folded(mul(sums, hot), cases)
        head_ref[:, columns] = jnp.where(
            live_of(len_ref, sub, width), fetched, edge_ref[:, columns]
        )


def share_kernel(
    place_ref,
    len_ref,
    own_ref,
    from_mate_ref,
    from_far_ref,
    dof_ref,
    basis_ref,
    after_ref,
    shared_ref,
    map_ref,
    first_ref,
    second_ref,
):
    subs, coarse, _ = basis_ref.shape
    entries, spots = own_ref.shape
    owned = spots // 2
    width = dof_ref.shape[1]
    cases = from_mate_ref.shape[0] - 16 - coarse
    for ref, arrived, start in ((first_ref, from_mate_ref, 0), (second_ref, from_far_ref, owned)):
        ref[:entries] = own_ref[:, start : start + owned]
        row = arrived[cases + coarse : cases + coarse + 1]
        basis = arrived[cases : cases + coarse]
        for sub in range(subs):
            ref[entries + sub * coarse : entries + (sub + 1) * coarse] = jnp.where(
                row == sub, basis, 0.0
            ).astype(jnp.bfloat16)
    for sub in range(subs):
        columns = slice(sub * width, (sub + 1) * width)
        hot = slots_of(place_ref, len_ref, dof_ref, sub, spots)
        mate = mul(first_ref[...], hot[:owned])
        far = mul(second_ref[...], hot[owned:])
        own = mate[:entries] + far[:entries]
        rows = slice(sub * coarse, (sub + 1) * coarse)
        full = jnp.concatenate([own, mate[entries:], far[entries:]], axis=0)
        shared_ref[:, columns] = full.astype(jnp.bfloat16)
        dead = jnp.where(
            live_of(len_ref, sub, width), 0.0, basis_ref[sub, :, :width].astype(jnp.float32)
        )
        shared_ref[rows, columns] = (own[rows] + dead).astype(jnp.bfloat16)
    number = from_far_ref[cases + coarse + 8 : cases + coarse + 9, :entries]
    map_ref[...] = number.astype(jnp.int32)


def correct_kernel(
    core_ref,
    own_ref,
    mate_ref,
    far_ref,
    mine_ref,
    other_ref,
    basis_ref,
    head_ref,
    shared_hbm,
    inner_hbm,
    *refs,
):
    *inputs, wide_ref, shared_ref, inner_ref, values_ref, sems = refs
    out_hbm = inputs[0] if len(inputs) == 1 else inputs[1]
    subs, cases, _ = values_ref.shape
    chips, half, _ = mine_ref.shape
    entries = own_ref.shape[1]
    width = head_ref.shape[1] // subs
    arrive = [
        pltpu.make_async_copy(shared_hbm, shared_ref, sems.at[0]),
        pltpu.make_async_copy(inner_hbm, inner_ref, sems.at[1]),
    ]
    leave = [
        pltpu.make_async_copy(values_ref.at[sub], out_hbm.at[sub], sems.at[2 + sub])
        for sub in range(subs)
    ]
    for copy in arrive:
        copy.start()
    widen(basis_ref, wide_ref)
    maps = jnp.concatenate([own_ref[...], mate_ref[...], far_ref[...]], axis=1)
    looked = jnp.zeros((4 * half, 3 * entries), jnp.float32)
    for pair in range(chips // 2):
        mine = jnp.concatenate([mine_ref[2 * pair], mine_ref[2 * pair + 1]], axis=1)
        other = jnp.concatenate([other_ref[2 * pair], other_ref[2 * pair + 1]], axis=1)
        both = halves(jnp.concatenate([mine, other], axis=0))
        looked = looked + mul(both, hot_pair(maps, pair))
    looked = folded(looked, cases)
    turned = jnp.concatenate([looked[half:], looked[:half]], axis=0)
    looked = jnp.where(core_ref[0] == 0, looked, turned)
    own = thirds(looked[:, :entries])
    looked = thirds(looked)
    for copy in arrive:
        copy.wait()
    for sub in range(subs):
        columns = slice(sub * width, (sub + 1) * width)
        values_ref[sub, :, :width] = head_ref[:, columns] + folded(
            mul(looked, shared_ref[:, columns]), cases
        )
        values_ref[sub, :, width:] = inner_ref[sub] + folded(
            mul(own, wide_ref[sub, :, width:]), cases
        )
        leave[sub].start()
    if len(inputs) > 1:
        mult_ref, _, scaled_ref, keep_ref, send_ref = inputs
        for sub in range(subs):
            scaled = values_ref[sub] * weights_of(mult_ref[sub : sub + 1])
            scaled_ref[sub] = scaled.astype(jnp.bfloat16)
        part_out(core_ref, scaled_ref, wide_ref, keep_ref, send_ref)
    for copy in leave:
        copy.wait()


def swap(value):
    return lax.ppermute(value, "c", [(0, 1), (1, 0)])


def far_swap(value):
    count = lax.axis_size(DOM)
    pairs = []
    for device in range(1, count, 2):
        after = (device + 1) % count
        pairs += [(device, after), (after, device)]
    return lax.ppermute(value, DOM, pairs)


def by_chip(value):
    return lax.all_to_all(value, CHIPS, 0, 0, tiled=True)


def local(
    residual_in,
    local_inverse,
    coarse_basis,
    coarse_inverse,
    multiplicity,
    iface_len,
    iface_dof,
    coarse_map,
):
    subs, cases, length = residual_in.shape
    coarse = coarse_basis.shape[1]
    width = iface_dof.shape[1]
    rows, order = coarse_inverse.shape
    chips = lax.axis_size(DOM) // 2
    half = cases // 2
    entries = subs * coarse
    spots = subs * width
    owned = spots // 2
    place = jnp.stack([lax.axis_index(DOM), lax.axis_index("c")]).astype(jnp.int32)
    core = place[1:]
    own_map = coarse_map.reshape(1, entries)
    slot_flops = 2 * 3 * cases * spots * spots
    sent = cases + coarse + 16
    blocks = f32(chips, half, order // chips)

    def buffers(count):
        return [
            pltpu.VMEM((subs, length, count), jnp.bfloat16),
            pltpu.SemaphoreType.DMA((subs,)),
        ]

    mate_map = swap(own_map)
    scaled, keep, send = call(
        first_kernel,
        "first",
        (bf16(subs, cases, length), f32(half, entries), f32(half, entries)),
        (core, residual_in, multiplicity, coarse_basis),
        [SMEM, VMEM, VMEM, VMEM],
        mib=60,
        scratch_shapes=[pltpu.VMEM((subs, entries, length), jnp.bfloat16)],
    )
    got = swap(send)
    other_rows = swap(coarse_inverse)

    def dense(keep, got, *after):
        parts = call(
            dense_kernel,
            "dense",
            blocks,
            (own_map, mate_map, keep, got, *after),
            [VMEM] * 4 + [ANY] * len(after),
        )
        return by_chip(parts)

    def local_solve(scaled, *more):
        specs = [SMEM] * 2 + [VMEM] * 3 + [HBM] + [VMEM] * len(more)
        rows = sent if more else cases
        outs = [bf16(entries, spots)] if more else []
        outs += [f32(cases, spots), f32(rows, owned), f32(rows, owned)]
        *own_basis, edge, mate, far = call(
            edge_kernel,
            "edge",
            tuple(outs),
            (place, iface_len, scaled, multiplicity, iface_dof, local_inverse, *more),
            specs,
            flops=slot_flops,
            moved=local_inverse.size // 2,
            mib=50,
            scratch_shapes=buffers(width),
        )
        from_far, from_mate = far_swap(far), swap(mate)
        inner = call(
            inner_kernel,
            "inner",
            f32(subs, cases, length - width),
            (scaled, local_inverse, mate, far),
            [VMEM, HBM, ANY, ANY],
            flops=2 * scaled.size * (length - width),
            moved=local_inverse.size * 3 // 2,
            mib=50,
            scratch_shapes=buffers(length - width),
        )
        return inner, edge, mate, far, from_mate, from_far, own_basis

    def coarse_solve(parts, after):
        rhs = call(
            sum_kernel, "sum", blocks, (parts, *after), [VMEM] + [ANY] * len(after)
        )
        rhs = by_chip(rhs)
        own = call(
            solve_kernel,
            "solve",
            blocks,
            (core, rhs, coarse_inverse, other_rows),
            [SMEM] + [VMEM] * 3,
        )
        return by_chip(own)

    def assemble(edge, mate, far, from_mate, from_far, after):
        return call(
            head_kernel,
            "head",
            f32(cases, spots),
            (place, iface_len, edge, mate, far, from_mate, from_far, iface_dof, after),
            [SMEM] * 2 + [VMEM] * 6 + [ANY],
            flops=slot_flops,
        )

    def correct(mine, head, shared, inner, *more):
        specs = [SMEM] + [VMEM] * 7 + [HBM] * 2 + [VMEM] * len(more)
        outs, out_specs = [f32(subs, cases, length)], [HBM]
        if more:
            outs += [bf16(subs, cases, length), f32(half, entries), f32(half, entries)]
            out_specs += [VMEM] * 3
        return call(
            correct_kernel,
            "correct",
            tuple(outs),
            (
                core,
                own_map,
                mate_map,
                far_map,
                mine,
                swap(mine),
                coarse_basis,
                head,
                shared,
                inner,
                *more,
            ),
            specs,
            out_specs=tuple(out_specs),
            scratch_shapes=[
                pltpu.VMEM((subs, entries, length), jnp.bfloat16),
                pltpu.VMEM((3 * entries, spots), jnp.bfloat16),
                pltpu.VMEM((subs, cases, length - width), jnp.float32),
                pltpu.VMEM((subs, cases, length), jnp.float32),
                pltpu.SemaphoreType.DMA((2 + subs,)),
            ],
        )

    inner, *arrays, from_mate, from_far, (own_basis,) = local_solve(scaled, coarse_basis, own_map)
    parts = dense(keep, got, inner, from_far, from_mate)
    head = assemble(*arrays, from_mate, from_far, parts)
    shared, far_map = call(
        share_kernel,
        "share",
        (bf16(3 * entries, spots), jax.ShapeDtypeStruct((1, entries), jnp.int32)),
        (place, iface_len, own_basis, from_mate, from_far, iface_dof, coarse_basis, parts),
        [SMEM] * 2 + [VMEM] * 5 + [ANY],
        flops=2 * 2 * entries * spots * spots,
        scratch_shapes=[pltpu.VMEM((2 * entries, owned), jnp.bfloat16)] * 2,
    )
    mine = coarse_solve(parts, (head, shared))
    first_apply, scaled, keep, send = correct(mine, head, shared, inner, multiplicity)

    inner, *arrays, from_mate, from_far, _ = local_solve(scaled)
    parts = dense(keep, swap(send), inner, from_far, from_mate)
    head = assemble(*arrays, from_mate, from_far, parts)
    mine = coarse_solve(parts, (head,))
    (second_apply,) = correct(mine, head, shared, inner)
    return first_apply, second_apply


def solution(mesh):
    grid = Mesh(mesh.devices.reshape(4, 4, 4, 2), DOM)
    placed = (
        P(DOM, None, None),
        P(DOM, None, None),
        P(DOM, None, None),
        P(DOM, None),
        P(DOM, None),
        P(DOM),
        P(DOM, None),
        P(DOM, None),
    )
    return jax.shard_map(
        local,
        mesh=grid,
        in_specs=placed,
        out_specs=(P(DOM, None, None), P(DOM, None, None)),
        check_vma=False,
    )
```

time: 584 us -> 175 us (0.30)
  waiting for transfers between devices: 440 us -> 7.13 us
  blocking collectives: 0 us -> 105 us
  Pallas kernels: 0 us -> 43.8 us
  other arithmetic: 41.4 us -> 0.07 us
  matrix products: 41.3 us -> 0 us
  local copies, waits for them, and re-layouts: 38.8 us -> 4.9 us
  between operations: 14.1 us -> 1.04 us
    psum x2 -> x0, waiting for transfers between devices: 290 us -> none  [precondition(): coarse_rhs = lax.psum(local_rhs, 'dom')]
    all_gather x2 -> x0, waiting for transfers between devices: 110 us -> none  [precondition(): coarse_sol = lax.all_gather(own_sol, 'dom', axis=1, tiled=True)]
    all_to_all x0 -> x6, blocking collectives: none -> 105 us  [by_chip(): return lax.all_to_all(value, CHIPS, 0, 0, tiled=True)]
    pallas_call x0 -> x16, Pallas kernels: none -> 43.8 us  [call(): pl.pallas_call(kernel, out_shape=out_shape, in_specs=specs, compiler_para...]
    dot_general x12 -> x0, matrix products: 41.3 us -> none  [the longest x2 19.5 us: precondition(): jnp.einsum('srl,slm->srm', scaled, local_inverse, preferred_element_type=...]
    ppermute x4 -> x10, waiting for transfers between devices: 40.8 us -> 7.13 us  [the longest x8 3.83 us: swap(): return lax.ppermute(value, 'c', [(0, 1), (1, 0)])]
    scatter-add x2 -> x0, other arithmetic: 29.5 us -> none  [precondition(): jnp.zeros((cases, 2 * own_width), jnp.float32).at[:, position]]
    gather x2 -> x0, local copies, waits for them, and re-layouts: 15.2 us -> none  [precondition(): jnp.take(both, position, axis=1).reshape(cases, sub_count, iface_width)]
  transfers between devices with their start and end apart: 8 -> 10, of which waited for: 8 -> 3; matrix products, arithmetic and copies ran while one was open for 4% -> 0% of each run, Pallas kernels for 0% -> 15%
where the time goes in v2:
time: 175 us; the launch traced here: 173 us
  blocking collectives  105 us (60%)
  Pallas kernels  43.8 us (25%)
  starting transfers between devices  11.2 us (6%)
  waiting for transfers between devices  7.13 us (4%)
  local copies, waits for them, and re-layouts  4.9 us (3%)
    all_to_all x6, blocking collectives, by_chip(): return lax.all_to_all(value, CHIPS, 0, 0, tiled=True)  105 us
    pallas_call x16, Pallas kernels, call(): pl.pallas_call(kernel, out_shape=out_shape, in_specs=specs, compiler_para...  43.8 us
    ppermute x2, starting transfers between devices, far_swap(): return lax.ppermute(value, DOM, pairs)  9.84 us
    unnamed x24, local copies, waits for them, and re-layouts  4.13 us
    ppermute x8, waiting for transfers between devices, swap(): return lax.ppermute(value, 'c', [(0, 1), (1, 0)])  3.83 us
  transfers between devices with their start and end apart: 10, of which 3 were waited for; matrix products, arithmetic and copies ran while one was open for 0% of the time, Pallas kernels for 15%

profile of v2, /device:TPU:0, one launch (start us, length us, event | category | flops | bytes accessed | tf_op | source)
XLA Modules:
  0.0 173.4 jit_solution(3947928999396282922)
XLA Ops:
  0.6 0.1 collective-permute-start.4
  0.7 0.8 reshape.7.refs_1_.own_ref
  1.5 2.5 %first.1 = (bf16[8,32,1024]{2,1,0:T(8,128)(2,1)}, f32[16,128]{1,0:T(8,128)}, f32[16,128]{1,0:T(8,128)}) custom-call(s32[1]{0:T(128)} %bitcast.core_ref, bf16[8,32,1024]{2,1,0:T(8,128)(2,1)} %values_ref.1, s32[8,1024]{1,0:T(8,128)} %mult_ref.5, bf16[8,16,1024]{2,1,0:T(8,128)(2,1)} %basis_ref.7), custom_call_target="tpu_custom_call" | custom-call | flops 1000000 | bytes 1048576 | tf_op jit(solution)/shard_map/first/pallas_call | solution.py:49
  4.0 0.1 pad_add_fusion.place_ref
  4.1 0.9 copy-done.1
  5.0 1.0 copy-done.3
  6.1 0.8 copy-done.5
  6.8 0.7 copy-done.6
  7.5 0.7 copy-done.9
  8.2 6.4 %edge.2 = (bf16[128,2048]{1,0:T(8,128)(2,1)S(1)}, f32[32,2048]{1,0:T(8,128)S(1)}, f32[64,1024]{1,0:T(8,128)S(1)}, f32[64,1024]{1,0:T(8,128)S(1)}) custom-call(s32[2]{0:T(128)S(1)} %pad_add_fusion.place_ref, s32[8]{0:T(128)S(1)} %copy-done.9, bf16[8,32,1024]{2,1,0:T(8,128)(2,1)S(1)} %copy-done.3, s32[8,1024]{1,0:T(8,128)S(1)} %copy-done.5, ...), custom_call_target="tpu_custom_call" | custom-call | flops 805306368 | bytes 4194304 | tf_op jit(solution)/shard_map/edge/pallas_call | solution.py:49
  14.6 0.6 collective-permute-start.1
  15.2 8.5 %collective-permute-start.2 = (f32[64,1024]{1,0:T(8,128)S(1)}, f32[64,1024]{1,0:T(8,128)S(1)}, u32[]{:S(2)}, u32[]{:S(2)}) collective-permute-start(f32[64,1024]{1,0:T(8,128)S(1)} %get-tuple-element.21.after_too_ref.far_ref), channel_id=1, source_target_pairs={{1,2},{2,1},{3,4},{4,3},{5,6},{6,5},{7,8},{8,7},{9,10},{10,9},{11,... | collective-permute-start | bytes 786440 | tf_op jit(solution)/shard_map/ppermute | solution.py:385
  23.7 0.0 collective-permute-start
  23.7 0.5 collective-permute-start.3
  24.2 5.1 %inner.2.refs_0_.inner_hbm = f32[8,32,768]{2,1,0:T(8,128)S(1)} custom-call(bf16[8,32,1024]{2,1,0:T(8,128)(2,1)S(1)} %copy-done.4, bf16[8,1024,1024]{2,1,0:T(8,128)(2,1)} %inverse_ref.7, f32[64,1024]{1,0:T(8,128)S(1)} %get-tuple-element.20.after_ref.mate_ref, f32[64,1024]{1,0:T(8,128)S(1)} %get-tuple-element.21.after_too_ref.far_ref), custom_call_target="tpu_custom_call" | custom-call | flops 402653184 | bytes 12582912 | tf_op jit(solution)/shard_map/inner/pallas_call | solution.py:49
  29.3 0.0 collective-permute-done.mate_ref
  29.3 0.0 collective-permute-done.3.got_ref
  29.3 0.0 collective-permute-done.1.refs_2_.from_mate_ref
  29.3 0.0 collective-permute-done.2.refs_1_.from_far_ref
  29.4 1.0 dense.2
  30.4 16.2 %all_to_all.30.after_ref.parts_ref = f32[64,16,128]{2,1,0:T(8,128)S(1)} all-to-all(f32[64,16,128]{2,1,0:T(8,128)S(1)} %dense.2), channel_id=1, replica_groups=mesh['y'=4,'z'=4,'x'=4,'c'=2] {'y','z','x'}, dimensions={0} | all-to-all | bytes 1048576 | tf_op jit(solution)/shard_map/all_to_all | solution.py:389
  46.6 2.0 %head.2.refs_0_.head_ref = f32[32,2048]{1,0:T(8,128)S(1)} custom-call(s32[2]{0:T(128)S(1)} %pad_add_fusion.place_ref, s32[8]{0:T(128)S(1)} %copy-done.9, f32[32,2048]{1,0:T(8,128)S(1)} %get-tuple-element.25.edge_ref, f32[64,1024]{1,0:T(8,128)S(1)} %get-tuple-element.20.after_ref.mate_ref, f32[64,1024]{1,0:T(8,128)S(1)} %get-tuple-element.21.after_too_ref.far_ref, ...), custom_call_target="tpu_custom_call" | custom-call | flops 805306368 | bytes 1048576 | tf_op jit(solution)/shard_map/head/pallas_call | solution.py:49
  48.6 0.0 copy-done.2
  48.6 2.9 %share.1 = (bf16[384,2048]{1,0:T(8,128)(2,1)S(1)}, s32[1,128]{1,0:T(1,128)S(1)}) custom-call(s32[2]{0:T(128)S(1)} %pad_add_fusion.place_ref, s32[8]{0:T(128)S(1)} %copy-done.9, bf16[128,2048]{1,0:T(8,128)(2,1)S(1)} %get-tuple-element.19.own_ref, f32[64,1024]{1,0:T(8,128)S(1)} %collective-permute-done.1.refs_2_.from_mate_ref, ...), custom_call_target="tpu_custom_call" | custom-call | flops 2147483648 | bytes 1048576 | tf_op jit(solution)/shard_map/share/pallas_call | solution.py:49
  51.6 0.0 copy-start
  51.6 0.1 sum.2
  51.7 18.3 %all_to_all.31.rhs_ref = f32[64,16,128]{2,1,0:T(8,128)S(1)} all-to-all(f32[64,16,128]{2,1,0:T(8,128)S(1)} %sum.2), channel_id=1, replica_groups=mesh['y'=4,'z'=4,'x'=4,'c'=2] {'y','z','x'}, dimensions={0} | all-to-all | bytes 1048576 | tf_op jit(solution)/shard_map/all_to_all | solution.py:389
  70.0 0.0 collective-permute-done.4.other_ref
  70.0 1.4 solve.2
  71.4 19.1 %all_to_all.32.mine_ref = f32[64,16,128]{2,1,0:T(8,128)S(1)} all-to-all(f32[64,16,128]{2,1,0:T(8,128)S(1)} %solve.2), channel_id=1, replica_groups=mesh['y'=4,'z'=4,'x'=4,'c'=2] {'y','z','x'}, dimensions={0} | all-to-all | bytes 1048576 | tf_op jit(solution)/shard_map/all_to_all | solution.py:389
  90.5 0.0 collective-permute-start.5
  90.5 1.9 %collective-permute-done.5.other_ref = f32[64,16,128]{2,1,0:T(8,128)S(1)} collective-permute-done((f32[64,16,128]{2,1,0:T(8,128)S(1)}, f32[64,16,128]{2,1,0:T(8,128)S(1)}, u32[]{:S(2)}, u32[]{:S(2)}) %collective-permute-start.5) | collective-permute-done | bytes 524320 | tf_op jit(solution)/shard_map/ppermute | solution.py:376
  92.4 3.6 %correct.2 = (f32[8,32,1024]{2,1,0:T(8,128)}, bf16[8,32,1024]{2,1,0:T(8,128)(2,1)S(1)}, f32[16,128]{1,0:T(8,128)S(1)}, f32[16,128]{1,0:T(8,128)S(1)}) custom-call(s32[1]{0:T(128)} %bitcast.core_ref, s32[1,128]{1,0:T(1,128)S(1)} %reshape.7.refs_1_.own_ref, s32[1,128]{1,0:T(1,128)S(1)} %collective-permute-done.mate_ref, ...), custom_call_target="tpu_custom_call" | custom-call | flops 1000000 | bytes 1048576 | tf_op jit(solution)/shard_map/correct/pallas_call | solution.py:49
  96.1 5.5 %edge.3 = (f32[32,2048]{1,0:T(8,128)S(1)}, f32[32,1024]{1,0:T(8,128)S(1)}, f32[32,1024]{1,0:T(8,128)S(1)}) custom-call(s32[2]{0:T(128)S(1)} %pad_add_fusion.place_ref, s32[8]{0:T(128)S(1)} %copy-done.10, bf16[8,32,1024]{2,1,0:T(8,128)(2,1)S(1)} %get-tuple-element.30.scaled_ref, s32[8,1024]{1,0:T(8,128)S(1)} %copy-done.5, s32[8,256]{1,0:T(8,128)S(1)} %copy-done.7, ...), custom_call_target="tpu_custom_call" | custom-call | flops 805306368 | bytes 4194304 | tf_op jit(solution)/shard_map/edge/pallas_call | solution.py:49
  101.6 0.2 collective-permute-start.8
  101.8 1.4 collective-permute-start.7
  103.2 5.1 %inner.3.refs_0_.inner_hbm = f32[8,32,768]{2,1,0:T(8,128)S(1)} custom-call(bf16[8,32,1024]{2,1,0:T(8,128)(2,1)S(1)} %get-tuple-element.30.scaled_ref, bf16[8,1024,1024]{2,1,0:T(8,128)(2,1)} %inverse_ref.7, f32[32,1024]{1,0:T(8,128)S(1)} %get-tuple-element.31.after_ref.mate_ref, f32[32,1024]{1,0:T(8,128)S(1)} %get-tuple-element.32.after_too_ref.far_ref), custom_call_target="tpu_custom_call" | custom-call | flops 402653184 | bytes 12582912 | tf_op jit(solution)/shard_map/inner/pallas_call | solution.py:49
  108.3 0.0 collective-permute-done.6.got_ref
  108.3 3.3 %collective-permute-done.7.refs_1_.from_far_ref = f32[32,1024]{1,0:T(8,128)S(1)} collective-permute-done((f32[32,1024]{1,0:T(8,128)S(1)}, f32[32,1024]{1,0:T(8,128)S(1)}, u32[]{:S(2)}, u32[]{:S(2)}) %collective-permute-start.7) | collective-permute-done | bytes 131104 | tf_op jit(solution)/shard_map/ppermute | solution.py:385
  111.6 1.0 dense.3
  112.7 18.6 %all_to_all.33.after_ref.parts_ref = f32[64,16,128]{2,1,0:T(8,128)S(1)} all-to-all(f32[64,16,128]{2,1,0:T(8,128)S(1)} %dense.3), channel_id=1, replica_groups=mesh['y'=4,'z'=4,'x'=4,'c'=2] {'y','z','x'}, dimensions={0} | all-to-all | bytes 1048576 | tf_op jit(solution)/shard_map/all_to_all | solution.py:389
  131.3 2.0 %head.3.refs_0_.head_ref = f32[32,2048]{1,0:T(8,128)S(1)} custom-call(s32[2]{0:T(128)S(1)} %pad_add_fusion.place_ref, s32[8]{0:T(128)S(1)} %copy-done.10, f32[32,2048]{1,0:T(8,128)S(1)} %get-tuple-element.33.edge_ref, f32[32,1024]{1,0:T(8,128)S(1)} %get-tuple-element.31.after_ref.mate_ref, f32[32,1024]{1,0:T(8,128)S(1)} %get-tuple-element.32.after_too_ref.far_ref, ...), custom_call_target="tpu_custom_call" | custom-call | flops 805306368 | bytes 1048576 | tf_op jit(solution)/shard_map/head/pallas_call | solution.py:49
  133.3 0.1 sum.3
  133.4 16.6 %all_to_all.34.rhs_ref = f32[64,16,128]{2,1,0:T(8,128)S(1)} all-to-all(f32[64,16,128]{2,1,0:T(8,128)S(1)} %sum.3), channel_id=1, replica_groups=mesh['y'=4,'z'=4,'x'=4,'c'=2] {'y','z','x'}, dimensions={0} | all-to-all | bytes 1048576 | tf_op jit(solution)/shard_map/all_to_all | solution.py:389
  150.0 1.4 solve.3
  151.4 16.5 %all_to_all.35.mine_ref = f32[64,16,128]{2,1,0:T(8,128)S(1)} all-to-all(f32[64,16,128]{2,1,0:T(8,128)S(1)} %solve.3), channel_id=1, replica_groups=mesh['y'=4,'z'=4,'x'=4,'c'=2] {'y','z','x'}, dimensions={0} | all-to-all | bytes 1048576 | tf_op jit(solution)/shard_map/all_to_all | solution.py:389
  167.9 1.9 %collective-permute-done.9.other_ref = f32[64,16,128]{2,1,0:T(8,128)S(1)} collective-permute-done((f32[64,16,128]{2,1,0:T(8,128)S(1)}, f32[64,16,128]{2,1,0:T(8,128)S(1)}, u32[]{:S(2)}, u32[]{:S(2)}) %collective-permute-start.9) | collective-permute-done | bytes 524320 | tf_op jit(solution)/shard_map/ppermute | solution.py:376
  169.8 3.4 %correct.3 = f32[8,32,1024]{2,1,0:T(8,128)} custom-call(s32[1]{0:T(128)} %bitcast.core_ref, s32[1,128]{1,0:T(1,128)S(1)} %reshape.7.refs_1_.own_ref, s32[1,128]{1,0:T(1,128)S(1)} %collective-permute-done.mate_ref, s32[1,128]{1,0:T(1,128)S(1)} %get-tuple-element.24.far_ref, f32[64,16,128]{2,1,0:T(8,128)S(1)} %all_to_all.35.mine_ref, ...), custom_call_target="tpu_custom_call" | custom-call | flops 1000000 | bytes 1048576 | tf_op jit(solution)/shard_map/correct/pallas_call | solution.py:49
  (20 shorter events, 0.0 us)
Async XLA Ops:
  0.6 69.4 %collective-permute-start.4 = (f32[64,8192]{1,0:T(8,128)}, f32[64,8192]{1,0:T(8,128)S(1)}, u32[]{:S(2)}, u32[]{:S(2)}) collective-permute-start(f32[64,8192]{1,0:T(8,128)} %mine_ref.3), channel_id=1, source_target_pairs={{0,1},{1,0},{2,3},{3,2},{4,5},{5,4},{6,7},{7,6},{8,9},{9,8},{10,11... | collective-permute-start | bytes 6291464 | tf_op jit(solution)/shard_map/ppermute | solution.py:376
  4.1 0.9 copy-start.1
  5.0 1.0 copy-start.3
  6.1 0.8 copy-start.5
  6.8 0.7 copy-start.6
  7.5 0.7 copy-start.9
  8.2 15.5 %copy-start.11 = (f32[16,128]{1,0:T(8,128)S(1)}, f32[16,128]{1,0:T(8,128)}, u32[]{:S(2)}) copy-start(f32[16,128]{1,0:T(8,128)} %get-tuple-element.23) | copy-start | bytes 24580
  8.2 16.0 %copy-start.4 = (bf16[8,32,1024]{2,1,0:T(8,128)(2,1)S(1)}, bf16[8,32,1024]{2,1,0:T(8,128)(2,1)}, u32[]{:S(2)}) copy-start(bf16[8,32,1024]{2,1,0:T(8,128)(2,1)} %get-tuple-element.18.scaled_ref) | copy-start | bytes 1572868
  14.6 14.7 %collective-permute-start.1 = (f32[64,1024]{1,0:T(8,128)S(1)}, f32[64,1024]{1,0:T(8,128)S(1)}, u32[]{:S(2)}, u32[]{:S(2)}) collective-permute-start(f32[64,1024]{1,0:T(8,128)S(1)} %get-tuple-element.20.after_ref.mate_ref), channel_id=1, source_target_pairs={{0,1},{1,0},{2,3},{3,2},{4,5},{5,4},{6,7},{7,6},{8,9},{9,8},{10,11... | collective-permute-start | bytes 786440 | tf_op jit(solution)/shard_map/ppermute | solution.py:376
  15.2 14.1 %collective-permute-start.2 = (f32[64,1024]{1,0:T(8,128)S(1)}, f32[64,1024]{1,0:T(8,128)S(1)}, u32[]{:S(2)}, u32[]{:S(2)}) collective-permute-start(f32[64,1024]{1,0:T(8,128)S(1)} %get-tuple-element.21.after_too_ref.far_ref), channel_id=1, source_target_pairs={{1,2},{2,1},{3,4},{4,3},{5,6},{6,5},{7,8},{8,7},{9,10},{10,9},{11,... | collective-permute-start | bytes 786440 | tf_op jit(solution)/shard_map/ppermute | solution.py:385
  23.7 5.7 %collective-permute-start = (s32[1,128]{1,0:T(1,128)S(1)}, s32[1,128]{1,0:T(1,128)S(1)}, u32[]{:S(2)}, u32[]{:S(2)}) collective-permute-start(s32[1,128]{1,0:T(1,128)S(1)} %reshape.7.refs_1_.own_ref), channel_id=1, source_target_pairs={{0,1},{1,0},{2,3},{3,2},{4,5},{5,4},{6,7},{7,6},{8,9},{9,8},{10,11... | collective-permute-start | bytes 1544 | tf_op jit(solution)/shard_map/ppermute | solution.py:376
  23.7 5.7 %copy-start.8 = (f32[16,128]{1,0:T(8,128)S(1)}, f32[16,128]{1,0:T(8,128)}, u32[]{:S(2)}) copy-start(f32[16,128]{1,0:T(8,128)} %get-tuple-element.22.keep_ref) | copy-start | bytes 24580
  23.7 5.7 %collective-permute-start.3 = (f32[16,128]{1,0:T(8,128)S(1)}, f32[16,128]{1,0:T(8,128)S(1)}, u32[]{:S(2)}, u32[]{:S(2)}) collective-permute-start(f32[16,128]{1,0:T(8,128)S(1)} %copy-done.11), channel_id=1, source_target_pairs={{0,1},{1,0},{2,3},{3,2},{4,5},{5,4},{6,7},{7,6},{8,9},{9,8},{10,11... | collective-permute-start | bytes 24584 | tf_op jit(solution)/shard_map/ppermute | solution.py:376
  30.4 18.2 %copy-start.2 = (bf16[8,16,1024]{2,1,0:T(8,128)(2,1)S(1)}, bf16[8,16,1024]{2,1,0:T(8,128)(2,1)}, u32[]{:S(2)}) copy-start(bf16[8,16,1024]{2,1,0:T(8,128)(2,1)} %basis_ref.7) | copy-start | bytes 786436
  51.6 18.4 %copy-start = (f32[64,8192]{1,0:T(8,128)S(1)}, f32[64,8192]{1,0:T(8,128)}, u32[]{:S(2)}) copy-start(f32[64,8192]{1,0:T(8,128)} %mine_ref.3) | copy-start | bytes 6291460
  90.5 5.5 %copy-start.7 = (s32[8,256]{1,0:T(8,128)S(1)}, s32[8,256]{1,0:T(8,128)}, u32[]{:S(2)}) copy-start(s32[8,256]{1,0:T(8,128)} %dof_ref.9) | copy-start | bytes 24580
  90.5 5.5 %copy-start.10 = (s32[8]{0:T(128)S(1)}, s32[8]{0:T(128)}, u32[]{:S(2)}) copy-start(s32[8]{0:T(128)} %len_ref.9) | copy-start | bytes 100
  90.5 1.9 %collective-permute-start.5 = (f32[64,16,128]{2,1,0:T(8,128)S(1)}, f32[64,16,128]{2,1,0:T(8,128)S(1)}, u32[]{:S(2)}, u32[]{:S(2)}) collective-permute-start(f32[64,16,128]{2,1,0:T(8,128)S(1)} %all_to_all.32.mine_ref), channel_id=1, source_target_pairs={{0,1},{1,0},{2,3},{3,2},{4,5},{5,4},{6,7},{7,6},{8,9},{9,8},{10,11... | collective-permute-start | bytes 1572872 | tf_op jit(solution)/shard_map/ppermute | solution.py:376
  101.6 6.7 %collective-permute-start.8 = (f32[32,1024]{1,0:T(8,128)S(1)}, f32[32,1024]{1,0:T(8,128)S(1)}, u32[]{:S(2)}, u32[]{:S(2)}) collective-permute-start(f32[32,1024]{1,0:T(8,128)S(1)} %get-tuple-element.31.after_ref.mate_ref), channel_id=1, source_target_pairs={{0,1},{1,0},{2,3},{3,2},{4,5},{5,4},{6,7},{7,6},{8,9},{9,8},{10,11... | collective-permute-start | bytes 393224 | tf_op jit(solution)/shard_map/ppermute | solution.py:376
  101.8 9.8 %collective-permute-start.7 = (f32[32,1024]{1,0:T(8,128)S(1)}, f32[32,1024]{1,0:T(8,128)S(1)}, u32[]{:S(2)}, u32[]{:S(2)}) collective-permute-start(f32[32,1024]{1,0:T(8,128)S(1)} %get-tuple-element.32.after_too_ref.far_ref), channel_id=1, source_target_pairs={{1,2},{2,1},{3,4},{4,3},{5,6},{6,5},{7,8},{8,7},{9,10},{10,9},{11,... | collective-permute-start | bytes 393224 | tf_op jit(solution)/shard_map/ppermute | solution.py:385
  103.2 5.1 %collective-permute-start.6 = (f32[16,128]{1,0:T(8,128)S(1)}, f32[16,128]{1,0:T(8,128)S(1)}, u32[]{:S(2)}, u32[]{:S(2)}) collective-permute-start(f32[16,128]{1,0:T(8,128)S(1)} %get-tuple-element.29), channel_id=1, source_target_pairs={{0,1},{1,0},{2,3},{3,2},{4,5},{5,4},{6,7},{7,6},{8,9},{9,8},{10,11... | collective-permute-start | bytes 24584 | tf_op jit(solution)/shard_map/ppermute | solution.py:376
  167.9 1.9 %collective-permute-start.9 = (f32[64,16,128]{2,1,0:T(8,128)S(1)}, f32[64,16,128]{2,1,0:T(8,128)S(1)}, u32[]{:S(2)}, u32[]{:S(2)}) collective-permute-start(f32[64,16,128]{2,1,0:T(8,128)S(1)} %all_to_all.35.mine_ref), channel_id=1, source_target_pairs={{0,1},{1,0},{2,3},{3,2},{4,5},{5,4},{6,7},{7,6},{8,9},{9,8},{10,11... | collective-permute-start | bytes 1572872 | tf_op jit(solution)/shard_map/ppermute | solution.py:376

commit v3 on v2

v3 whole, which is shorter than its diff:
```python
import jax
import jax.numpy as jnp
from jax import lax
from jax.experimental import pallas as pl
from jax.experimental.pallas import tpu as pltpu
from jax.sharding import Mesh
from jax.sharding import PartitionSpec as P

CHIPS = ("y", "z", "x")
DOM = ("y", "z", "x", "c")
MIB = 2**20
VMEM = pl.BlockSpec(memory_space=pltpu.VMEM)
SMEM = pl.BlockSpec(memory_space=pltpu.SMEM)
ANY = pl.BlockSpec(memory_space=pl.ANY)
HBM = pl.BlockSpec(memory_space=pltpu.HBM)
BY_ROW = (((1,), (1,)), ((), ()))


def halves(value):
    high = value.astype(jnp.bfloat16)
    low = (value - high.astype(jnp.float32)).astype(jnp.bfloat16)
    return jnp.concatenate([high, low], axis=0)


def thirds(value):
    high = value.astype(jnp.bfloat16)
    rest = value - high.astype(jnp.float32)
    middle = rest.astype(jnp.bfloat16)
    low = (rest - middle.astype(jnp.float32)).astype(jnp.bfloat16)
    return jnp.concatenate([high, middle, low], axis=0)


def folded(out, rows):
    total = out[:rows]
    for start in range(rows, out.shape[0], rows):
        total = total + out[start : start + rows]
    return total


def mul(left, right):
    return jnp.dot(left, right, preferred_element_type=jnp.float32)


def mul_rows(left, right):
    return lax.dot_general(left, right, BY_ROW, preferred_element_type=jnp.float32)


def call(kernel, name, out_shape, args, specs, flops=1e6, moved=MIB, mib=16, **more):
    return pl.pallas_call(
        kernel,
        out_shape=out_shape,
        in_specs=specs,
        compiler_params=pltpu.CompilerParams(vmem_limit_bytes=mib * MIB),
        cost_estimate=pl.CostEstimate(
            flops=int(flops), bytes_accessed=int(moved), transcendentals=0
        ),
        name=name,
        **more,
    )(*args)


def f32(*shape):
    return jax.ShapeDtypeStruct(shape, jnp.float32)


def bf16(*shape):
    return jax.ShapeDtypeStruct(shape, jnp.bfloat16)


def weights_of(multiplicity):
    return 1.0 / multiplicity.astype(jnp.float32)


def part_out(place_ref, scaled_ref, basis_ref, keep_ref, send_ref):
    parts = mul_rows(scaled_ref[0], basis_ref[0])
    for sub in range(1, basis_ref.shape[0]):
        parts = parts + mul_rows(scaled_ref[sub], basis_ref[sub])
    half = keep_ref.shape[0]
    first = place_ref[1] == 0
    keep_ref[...] = jnp.where(first, parts[:half], parts[half:])
    send_ref[...] = jnp.where(first, parts[half:], parts[:half])


def widen(basis_ref, wide_ref):
    subs, coarse, _ = basis_ref.shape
    for sub in range(subs):
        wide_ref[sub] = jnp.zeros_like(wide_ref[sub])
        wide_ref[sub, sub * coarse : (sub + 1) * coarse] = basis_ref[sub]


def flat_map(map_ref):
    subs, coarse = map_ref.shape
    entries = subs * coarse
    value = map_ref[...]
    digits = jnp.concatenate([lax.div(value, 128), lax.rem(value, 128)], axis=0)
    lane = lax.broadcasted_iota(jnp.int32, (coarse, entries), 1)
    row = lax.broadcasted_iota(jnp.int32, (coarse, entries), 0)
    spread = jnp.where(lax.rem(lane, coarse) == row, 1.0, 0.0).astype(jnp.bfloat16)
    digits = mul(digits.astype(jnp.float32).astype(jnp.bfloat16), spread)
    value = digits[:subs] * 128.0 + digits[subs:]
    lane = lax.broadcasted_iota(jnp.int32, (subs, entries), 1)
    row = lax.broadcasted_iota(jnp.int32, (subs, entries), 0)
    own = jnp.where(lax.div(lane, coarse) == row, value, 0.0)
    return jnp.sum(own, axis=0, keepdims=True)


def hot_pair(maps, pair):
    rows = lax.broadcasted_iota(jnp.int32, (256, maps.shape[1]), 0) + 256 * pair
    return jnp.where(rows.astype(jnp.float32) == maps, 1.0, 0.0).astype(jnp.bfloat16)


def columns_of(rows):
    if rows.shape[0] == 1:
        rows = jnp.broadcast_to(rows, (8, rows.shape[1]))
    return rows.astype(jnp.float32).T


def dense_kernel(own_ref, mate_ref, keep_ref, got_ref, *refs):
    out_ref = refs[-1]
    cases, width = keep_ref.shape
    value = halves(jnp.concatenate([keep_ref[...], got_ref[...]], axis=1))
    maps = jnp.concatenate([flat_map(own_ref), flat_map(mate_ref)], axis=1)
    maps = columns_of(maps)[:, :1]
    wide = 2 * out_ref.shape[2]
    for pair in range(out_ref.shape[0] // 2):
        numbers = lax.broadcasted_iota(jnp.int32, (maps.shape[0], wide), 1) + wide * pair
        hot = jnp.where(numbers.astype(jnp.float32) == maps, 1.0, 0.0).astype(jnp.bfloat16)
        part = folded(mul(value, hot), cases)
        out_ref[2 * pair] = part[:, : wide // 2]
        out_ref[2 * pair + 1] = part[:, wide // 2 :]


def sum_kernel(parts_ref, *refs):
    out_ref = refs[-1]
    total = parts_ref[0]
    for chip in range(1, parts_ref.shape[0]):
        total = total + parts_ref[chip]
    for chip in range(out_ref.shape[0]):
        out_ref[chip] = total


def solve_kernel(core_ref, rhs_ref, mine_ref, other_ref, out_ref):
    cases, width = rhs_ref.shape[1:]
    total = jnp.zeros((2 * cases, 4 * mine_ref.shape[0]), jnp.float32)
    for pair in range(rhs_ref.shape[0] // 2):
        value = jnp.concatenate([rhs_ref[2 * pair], rhs_ref[2 * pair + 1]], axis=1)
        columns = slice(2 * pair * width, 2 * (pair + 1) * width)
        rows = jnp.concatenate([mine_ref[:, columns], other_ref[:, columns]], axis=0)
        total = total + mul_rows(halves(value), halves(rows))
    total = folded(total, cases)
    own = total[:, :width] + total[:, width:]
    half = width // 2
    turned = jnp.concatenate([own[:, half:], own[:, :half]], axis=1)
    own = jnp.where(core_ref[0] == 0, own, turned)
    for chip in range(out_ref.shape[0]):
        out_ref[chip] = own


def live_of(len_ref, sub, width):
    return lax.broadcasted_iota(jnp.int32, (1, width), 1) < len_ref[sub]


def slot_row(place_ref, len_ref, dof_ref, sub, spots):
    owned = spots // 2
    dof = dof_ref[sub : sub + 1]
    owner = lax.div(dof, owned)
    away = (owner != place_ref[0]).astype(jnp.int32)
    far = jnp.where(place_ref[1] == 0, away, 1 - away)
    live = live_of(len_ref, sub, dof.shape[1])
    return jnp.where(live, far * owned + (dof - owner * owned), -1)


def slots_of(place_ref, len_ref, dof_ref, sub, spots):
    slot = slot_row(place_ref, len_ref, dof_ref, sub, spots)
    rows = lax.broadcasted_iota(jnp.int32, (spots, slot.shape[1]), 0)
    return jnp.where(rows == slot, 1.0, 0.0).astype(jnp.bfloat16)


def column_copies(inverse_ref, buffer_ref, sems, start):
    copies = []
    for sub in range(inverse_ref.shape[0]):
        columns = pl.ds(start, buffer_ref.shape[2])
        copies.append(
            pltpu.make_async_copy(
                inverse_ref.at[sub, :, columns], buffer_ref.at[sub], sems.at[sub]
            )
        )
    for copy in copies:
        copy.start()
    return copies


def interface(len_ref, mult_ref, sub, width):
    live = live_of(len_ref, sub, width)
    return live, jnp.where(live, weights_of(mult_ref[sub : sub + 1, :width]), 0.0)


def slot_sums(
    place_ref, len_ref, mult_ref, dof_ref, start, edge_ref, sums_ref, basis_ref, map_ref, own_ref
):
    subs, width = dof_ref.shape
    owned = sums_ref.shape[1]
    slots = [slot_row(place_ref, len_ref, dof_ref, sub, 2 * owned) for sub in range(subs)]
    slots = columns_of(jnp.concatenate(slots, axis=0))
    numbers = lax.broadcasted_iota(jnp.int32, (width, owned), 1) + start
    numbers = numbers.astype(jnp.float32)
    total = None
    for sub in range(subs):
        live, mask = interface(len_ref, mult_ref, sub, width)
        hot = jnp.where(numbers == slots[:, sub : sub + 1], 1.0, 0.0).astype(jnp.bfloat16)
        solved = edge_ref[:, sub * width : (sub + 1) * width]
        cases = solved.shape[0]
        pieces = [thirds(solved * mask)]
        if basis_ref is not None:
            coarse = basis_ref.shape[1]
            weighted = basis_ref[sub, :, :width].astype(jnp.float32) * mask
            pieces.append(weighted.astype(jnp.bfloat16))
            number = jnp.where(live, float(sub), 0.0).astype(jnp.bfloat16)
            pieces.append(jnp.broadcast_to(number, (16, width)))
        out = mul(jnp.concatenate(pieces, axis=0), hot)
        moved = folded(out[: 3 * cases], cases)
        if basis_ref is not None:
            rest = out[3 * cases : 3 * cases + coarse + 8]
            own_ref[sub * coarse : (sub + 1) * coarse, :] = rest[:coarse].astype(jnp.bfloat16)
            moved = jnp.concatenate([moved, rest], axis=0)
        total = moved if total is None else total + moved
    count = total.shape[0]
    sums_ref[:count] = total
    if basis_ref is not None:
        flat = flat_map(map_ref)
        sums_ref[count:] = jnp.zeros_like(sums_ref[count:])
        sums_ref[count : count + 1, : flat.shape[1]] = flat


def edge_far(
    copies, place_ref, len_ref, mult_ref, dof_ref, scaled_ref, columns_ref, edge_ref, far_ref, *more
):
    subs, width = dof_ref.shape
    for copy in copies:
        copy.wait()
    solved = [mul(scaled_ref[sub], columns_ref[sub]) for sub in range(subs)]
    for sub in range(subs):
        edge_ref[:, sub * width : (sub + 1) * width] = solved[sub]
    start = far_ref.shape[1]
    slot_sums(place_ref, len_ref, mult_ref, dof_ref, start, edge_ref, far_ref, *more)


def first_kernel(
    place_ref,
    len_ref,
    values_hbm,
    mult_hbm,
    dof_hbm,
    map_hbm,
    basis_hbm,
    inverse_hbm,
    scaled_ref,
    keep_ref,
    send_ref,
    edge_ref,
    far_ref,
    own_ref,
    values_ref,
    mult_ref,
    dof_ref,
    map_ref,
    basis_ref,
    wide_ref,
    columns_ref,
    small_sems,
    sems,
):
    pairs = (
        (basis_hbm, basis_ref),
        (mult_hbm, mult_ref),
        (values_hbm, values_ref),
        (dof_hbm, dof_ref),
        (map_hbm, map_ref),
    )
    small = [
        pltpu.make_async_copy(source, target, small_sems.at[place])
        for place, (source, target) in enumerate(pairs)
    ]
    for copy in small:
        copy.start()
    copies = column_copies(inverse_hbm, columns_ref, sems, 0)
    subs, coarse, _ = basis_ref.shape
    for sub in range(subs):
        wide_ref[sub] = jnp.zeros_like(wide_ref[sub])
    for copy in small:
        copy.wait()
    for sub in range(subs):
        wide_ref[sub, sub * coarse : (sub + 1) * coarse] = basis_ref[sub]
        scaled = values_ref[sub].astype(jnp.float32) * weights_of(mult_ref[sub : sub + 1])
        scaled_ref[sub] = scaled.astype(jnp.bfloat16)
    part_out(place_ref, scaled_ref, wide_ref, keep_ref, send_ref)
    edge_far(
        copies,
        place_ref,
        len_ref,
        mult_ref,
        dof_ref,
        scaled_ref,
        columns_ref,
        edge_ref,
        far_ref,
        basis_ref,
        map_ref,
        own_ref,
    )


def inner_kernel(place_ref, len_ref, scaled_ref, mult_ref, dof_ref, edge_ref, inverse_ref, *refs):
    *inputs, buffer_ref, sems = refs
    if len(inputs) == 6:
        basis_ref, map_ref, after_ref, inner_ref, mate_ref, own_ref = inputs
    else:
        (after_ref, inner_ref, mate_ref), basis_ref, map_ref, own_ref = inputs, None, None, None
    copies = column_copies(
        inverse_ref, buffer_ref, sems, inverse_ref.shape[2] - buffer_ref.shape[2]
    )
    slot_sums(
        place_ref,
        len_ref,
        mult_ref,
        dof_ref,
        0,
        edge_ref,
        mate_ref,
        basis_ref,
        map_ref,
        own_ref,
    )
    for sub in range(scaled_ref.shape[0]):
        copies[sub].wait()
        inner_ref[sub] = mul(scaled_ref[sub], buffer_ref[sub])


def head_kernel(
    place_ref,
    len_ref,
    edge_ref,
    mate_ref,
    far_ref,
    from_mate_ref,
    from_far_ref,
    dof_ref,
    after_ref,
    *refs,
):
    subs, width = dof_ref.shape
    cases = edge_ref.shape[0]
    owned = mate_ref.shape[1]
    near = thirds(mate_ref[:cases] + from_mate_ref[:cases])
    far = thirds(far_ref[:cases] + from_far_ref[:cases])
    count = near.shape[0]
    if len(refs) == 1:
        (head_ref,) = refs
    else:
        basis_ref, own_mate_ref, own_far_ref, head_ref, shared_ref, map_ref, near_ref, wide_ref = refs
        coarse = basis_ref.shape[1]
        entries = own_mate_ref.shape[0]
        for ref, sums, own, arrived in (
            (near_ref, near, own_mate_ref, from_mate_ref),
            (wide_ref, far, own_far_ref, from_far_ref),
        ):
            ref[:count] = sums
            ref[count : count + entries] = own[...]
            row = arrived[cases + coarse : cases + coarse + 1]
            basis = arrived[cases : cases + coarse]
            for sub in range(subs):
                start = count + entries + sub * coarse
                ref[start : start + coarse] = jnp.where(row == float(sub), basis, 0.0).astype(
                    jnp.bfloat16
                )
        near, far = near_ref[...], wide_ref[...]
        map_ref[...] = from_far_ref[cases + coarse + 8 : cases + coarse + 9, :entries]
    for sub in range(subs):
        columns = slice(sub * width, (sub + 1) * width)
        hot = slots_of(place_ref, len_ref, dof_ref, sub, 2 * owned)
        by_mate = mul(near, hot[:owned])
        by_far = mul(far, hot[owned:])
        live = live_of(len_ref, sub, width)
        fetched = folded(by_mate[:count] + by_far[:count], cases)
        head_ref[:, columns] = jnp.where(live, fetched, edge_ref[:, columns])
        if len(refs) > 1:
            by_mate, by_far = by_mate[count:], by_far[count:]
            own = by_mate[:entries] + by_far[:entries]
            full = jnp.concatenate([own, by_mate[entries:], by_far[entries:]], axis=0)
            shared_ref[:, columns] = full.astype(jnp.bfloat16)
            rows = slice(sub * coarse, (sub + 1) * coarse)
            dead = jnp.where(live, 0.0, basis_ref[sub, :, :width].astype(jnp.float32))
            shared_ref[rows, columns] = (own[rows] + dead).astype(jnp.bfloat16)


def correct_kernel(
    place_ref,
    own_ref,
    mate_ref,
    far_map_ref,
    mine_ref,
    other_ref,
    basis_ref,
    head_ref,
    shared_ref,
    inner_ref,
    *refs,
):
    *inputs, wide_ref, values_ref, leave_sems = refs
    if len(inputs) == 1:
        (out_hbm,) = inputs
    else:
        (
            len_ref,
            mult_ref,
            dof_ref,
            inverse_hbm,
            out_hbm,
            scaled_ref,
            keep_ref,
            send_ref,
            edge_ref,
            far_ref,
            columns_ref,
            sems,
        ) = inputs
        copies = column_copies(inverse_hbm, columns_ref, sems, 0)
    subs, cases, _ = values_ref.shape
    chips, half, _ = mine_ref.shape
    entries = far_map_ref.shape[1]
    width = head_ref.shape[1] // subs
    leave = [
        pltpu.make_async_copy(values_ref.at[sub], out_hbm.at[sub], leave_sems.at[sub])
        for sub in range(subs)
    ]
    widen(basis_ref, wide_ref)
    maps = jnp.concatenate([flat_map(own_ref), flat_map(mate_ref), far_map_ref[...]], axis=1)
    looked = jnp.zeros((4 * half, 3 * entries), jnp.float32)
    for pair in range(chips // 2):
        mine = jnp.concatenate([mine_ref[2 * pair], mine_ref[2 * pair + 1]], axis=1)
        other = jnp.concatenate([other_ref[2 * pair], other_ref[2 * pair + 1]], axis=1)
        both = halves(jnp.concatenate([mine, other], axis=0))
        looked = looked + mul(both, hot_pair(maps, pair))
    looked = folded(looked, cases)
    turned = jnp.concatenate([looked[half:], looked[:half]], axis=0)
    looked = jnp.where(place_ref[1] == 0, looked, turned)
    own = thirds(looked[:, :entries])
    looked = thirds(looked)
    for sub in range(subs):
        columns = slice(sub * width, (sub + 1) * width)
        values_ref[sub, :, :width] = head_ref[:, columns] + folded(
            mul(looked, shared_ref[:, columns]), cases
        )
        values_ref[sub, :, width:] = inner_ref[sub] + folded(
            mul(own, wide_ref[sub, :, width:]), cases
        )
        leave[sub].start()
    if len(inputs) > 1:
        for sub in range(subs):
            scaled = values_ref[sub] * weights_of(mult_ref[sub : sub + 1])
            scaled_ref[sub] = scaled.astype(jnp.bfloat16)
        part_out(place_ref, scaled_ref, wide_ref, keep_ref, send_ref)
        edge_far(
            copies,
            place_ref,
            len_ref,
            mult_ref,
            dof_ref,
            scaled_ref,
            columns_ref,
            edge_ref,
            far_ref,
            None,
            None,
            None,
        )
    for copy in leave:
        copy.wait()


def swap(value):
    return lax.ppermute(value, "c", [(0, 1), (1, 0)])


def far_swap(value):
    count = lax.axis_size(DOM)
    pairs = []
    for device in range(1, count, 2):
        after = (device + 1) % count
        pairs += [(device, after), (after, device)]
    return lax.ppermute(value, DOM, pairs)


def by_chip(value):
    return lax.all_to_all(value, CHIPS, 0, 0, tiled=True)


def local(
    residual_in,
    local_inverse,
    coarse_basis,
    coarse_inverse,
    multiplicity,
    iface_len,
    iface_dof,
    coarse_map,
):
    subs, cases, length = residual_in.shape
    coarse = coarse_basis.shape[1]
    width = iface_dof.shape[1]
    rows, order = coarse_inverse.shape
    chips = lax.axis_size(DOM) // 2
    half = cases // 2
    entries = subs * coarse
    spots = subs * width
    owned = spots // 2
    place = jnp.stack([lax.axis_index(DOM), lax.axis_index("c")]).astype(jnp.int32)
    core = place[1:]
    slot_flops = 2 * 3 * cases * spots * spots
    sent = cases + coarse + 16
    blocks = f32(chips, half, order // chips)
    inverse_bytes = 2 * local_inverse.size

    def buffers(count):
        return [
            pltpu.VMEM((subs, length, count), jnp.bfloat16),
            pltpu.SemaphoreType.DMA((subs,)),
        ]

    mate_map = swap(coarse_map)
    other_rows = swap(coarse_inverse)
    wide = pltpu.VMEM((subs, entries, length), jnp.bfloat16)
    opened = (bf16(subs, cases, length), f32(half, entries), f32(half, entries), f32(cases, spots))

    def dense(keep, got, *after):
        parts = call(
            dense_kernel,
            "dense",
            blocks,
            (coarse_map, mate_map, keep, got, *after),
            [VMEM] * 4 + [ANY] * len(after),
        )
        return by_chip(parts)

    def inner_solve(scaled, edge, far, *more):
        outs = [f32(subs, cases, length - width), f32(sent if more else cases, owned)]
        if more:
            outs.append(bf16(entries, owned))
        return call(
            inner_kernel,
            "inner",
            tuple(outs),
            (place, iface_len, scaled, multiplicity, iface_dof, edge, local_inverse, *more, far),
            [SMEM] * 2 + [VMEM] * 4 + [HBM] + [VMEM] * len(more) + [ANY],
            flops=2 * scaled.size * (length - width) + slot_flops // 2,
            moved=inverse_bytes * 3 // 4,
            mib=60 if more else 50,
            scratch_shapes=buffers(length - width),
        )

    def coarse_solve(parts, after):
        rhs = call(
            sum_kernel, "sum", blocks, (parts, *after), [VMEM] + [ANY] * len(after)
        )
        rhs = by_chip(rhs)
        own = call(
            solve_kernel,
            "solve",
            blocks,
            (core, rhs, coarse_inverse, other_rows),
            [SMEM] + [VMEM] * 3,
        )
        return by_chip(own)

    def assemble(edge, mate, far, from_mate, from_far, after, *more):
        outs, scratch = [f32(cases, spots)], []
        if more:
            outs += [bf16(3 * entries, spots), f32(1, entries)]
            scratch = [pltpu.VMEM((3 * cases + 2 * entries, owned), jnp.bfloat16)] * 2
        return call(
            head_kernel,
            "head",
            tuple(outs),
            (place, iface_len, edge, mate, far, from_mate, from_far, iface_dof, after, *more),
            [SMEM] * 2 + [VMEM] * 6 + [ANY] + [VMEM] * len(more),
            flops=slot_flops,
            scratch_shapes=scratch,
        )

    def correct(mine, head, shared, inner, *more):
        outs, out_specs, specs, scratch = [f32(subs, cases, length)], [HBM], [], []
        if more:
            outs += [*opened, f32(cases, owned)]
            out_specs += [VMEM] * 5
            specs = [SMEM, VMEM, VMEM, HBM]
            scratch = buffers(width)
        return call(
            correct_kernel,
            "correct",
            tuple(outs),
            (
                place,
                coarse_map,
                mate_map,
                far_map,
                mine,
                swap(mine),
                coarse_basis,
                head,
                shared,
                inner,
                *more,
            ),
            [SMEM] + [VMEM] * 9 + specs,
            mib=50 if more else 16,
            out_specs=tuple(out_specs),
            scratch_shapes=[
                *scratch,
                wide,
                pltpu.VMEM((subs, cases, length), jnp.float32),
                pltpu.SemaphoreType.DMA((subs,)),
            ],
        )

    scaled, keep, send, edge, far, own_far = call(
        first_kernel,
        "first",
        (*opened, f32(sent, owned), bf16(entries, owned)),
        (
            place,
            iface_len,
            residual_in,
            multiplicity,
            iface_dof,
            coarse_map,
            coarse_basis,
            local_inverse,
        ),
        [SMEM] * 2 + [HBM] * 6,
        mib=60,
        scratch_shapes=[
            pltpu.VMEM(residual_in.shape, jnp.bfloat16),
            pltpu.VMEM(multiplicity.shape, jnp.int32),
            pltpu.VMEM(iface_dof.shape, jnp.int32),
            pltpu.VMEM(coarse_map.shape, jnp.int32),
            pltpu.VMEM(coarse_basis.shape, jnp.bfloat16),
            wide,
            buffers(width)[0],
            pltpu.SemaphoreType.DMA((5,)),
            buffers(width)[1],
        ],
    )
    got, from_far = swap(send), far_swap(far)
    inner, mate, own_mate = inner_solve(scaled, edge, far, coarse_basis, coarse_map)
    from_mate = swap(mate)
    parts = dense(keep, got, from_mate, from_far)
    head, shared, far_map = assemble(
        edge, mate, far, from_mate, from_far, parts, coarse_basis, own_mate, own_far
    )
    mine = coarse_solve(parts, (head,))
    first_apply, scaled, keep, send, edge, far = correct(
        mine, head, shared, inner, iface_len, multiplicity, iface_dof, local_inverse
    )

    got, from_far = swap(send), far_swap(far)
    inner, mate = inner_solve(scaled, edge, far)
    from_mate = swap(mate)
    parts = dense(keep, got, from_mate, from_far)
    (head,) = assemble(edge, mate, far, from_mate, from_far, parts)
    mine = coarse_solve(parts, (head,))
    (second_apply,) = correct(mine, head, shared, inner)
    return first_apply, second_apply


def solution(mesh):
    grid = Mesh(mesh.devices.reshape(4, 4, 4, 2), DOM)
    placed = (
        P(DOM, None, None),
        P(DOM, None, None),
        P(DOM, None, None),
        P(DOM, None),
        P(DOM, None),
        P(DOM),
        P(DOM, None),
        P(DOM, None),
    )
    return jax.shard_map(
        local,
        mesh=grid,
        in_specs=placed,
        out_specs=(P(DOM, None, None), P(DOM, None, None)),
        check_vma=False,
    )
```

time: 175 us -> 172 us (0.983)
  local copies, waits for them, and re-layouts: 4.9 us -> 0.08 us
    unnamed x24 -> x34, local copies, waits for them, and re-layouts: 4.13 us -> 0.08 us
    ppermute x2, waiting for transfers between devices: 3.3 us -> 0.87 us  [far_swap(): return lax.ppermute(value, DOM, pairs)]
    ppermute x8, waiting for transfers between devices: 3.83 us -> 5.79 us  [swap(): return lax.ppermute(value, 'c', [(0, 1), (1, 0)])]
    pallas_call x16 -> x13, Pallas kernels: 43.8 us -> 44.1 us  [call(): pl.pallas_call(kernel, out_shape=out_shape, in_specs=specs, compiler_para...]
  transfers between devices with their start and end apart: 10 -> 10, of which waited for: 3 -> 6; matrix products, arithmetic and copies ran while one was open for 0% -> 0% of each run, Pallas kernels for 15% -> 15%
where the time goes in v3:
time: 172 us; the launch traced here: 171 us
  blocking collectives  106 us (62%)
  Pallas kernels  44.1 us (26%)
  starting transfers between devices  12 us (7%)
  waiting for transfers between devices  6.66 us (4%)
    all_to_all x6, blocking collectives, by_chip(): return lax.all_to_all(value, CHIPS, 0, 0, tiled=True)  106 us
    pallas_call x13, Pallas kernels, call(): pl.pallas_call(kernel, out_shape=out_shape, in_specs=specs, compiler_para...  44.1 us
    ppermute x2, starting transfers between devices, far_swap(): return lax.ppermute(value, DOM, pairs)  10.6 us
    ppermute x8, waiting for transfers between devices, swap(): return lax.ppermute(value, 'c', [(0, 1), (1, 0)])  5.79 us
  transfers between devices with their start and end apart: 10, of which 6 were waited for; matrix products, arithmetic and copies ran while one was open for 0% of the time, Pallas kernels for 15%

profile of v3, /device:TPU:0, one launch (start us, length us, event | category | flops | bytes accessed | tf_op | source)
XLA Modules:
  0.0 170.6 jit_solution(4870113222688756115)
XLA Ops:
  0.6 0.1 collective-permute-start.4
  0.7 0.7 pad_add_fusion.place_ref
  1.4 6.7 %first.1 = (bf16[8,32,1024]{2,1,0:T(8,128)(2,1)}, f32[16,128]{1,0:T(8,128)}, f32[16,128]{1,0:T(8,128)}, f32[32,2048]{1,0:T(8,128)}, f32[64,1024]{1,0:T(8,128)}, /*index=5*/bf16[128,1024]{1,0:T(8,128)(2,1)}) custom-call(s32[2]{0:T(128)} %pad_add_fusion.place_ref, s32[8]{0:T(128)} %len_ref.9, bf16[8,32,1024]{2,1,0:T(8,128)(2,1)} %values_hbm.1, ...), custom_call_target="tpu_custom_call" | custom-call | flops 1000000 | bytes 1048576 | tf_op jit(solution)/shard_map/first/pallas_call | solution.py:49
  8.1 8.9 %collective-permute-start.2 = (f32[64,1024]{1,0:T(8,128)}, f32[64,1024]{1,0:T(8,128)S(1)}, u32[]{:S(2)}, u32[]{:S(2)}) collective-permute-start(f32[64,1024]{1,0:T(8,128)} %get-tuple-element.24.refs_2_.far_ref), channel_id=1, source_target_pairs={{1,2},{2,1},{3,4},{4,3},{5,6},{6,5},{7,8},{8,7},{9,10},{10,9},{11,... | collective-permute-start | bytes 786440 | tf_op jit(solution)/shard_map/ppermute | solution.py:491
  17.1 7.5 %inner.2 = (f32[8,32,768]{2,1,0:T(8,128)}, f32[64,1024]{1,0:T(8,128)}, bf16[128,1024]{1,0:T(8,128)(2,1)}) custom-call(s32[2]{0:T(128)} %pad_add_fusion.place_ref, s32[8]{0:T(128)} %len_ref.9, bf16[8,32,1024]{2,1,0:T(8,128)(2,1)} %get-tuple-element.23.scaled_ref, s32[8,1024]{1,0:T(8,128)} %mult_ref.3, s32[8,256]{1,0:T(8,128)} %dof_ref.7, ...), custom_call_target="tpu_custom_call" | custom-call | flops 805306368 | bytes 12582912 | tf_op jit(solution)/shard_map/inner/pallas_call | solution.py:49
  24.6 0.0 copy-start.3
  24.6 0.0 copy-start.9
  24.6 0.0 copy-start.10
  24.6 0.0 copy-start.11
  24.7 0.1 collective-permute-start.1
  24.8 0.5 collective-permute-start.3
  25.3 0.0 copy-done.8
  25.3 0.1 collective-permute-start
  25.4 1.1 collective-permute-done.mate_ref
  26.4 0.0 collective-permute-done.3.got_ref
  26.4 0.0 collective-permute-done.2.refs_1_.from_far_ref
  26.4 0.1 collective-permute-done.1.refs_0_.from_mate_ref
  26.5 0.0 copy-done.12
  26.5 1.1 dense.2
  27.6 18.1 %all_to_all.30.after_ref.parts_ref = f32[64,16,128]{2,1,0:T(8,128)S(1)} all-to-all(f32[64,16,128]{2,1,0:T(8,128)S(1)} %dense.2), channel_id=1, replica_groups=mesh['y'=4,'z'=4,'x'=4,'c'=2] {'y','z','x'}, dimensions={0} | all-to-all | bytes 1048576 | tf_op jit(solution)/shard_map/all_to_all | solution.py:495
  45.8 0.0 copy-start
  45.9 3.7 %head.2 = (f32[32,2048]{1,0:T(8,128)S(1)}, bf16[384,2048]{1,0:T(8,128)(2,1)S(1)}, f32[1,128]{1,0:T(1,128)S(1)}) custom-call(s32[2]{0:T(128)S(1)} %copy-done.10, s32[8]{0:T(128)S(1)} %copy-done.11, f32[32,2048]{1,0:T(8,128)S(1)} %copy-done.6, f32[64,1024]{1,0:T(8,128)S(1)} %copy-done.14, f32[64,1024]{1,0:T(8,128)S(1)} %copy-done.7, ...), custom_call_target="tpu_custom_call" | custom-call | flops 805306368 | bytes 1048576 | tf_op jit(solution)/shard_map/head/pallas_call | solution.py:49
  49.6 0.0 copy-start.1
  49.6 0.1 sum.2
  49.7 17.3 %all_to_all.31.rhs_ref = f32[64,16,128]{2,1,0:T(8,128)S(1)} all-to-all(f32[64,16,128]{2,1,0:T(8,128)S(1)} %sum.2), channel_id=1, replica_groups=mesh['y'=4,'z'=4,'x'=4,'c'=2] {'y','z','x'}, dimensions={0} | all-to-all | bytes 1048576 | tf_op jit(solution)/shard_map/all_to_all | solution.py:495
  67.0 0.0 collective-permute-done.4.other_ref
  67.0 1.4 solve.2
  68.4 16.5 %all_to_all.32.mine_ref = f32[64,16,128]{2,1,0:T(8,128)S(1)} all-to-all(f32[64,16,128]{2,1,0:T(8,128)S(1)} %solve.2), channel_id=1, replica_groups=mesh['y'=4,'z'=4,'x'=4,'c'=2] {'y','z','x'}, dimensions={0} | all-to-all | bytes 1048576 | tf_op jit(solution)/shard_map/all_to_all | solution.py:495
  84.9 0.0 collective-permute-start.5
  84.9 1.9 %collective-permute-done.5.other_ref = f32[64,16,128]{2,1,0:T(8,128)S(1)} collective-permute-done((f32[64,16,128]{2,1,0:T(8,128)S(1)}, f32[64,16,128]{2,1,0:T(8,128)S(1)}, u32[]{:S(2)}, u32[]{:S(2)}) %collective-permute-start.5) | collective-permute-done | bytes 524320 | tf_op jit(solution)/shard_map/ppermute | solution.py:482
  86.8 9.0 %correct.2 = (f32[8,32,1024]{2,1,0:T(8,128)}, bf16[8,32,1024]{2,1,0:T(8,128)(2,1)S(1)}, f32[16,128]{1,0:T(8,128)S(1)}, f32[16,128]{1,0:T(8,128)S(1)}, f32[32,2048]{1,0:T(8,128)S(1)}, /*index=5*/f32[32,1024]{1,0:T(8,128)S(1)}) custom-call(s32[2]{0:T(128)S(1)} %copy-done.10, s32[8,16]{1,0:T(8,128)S(1)} %copy-done.8, ...), custom_call_target="tpu_custom_call" | custom-call | flops 1000000 | bytes 1048576 | tf_op jit(solution)/shard_map/correct/pallas_call | solution.py:49
  95.8 1.7 collective-permute-start.8
  97.5 5.9 %inner.3 = (f32[8,32,768]{2,1,0:T(8,128)S(1)}, f32[32,1024]{1,0:T(8,128)S(1)}) custom-call(s32[2]{0:T(128)S(1)} %copy-done.10, s32[8]{0:T(128)S(1)} %copy-done.11, bf16[8,32,1024]{2,1,0:T(8,128)(2,1)S(1)} %get-tuple-element.37.scaled_ref, s32[8,1024]{1,0:T(8,128)S(1)} %copy-done.5, s32[8,256]{1,0:T(8,128)S(1)} %copy-done.9, ...), custom_call_target="tpu_custom_call" | custom-call | flops 805306368 | bytes 12582912 | tf_op jit(solution)/shard_map/inner/pallas_call | solution.py:49
  103.4 0.1 collective-permute-start.7
  103.5 0.5 collective-permute-start.6
  104.0 0.8 collective-permute-done.6.got_ref
  104.8 0.9 collective-permute-done.8.refs_1_.from_far_ref
  105.7 0.0 collective-permute-done.7.refs_0_.from_mate_ref
  105.7 1.1 dense.3
  106.9 20.8 %all_to_all.33.after_ref.parts_ref = f32[64,16,128]{2,1,0:T(8,128)S(1)} all-to-all(f32[64,16,128]{2,1,0:T(8,128)S(1)} %dense.3), channel_id=1, replica_groups=mesh['y'=4,'z'=4,'x'=4,'c'=2] {'y','z','x'}, dimensions={0} | all-to-all | bytes 1048576 | tf_op jit(solution)/shard_map/all_to_all | solution.py:495
  127.7 2.1 %head.3.refs_0_.head_ref = f32[32,2048]{1,0:T(8,128)S(1)} custom-call(s32[2]{0:T(128)S(1)} %copy-done.10, s32[8]{0:T(128)S(1)} %copy-done.11, f32[32,2048]{1,0:T(8,128)S(1)} %get-tuple-element.38.edge_ref, f32[32,1024]{1,0:T(8,128)S(1)} %get-tuple-element.40.mate_ref, f32[32,1024]{1,0:T(8,128)S(1)} %get-tuple-element.39.refs_0_.far_ref, ...), custom_call_target="tpu_custom_call" | custom-call | flops 805306368 | bytes 1048576 | tf_op jit(solution)/shard_map/head/pallas_call | solution.py:49
  129.7 0.1 sum.3
  129.8 16.8 %all_to_all.34.rhs_ref = f32[64,16,128]{2,1,0:T(8,128)S(1)} all-to-all(f32[64,16,128]{2,1,0:T(8,128)S(1)} %sum.3), channel_id=1, replica_groups=mesh['y'=4,'z'=4,'x'=4,'c'=2] {'y','z','x'}, dimensions={0} | all-to-all | bytes 1048576 | tf_op jit(solution)/shard_map/all_to_all | solution.py:495
  146.6 1.4 solve.3
  148.0 16.5 %all_to_all.35.mine_ref = f32[64,16,128]{2,1,0:T(8,128)S(1)} all-to-all(f32[64,16,128]{2,1,0:T(8,128)S(1)} %solve.3), channel_id=1, replica_groups=mesh['y'=4,'z'=4,'x'=4,'c'=2] {'y','z','x'}, dimensions={0} | all-to-all | bytes 1048576 | tf_op jit(solution)/shard_map/all_to_all | solution.py:495
  164.5 0.0 collective-permute-start.9
  164.6 1.9 %collective-permute-done.9.other_ref = f32[64,16,128]{2,1,0:T(8,128)S(1)} collective-permute-done((f32[64,16,128]{2,1,0:T(8,128)S(1)}, f32[64,16,128]{2,1,0:T(8,128)S(1)}, u32[]{:S(2)}, u32[]{:S(2)}) %collective-permute-start.9) | collective-permute-done | bytes 524320 | tf_op jit(solution)/shard_map/ppermute | solution.py:482
  166.5 3.9 %correct.3 = f32[8,32,1024]{2,1,0:T(8,128)} custom-call(s32[2]{0:T(128)S(1)} %copy-done.10, s32[8,16]{1,0:T(8,128)S(1)} %copy-done.8, s32[8,16]{1,0:T(8,128)S(1)} %collective-permute-done.mate_ref, f32[1,128]{1,0:T(1,128)S(1)} %get-tuple-element.30.far_map_ref, f32[64,16,128]{2,1,0:T(8,128)S(1)} %all_to_all.35.mine_ref, ...), custom_call_target="tpu_custom_call" | custom-call | flops 1000000 | bytes 1048576 | tf_op jit(solution)/shard_map/correct/pallas_call | solution.py:49
  (26 shorter events, 0.1 us)
Async XLA Ops:
  0.6 66.3 %collective-permute-start.4 = (f32[64,8192]{1,0:T(8,128)}, f32[64,8192]{1,0:T(8,128)S(1)}, u32[]{:S(2)}, u32[]{:S(2)}) collective-permute-start(f32[64,8192]{1,0:T(8,128)} %mine_ref.3), channel_id=1, source_target_pairs={{0,1},{1,0},{2,3},{3,2},{4,5},{5,4},{6,7},{7,6},{8,9},{9,8},{10,11... | collective-permute-start | bytes 6291464 | tf_op jit(solution)/shard_map/ppermute | solution.py:482
  8.1 18.3 %collective-permute-start.2 = (f32[64,1024]{1,0:T(8,128)}, f32[64,1024]{1,0:T(8,128)S(1)}, u32[]{:S(2)}, u32[]{:S(2)}) collective-permute-start(f32[64,1024]{1,0:T(8,128)} %get-tuple-element.24.refs_2_.far_ref), channel_id=1, source_target_pairs={{1,2},{2,1},{3,4},{4,3},{5,6},{6,5},{7,8},{8,7},{9,10},{10,9},{11,... | collective-permute-start | bytes 786440 | tf_op jit(solution)/shard_map/ppermute | solution.py:491
  17.1 7.7 %copy-start.16 = (f32[16,128]{1,0:T(8,128)S(1)}, f32[16,128]{1,0:T(8,128)}, u32[]{:S(2)}) copy-start(f32[16,128]{1,0:T(8,128)} %get-tuple-element.27) | copy-start | bytes 24580
  17.1 8.2 %copy-start.8 = (s32[8,16]{1,0:T(8,128)S(1)}, s32[8,16]{1,0:T(8,128)}, u32[]{:S(2)}) copy-start(s32[8,16]{1,0:T(8,128)} %own_ref.7) | copy-start | bytes 1540
  17.1 9.4 %copy-start.12 = (f32[16,128]{1,0:T(8,128)S(1)}, f32[16,128]{1,0:T(8,128)}, u32[]{:S(2)}) copy-start(f32[16,128]{1,0:T(8,128)} %get-tuple-element.26.keep_ref) | copy-start | bytes 24580
  24.6 21.2 %copy-start.3 = (bf16[8,16,1024]{2,1,0:T(8,128)(2,1)S(1)}, bf16[8,16,1024]{2,1,0:T(8,128)(2,1)}, u32[]{:S(2)}) copy-start(bf16[8,16,1024]{2,1,0:T(8,128)(2,1)} %basis_ref.3) | copy-start | bytes 786436
  24.6 21.2 %copy-start.6 = (f32[32,2048]{1,0:T(8,128)S(1)}, f32[32,2048]{1,0:T(8,128)}, u32[]{:S(2)}) copy-start(f32[32,2048]{1,0:T(8,128)} %get-tuple-element.22.edge_ref) | copy-start | bytes 786436
  24.6 21.2 %copy-start.7 = (f32[64,1024]{1,0:T(8,128)S(1)}, f32[64,1024]{1,0:T(8,128)}, u32[]{:S(2)}) copy-start(f32[64,1024]{1,0:T(8,128)} %get-tuple-element.24.refs_2_.far_ref) | copy-start | bytes 786436
  24.6 21.2 %copy-start.9 = (s32[8,256]{1,0:T(8,128)S(1)}, s32[8,256]{1,0:T(8,128)}, u32[]{:S(2)}) copy-start(s32[8,256]{1,0:T(8,128)} %dof_ref.7) | copy-start | bytes 24580
  24.6 21.2 %copy-start.10 = (s32[2]{0:T(128)S(1)}, s32[2]{0:T(128)}, u32[]{:S(2)}) copy-start(s32[2]{0:T(128)} %pad_add_fusion.place_ref) | copy-start | bytes 28
  24.6 21.2 %copy-start.11 = (s32[8]{0:T(128)S(1)}, s32[8]{0:T(128)}, u32[]{:S(2)}) copy-start(s32[8]{0:T(128)} %len_ref.9) | copy-start | bytes 100
  24.6 21.2 %copy-start.13 = (bf16[128,1024]{1,0:T(8,128)(2,1)S(1)}, bf16[128,1024]{1,0:T(8,128)(2,1)}, u32[]{:S(2)}) copy-start(bf16[128,1024]{1,0:T(8,128)(2,1)} %get-tuple-element.29.refs_2_) | copy-start | bytes 786436
  24.6 21.2 %copy-start.14 = (f32[64,1024]{1,0:T(8,128)S(1)}, f32[64,1024]{1,0:T(8,128)}, u32[]{:S(2)}) copy-start(f32[64,1024]{1,0:T(8,128)} %get-tuple-element.25.mate_ref) | copy-start | bytes 786436
  24.7 21.2 %copy-start.15 = (bf16[128,1024]{1,0:T(8,128)(2,1)S(1)}, bf16[128,1024]{1,0:T(8,128)(2,1)}, u32[]{:S(2)}) copy-start(bf16[128,1024]{1,0:T(8,128)(2,1)} %get-tuple-element.28.refs_1_) | copy-start | bytes 786436
  24.7 1.8 %collective-permute-start.1 = (f32[64,1024]{1,0:T(8,128)}, f32[64,1024]{1,0:T(8,128)S(1)}, u32[]{:S(2)}, u32[]{:S(2)}) collective-permute-start(f32[64,1024]{1,0:T(8,128)} %get-tuple-element.25.mate_ref), channel_id=1, source_target_pairs={{0,1},{1,0},{2,3},{3,2},{4,5},{5,4},{6,7},{7,6},{8,9},{9,8},{10,11... | collective-permute-start | bytes 786440 | tf_op jit(solution)/shard_map/ppermute | solution.py:482
  24.8 1.7 collective-permute-start.3
  25.3 1.2 collective-permute-start
  45.8 21.1 %copy-start = (f32[64,8192]{1,0:T(8,128)S(1)}, f32[64,8192]{1,0:T(8,128)}, u32[]{:S(2)}) copy-start(f32[64,8192]{1,0:T(8,128)} %mine_ref.3) | copy-start | bytes 6291460
  49.6 18.8 %copy-start.1 = (bf16[384,2048]{1,0:T(8,128)(2,1)}, bf16[384,2048]{1,0:T(8,128)(2,1)S(1)}, u32[]{:S(2)}) copy-start(bf16[384,2048]{1,0:T(8,128)(2,1)S(1)} %get-tuple-element.32.shared_ref) | copy-start | bytes 4718596
  67.0 19.9 %copy-start.4 = (f32[8,32,768]{2,1,0:T(8,128)S(1)}, f32[8,32,768]{2,1,0:T(8,128)}, u32[]{:S(2)}) copy-start(f32[8,32,768]{2,1,0:T(8,128)} %get-tuple-element.33.inner_ref) | copy-start | bytes 2359300
  67.0 19.9 %copy-start.5 = (s32[8,1024]{1,0:T(8,128)S(1)}, s32[8,1024]{1,0:T(8,128)}, u32[]{:S(2)}) copy-start(s32[8,1024]{1,0:T(8,128)} %mult_ref.3) | copy-start | bytes 98308
  84.9 1.9 %collective-permute-start.5 = (f32[64,16,128]{2,1,0:T(8,128)S(1)}, f32[64,16,128]{2,1,0:T(8,128)S(1)}, u32[]{:S(2)}, u32[]{:S(2)}) collective-permute-start(f32[64,16,128]{2,1,0:T(8,128)S(1)} %all_to_all.32.mine_ref), channel_id=1, source_target_pairs={{0,1},{1,0},{2,3},{3,2},{4,5},{5,4},{6,7},{7,6},{8,9},{9,8},{10,11... | collective-permute-start | bytes 1572872 | tf_op jit(solution)/shard_map/ppermute | solution.py:482
  95.8 9.9 %collective-permute-start.8 = (f32[32,1024]{1,0:T(8,128)S(1)}, f32[32,1024]{1,0:T(8,128)S(1)}, u32[]{:S(2)}, u32[]{:S(2)}) collective-permute-start(f32[32,1024]{1,0:T(8,128)S(1)} %get-tuple-element.39.refs_0_.far_ref), channel_id=1, source_target_pairs={{1,2},{2,1},{3,4},{4,3},{5,6},{6,5},{7,8},{8,7},{9,10},{10,9},{11,... | collective-permute-start | bytes 393224 | tf_op jit(solution)/shard_map/ppermute | solution.py:491
  103.4 2.3 %collective-permute-start.7 = (f32[32,1024]{1,0:T(8,128)S(1)}, f32[32,1024]{1,0:T(8,128)S(1)}, u32[]{:S(2)}, u32[]{:S(2)}) collective-permute-start(f32[32,1024]{1,0:T(8,128)S(1)} %get-tuple-element.40.mate_ref), channel_id=1, source_target_pairs={{0,1},{1,0},{2,3},{3,2},{4,5},{5,4},{6,7},{7,6},{8,9},{9,8},{10,11... | collective-permute-start | bytes 393224 | tf_op jit(solution)/shard_map/ppermute | solution.py:482
  103.5 1.3 collective-permute-start.6
  146.6 19.8 %copy-start.2 = (bf16[384,2048]{1,0:T(8,128)(2,1)S(1)}, bf16[384,2048]{1,0:T(8,128)(2,1)}, u32[]{:S(2)}) copy-start(bf16[384,2048]{1,0:T(8,128)(2,1)} %copy-done.1) | copy-start | bytes 4718596
  164.5 1.9 %collective-permute-start.9 = (f32[64,16,128]{2,1,0:T(8,128)S(1)}, f32[64,16,128]{2,1,0:T(8,128)S(1)}, u32[]{:S(2)}, u32[]{:S(2)}) collective-permute-start(f32[64,16,128]{2,1,0:T(8,128)S(1)} %all_to_all.35.mine_ref), channel_id=1, source_target_pairs={{0,1},{1,0},{2,3},{3,2},{4,5},{5,4},{6,7},{7,6},{8,9},{9,8},{10,11... | collective-permute-start | bytes 1572872 | tf_op jit(solution)/shard_map/ppermute | solution.py:482

commit v4 on v3

--- a/solution.py
+++ b/solution.py
@@ -174,6 +174,10 @@
     slot = slot_row(place_ref, len_ref, dof_ref, sub, spots)
     rows = lax.broadcasted_iota(jnp.int32, (spots, slot.shape[1]), 0)
     return jnp.where(rows == slot, 1.0, 0.0).astype(jnp.bfloat16)
+
+
+def started(place_ref):
+    return place_ref[0] >= 0
 
 
 def column_copies(inverse_ref, buffer_ref, sems, start):
@@ -255,8 +259,6 @@
     basis_hbm,
     inverse_hbm,
     scaled_ref,
-    keep_ref,
-    send_ref,
     edge_ref,
     far_ref,
     own_ref,
@@ -265,7 +267,6 @@
     dof_ref,
     map_ref,
     basis_ref,
-    wide_ref,
     columns_ref,
     small_sems,
     sems,
@@ -284,53 +285,58 @@
     for copy in small:
         copy.start()
     copies = column_copies(inverse_hbm, columns_ref, sems, 0)
-    subs, coarse, _ = basis_ref.shape
-    for sub in range(subs):
-        wide_ref[sub] = jnp.zeros_like(wide_ref[sub])
-    for copy in small:
-        copy.wait()
-    for sub in range(subs):
-        wide_ref[sub, sub * coarse : (sub + 1) * coarse] = basis_ref[sub]
-        scaled = values_ref[sub].astype(jnp.float32) * weights_of(mult_ref[sub : sub + 1])
-        scaled_ref[sub] = scaled.astype(jnp.bfloat16)
-    part_out(place_ref, scaled_ref, wide_ref, keep_ref, send_ref)
-    edge_far(
-        copies,
-        place_ref,
-        len_ref,
-        mult_ref,
-        dof_ref,
-        scaled_ref,
-        columns_ref,
-        edge_ref,
-        far_ref,
-        basis_ref,
-        map_ref,
-        own_ref,
-    )
-
-
-def inner_kernel(place_ref, len_ref, scaled_ref, mult_ref, dof_ref, edge_ref, inverse_ref, *refs):
-    *inputs, buffer_ref, sems = refs
-    if len(inputs) == 6:
-        basis_ref, map_ref, after_ref, inner_ref, mate_ref, own_ref = inputs
-    else:
-        (after_ref, inner_ref, mate_ref), basis_ref, map_ref, own_ref = inputs, None, None, None
+
+    @pl.when(started(place_ref))
+    def _():
+        for copy in small:
+            copy.wait()
+        for sub in range(values_ref.shape[0]):
+            scaled = values_ref[sub].astype(jnp.float32) * weights_of(mult_ref[sub : sub + 1])
+            scaled_ref[sub] = scaled.astype(jnp.bfloat16)
+        edge_far(
+            copies,
+            place_ref,
+            len_ref,
+            mult_ref,
+            dof_ref,
+            scaled_ref,
+            columns_ref,
+            edge_ref,
+            far_ref,
+            basis_ref,
+            map_ref,
+            own_ref,
+        )
+
+
+def inner_kernel(
+    place_ref,
+    len_ref,
+    scaled_ref,
+    mult_ref,
+    dof_ref,
+    edge_ref,
+    basis_ref,
+    inverse_ref,
+    *refs,
+):
+    *inputs, wide_ref, buffer_ref, sems = refs
     copies = column_copies(
         inverse_ref, buffer_ref, sems, inverse_ref.shape[2] - buffer_ref.shape[2]
     )
-    slot_sums(
-        place_ref,
-        len_ref,
-        mult_ref,
-        dof_ref,
-        0,
-        edge_ref,
-        mate_ref,
-        basis_ref,
-        map_ref,
-        own_ref,
-    )
+    if len(inputs) == 7:
+        map_ref, after_ref, inner_ref, mate_ref, keep_ref, send_ref, own_ref = inputs
+        more = (basis_ref, map_ref, own_ref)
+    else:
+        after_ref, inner_ref, mate_ref, keep_ref, send_ref = inputs
+        more = (None, None, None)
+
+    @pl.when(started(place_ref))
+    def _():
+        widen(basis_ref, wide_ref)
+        part_out(place_ref, scaled_ref, wide_ref, keep_ref, send_ref)
+        slot_sums(place_ref, len_ref, mult_ref, dof_ref, 0, edge_ref, mate_ref, *more)
+
     for sub in range(scaled_ref.shape[0]):
         copies[sub].wait()
         inner_ref[sub] = mul(scaled_ref[sub], buffer_ref[sub])
@@ -417,8 +423,6 @@
             inverse_hbm,
             out_hbm,
             scaled_ref,
-            keep_ref,
-            send_ref,
             edge_ref,
             far_ref,
             columns_ref,
@@ -433,47 +437,50 @@
         pltpu.make_async_copy(values_ref.at[sub], out_hbm.at[sub], leave_sems.at[sub])
         for sub in range(subs)
     ]
-    widen(basis_ref, wide_ref)
-    maps = jnp.concatenate([flat_map(own_ref), flat_map(mate_ref), far_map_ref[...]], axis=1)
-    looked = jnp.zeros((4 * half, 3 * entries), jnp.float32)
-    for pair in range(chips // 2):
-        mine = jnp.concatenate([mine_ref[2 * pair], mine_ref[2 * pair + 1]], axis=1)
-        other = jnp.concatenate([other_ref[2 * pair], other_ref[2 * pair + 1]], axis=1)
-        both = halves(jnp.concatenate([mine, other], axis=0))
-        looked = looked + mul(both, hot_pair(maps, pair))
-    looked = folded(looked, cases)
-    turned = jnp.concatenate([looked[half:], looked[:half]], axis=0)
-    looked = jnp.where(place_ref[1] == 0, looked, turned)
-    own = thirds(looked[:, :entries])
-    looked = thirds(looked)
-    for sub in range(subs):
-        columns = slice(sub * width, (sub + 1) * width)
-        values_ref[sub, :, :width] = head_ref[:, columns] + folded(
-            mul(looked, shared_ref[:, columns]), cases
-        )
-        values_ref[sub, :, width:] = inner_ref[sub] + folded(
-            mul(own, wide_ref[sub, :, width:]), cases
-        )
-        leave[sub].start()
-    if len(inputs) > 1:
+
+    @pl.when(started(place_ref))
+    def _():
+        widen(basis_ref, wide_ref)
+        maps = jnp.concatenate([flat_map(own_ref), flat_map(mate_ref), far_map_ref[...]], axis=1)
+        looked = jnp.zeros((4 * half, 3 * entries), jnp.float32)
+        for pair in range(chips // 2):
+            mine = jnp.concatenate([mine_ref[2 * pair], mine_ref[2 * pair + 1]], axis=1)
+            other = jnp.concatenate([other_ref[2 * pair], other_ref[2 * pair + 1]], axis=1)
+            both = halves(jnp.concatenate([mine, other], axis=0))
+            looked = looked + mul(both, hot_pair(maps, pair))
+        looked = folded(looked, cases)
+        turned = jnp.concatenate([looked[half:], looked[:half]], axis=0)
+        looked = jnp.where(place_ref[1] == 0, looked, turned)
+        own = thirds(looked[:, :entries])
+        looked = thirds(looked)
         for sub in range(subs):
-            scaled = values_ref[sub] * weights_of(mult_ref[sub : sub + 1])
-            scaled_ref[sub] = scaled.astype(jnp.bfloat16)
-        part_out(place_ref, scaled_ref, wide_ref, keep_ref, send_ref)
-        edge_far(
-            copies,
-            place_ref,
-            len_ref,
-            mult_ref,
-            dof_ref,
-            scaled_ref,
-            columns_ref,
-            edge_ref,
-            far_ref,
-            None,
-            None,
-            None,
-        )
+            columns = slice(sub * width, (sub + 1) * width)
+            values_ref[sub, :, :width] = head_ref[:, columns] + folded(
+                mul(looked, shared_ref[:, columns]), cases
+            )
+            values_ref[sub, :, width:] = inner_ref[sub] + folded(
+                mul(own, wide_ref[sub, :, width:]), cases
+            )
+            leave[sub].start()
+        if len(inputs) > 1:
+            for sub in range(subs):
+                scaled = values_ref[sub] * weights_of(mult_ref[sub : sub + 1])
+                scaled_ref[sub] = scaled.astype(jnp.bfloat16)
+            edge_far(
+                copies,
+                place_ref,
+                len_ref,
+                mult_ref,
+                dof_ref,
+                scaled_ref,
+                columns_ref,
+                edge_ref,
+                far_ref,
+                None,
+                None,
+                None,
+            )
+
     for copy in leave:
         copy.wait()
 
@@ -530,7 +537,7 @@
     mate_map = swap(coarse_map)
     other_rows = swap(coarse_inverse)
     wide = pltpu.VMEM((subs, entries, length), jnp.bfloat16)
-    opened = (bf16(subs, cases, length), f32(half, entries), f32(half, entries), f32(cases, spots))
+    opened = (bf16(subs, cases, length), f32(cases, spots))
 
     def dense(keep, got, *after):
         parts = call(
@@ -544,18 +551,30 @@
 
     def inner_solve(scaled, edge, far, *more):
         outs = [f32(subs, cases, length - width), f32(sent if more else cases, owned)]
+        outs += [f32(half, entries)] * 2
         if more:
             outs.append(bf16(entries, owned))
         return call(
             inner_kernel,
             "inner",
             tuple(outs),
-            (place, iface_len, scaled, multiplicity, iface_dof, edge, local_inverse, *more, far),
-            [SMEM] * 2 + [VMEM] * 4 + [HBM] + [VMEM] * len(more) + [ANY],
+            (
+                place,
+                iface_len,
+                scaled,
+                multiplicity,
+                iface_dof,
+                edge,
+                coarse_basis,
+                local_inverse,
+                *more,
+                far,
+            ),
+            [SMEM] * 2 + [VMEM] * 5 + [HBM] + [VMEM] * len(more) + [ANY],
             flops=2 * scaled.size * (length - width) + slot_flops // 2,
             moved=inverse_bytes * 3 // 4,
             mib=60 if more else 50,
-            scratch_shapes=buffers(length - width),
+            scratch_shapes=[wide, *buffers(length - width)],
         )
 
     def coarse_solve(parts, after):
@@ -591,7 +610,7 @@
         outs, out_specs, specs, scratch = [f32(subs, cases, length)], [HBM], [], []
         if more:
             outs += [*opened, f32(cases, owned)]
-            out_specs += [VMEM] * 5
+            out_specs += [VMEM] * 3
             specs = [SMEM, VMEM, VMEM, HBM]
             scratch = buffers(width)
         return call(
@@ -622,7 +641,7 @@
             ],
         )
 
-    scaled, keep, send, edge, far, own_far = call(
+    scaled, edge, far, own_far = call(
         first_kernel,
         "first",
         (*opened, f32(sent, owned), bf16(entries, owned)),
@@ -644,27 +663,26 @@
             pltpu.VMEM(iface_dof.shape, jnp.int32),
             pltpu.VMEM(coarse_map.shape, jnp.int32),
             pltpu.VMEM(coarse_basis.shape, jnp.bfloat16),
-            wide,
             buffers(width)[0],
             pltpu.SemaphoreType.DMA((5,)),
             buffers(width)[1],
         ],
     )
-    got, from_far = swap(send), far_swap(far)
-    inner, mate, own_mate = inner_solve(scaled, edge, far, coarse_basis, coarse_map)
-    from_mate = swap(mate)
+    from_far = far_swap(far)
+    inner, mate, keep, send, own_mate = inner_solve(scaled, edge, far, coarse_map)
+    got, from_mate = swap(send), swap(mate)
     parts = dense(keep, got, from_mate, from_far)
     head, shared, far_map = assemble(
         edge, mate, far, from_mate, from_far, parts, coarse_basis, own_mate, own_far
     )
     mine = coarse_solve(parts, (head,))
-    first_apply, scaled, keep, send, edge, far = correct(
+    first_apply, scaled, edge, far = correct(
         mine, head, shared, inner, iface_len, multiplicity, iface_dof, local_inverse
     )
 
-    got, from_far = swap(send), far_swap(far)
-    inner, mate = inner_solve(scaled, edge, far)
-    from_mate = swap(mate)
+    from_far = far_swap(far)
+    inner, mate, keep, send = inner_solve(scaled, edge, far)
+    got, from_mate = swap(send), swap(mate)
     parts = dense(keep, got, from_mate, from_far)
     (head,) = assemble(edge, mate, far, from_mate, from_far, parts)
     mine = coarse_solve(parts, (head,))

time: 172 us -> 169 us (0.983)
  Pallas kernels: 44.1 us -> 39.6 us
    pallas_call x13, Pallas kernels: 44.1 us -> 39.6 us  [call(): pl.pallas_call(kernel, out_shape=out_shape, in_specs=specs, compiler_para...]
  transfers between devices with their start and end apart: 10 -> 10, of which waited for: 6 -> 6; matrix products, arithmetic and copies ran while one was open for 0% -> 0% of each run, Pallas kernels for 15% -> 14%
where the time goes in v4:
time: 169 us; the launch traced here: 167 us
  blocking collectives  106 us (63%)
  Pallas kernels  39.6 us (23%)
  starting transfers between devices  12 us (7%)
  waiting for transfers between devices  6.89 us (4%)
    all_to_all x6, blocking collectives, by_chip(): return lax.all_to_all(value, CHIPS, 0, 0, tiled=True)  106 us
    pallas_call x13, Pallas kernels, call(): pl.pallas_call(kernel, out_shape=out_shape, in_specs=specs, compiler_para...  39.6 us
    ppermute x2, starting transfers between devices, far_swap(): return lax.ppermute(value, DOM, pairs)  10.6 us
    ppermute x8, waiting for transfers between devices, swap(): return lax.ppermute(value, 'c', [(0, 1), (1, 0)])  5.82 us
  transfers between devices with their start and end apart: 10, of which 6 were waited for; matrix products, arithmetic and copies ran while one was open for 0% of the time, Pallas kernels for 14%

profile of v4, /device:TPU:0, one launch (start us, length us, event | category | flops | bytes accessed | tf_op | source)
XLA Modules:
  0.0 167.0 jit_solution(17629282947569936199)
XLA Ops:
  0.6 0.1 collective-permute-start.4
  0.7 0.7 pad_add_fusion.place_ref
  1.4 5.8 %first.1 = (bf16[8,32,1024]{2,1,0:T(8,128)(2,1)}, f32[32,2048]{1,0:T(8,128)}, f32[64,1024]{1,0:T(8,128)}, bf16[128,1024]{1,0:T(8,128)(2,1)}) custom-call(s32[2]{0:T(128)} %pad_add_fusion.place_ref, s32[8]{0:T(128)} %len_ref.9, bf16[8,32,1024]{2,1,0:T(8,128)(2,1)} %values_hbm.1, s32[8,1024]{1,0:T(8,128)} %mult_ref.3, s32[8,256]{1,0:T(8,128)} %dof_ref.7, ...), custom_call_target="tpu_custom_call" | custom-call | flops 1000000 | bytes 1048576 | tf_op jit(solution)/shard_map/first/pallas_call | solution.py:49
  7.2 8.9 %collective-permute-start.2 = (f32[64,1024]{1,0:T(8,128)}, f32[64,1024]{1,0:T(8,128)S(1)}, u32[]{:S(2)}, u32[]{:S(2)}) collective-permute-start(f32[64,1024]{1,0:T(8,128)} %get-tuple-element.24.refs_1_.far_ref), channel_id=1, source_target_pairs={{1,2},{2,1},{3,4},{4,3},{5,6},{6,5},{7,8},{8,7},{9,10},{10,9},{11,... | collective-permute-start | bytes 786440 | tf_op jit(solution)/shard_map/ppermute | solution.py:498
  16.2 7.3 %inner.2 = (f32[8,32,768]{2,1,0:T(8,128)}, f32[64,1024]{1,0:T(8,128)}, f32[16,128]{1,0:T(8,128)}, f32[16,128]{1,0:T(8,128)}, bf16[128,1024]{1,0:T(8,128)(2,1)}) custom-call(s32[2]{0:T(128)} %pad_add_fusion.place_ref, s32[8]{0:T(128)} %len_ref.9, bf16[8,32,1024]{2,1,0:T(8,128)(2,1)} %get-tuple-element.23.scaled_ref, s32[8,1024]{1,0:T(8,128)} %mult_ref.3, ...), custom_call_target="tpu_custom_call" | custom-call | flops 805306368 | bytes 12582912 | tf_op jit(solution)/shard_map/inner/pallas_call | solution.py:49
  23.5 0.0 copy-start.1
  23.5 0.0 copy-start.6
  23.5 0.0 copy-start.9
  23.5 0.0 copy-start.11
  23.5 0.1 collective-permute-start.1
  23.6 0.5 collective-permute-start.3
  24.1 0.1 collective-permute-start
  24.2 1.1 collective-permute-done.mate_ref
  25.3 0.1 collective-permute-done.3.got_ref
  25.4 0.0 collective-permute-done.2.refs_1_.from_far_ref
  25.4 0.0 collective-permute-done.1.refs_0_.from_mate_ref
  25.4 0.7 copy-done.12
  26.1 1.1 dense.2
  27.2 18.2 %all_to_all.30.after_ref.parts_ref = f32[64,16,128]{2,1,0:T(8,128)S(1)} all-to-all(f32[64,16,128]{2,1,0:T(8,128)S(1)} %dense.2), channel_id=1, replica_groups=mesh['y'=4,'z'=4,'x'=4,'c'=2] {'y','z','x'}, dimensions={0} | all-to-all | bytes 1048576 | tf_op jit(solution)/shard_map/all_to_all | solution.py:502
  45.5 0.0 copy-done.13
  45.5 0.0 copy-start
  45.5 3.7 %head.2 = (f32[32,2048]{1,0:T(8,128)S(1)}, bf16[384,2048]{1,0:T(8,128)(2,1)S(1)}, f32[1,128]{1,0:T(1,128)S(1)}) custom-call(s32[2]{0:T(128)S(1)} %copy-done.10, s32[8]{0:T(128)S(1)} %copy-done.11, f32[32,2048]{1,0:T(8,128)S(1)} %copy-done.6, f32[64,1024]{1,0:T(8,128)S(1)} %copy-done.14, f32[64,1024]{1,0:T(8,128)S(1)} %copy-done.7, ...), custom_call_target="tpu_custom_call" | custom-call | flops 805306368 | bytes 1048576 | tf_op jit(solution)/shard_map/head/pallas_call | solution.py:49
  49.3 0.1 sum.2
  49.4 17.4 %all_to_all.31.rhs_ref = f32[64,16,128]{2,1,0:T(8,128)S(1)} all-to-all(f32[64,16,128]{2,1,0:T(8,128)S(1)} %sum.2), channel_id=1, replica_groups=mesh['y'=4,'z'=4,'x'=4,'c'=2] {'y','z','x'}, dimensions={0} | all-to-all | bytes 1048576 | tf_op jit(solution)/shard_map/all_to_all | solution.py:502
  66.8 0.0 collective-permute-done.4.other_ref
  66.8 1.4 solve.2
  68.2 16.5 %all_to_all.32.mine_ref = f32[64,16,128]{2,1,0:T(8,128)S(1)} all-to-all(f32[64,16,128]{2,1,0:T(8,128)S(1)} %solve.2), channel_id=1, replica_groups=mesh['y'=4,'z'=4,'x'=4,'c'=2] {'y','z','x'}, dimensions={0} | all-to-all | bytes 1048576 | tf_op jit(solution)/shard_map/all_to_all | solution.py:502
  84.7 0.0 collective-permute-start.5
  84.7 1.9 %collective-permute-done.5.other_ref = f32[64,16,128]{2,1,0:T(8,128)S(1)} collective-permute-done((f32[64,16,128]{2,1,0:T(8,128)S(1)}, f32[64,16,128]{2,1,0:T(8,128)S(1)}, u32[]{:S(2)}, u32[]{:S(2)}) %collective-permute-start.5) | collective-permute-done | bytes 524320 | tf_op jit(solution)/shard_map/ppermute | solution.py:489
  86.6 0.0 copy-done.4
  86.7 5.8 %correct.2 = (f32[8,32,1024]{2,1,0:T(8,128)}, bf16[8,32,1024]{2,1,0:T(8,128)(2,1)S(1)}, f32[32,2048]{1,0:T(8,128)S(1)}, f32[32,1024]{1,0:T(8,128)S(1)}) custom-call(s32[2]{0:T(128)S(1)} %copy-done.10, s32[8,16]{1,0:T(8,128)S(1)} %copy-done.8, s32[8,16]{1,0:T(8,128)S(1)} %collective-permute-done.mate_ref, f32[1,128]{1,0:T(1,128)S(1)} %get-tuple-element.30.far_map_ref, ...), custom_call_target="tpu_custom_call" | custom-call | flops 1000000 | bytes 1048576 | tf_op jit(solution)/shard_map/correct/pallas_call | solution.py:49
  92.5 1.7 %collective-permute-start.8 = (f32[32,1024]{1,0:T(8,128)S(1)}, f32[32,1024]{1,0:T(8,128)S(1)}, u32[]{:S(2)}, u32[]{:S(2)}) collective-permute-start(f32[32,1024]{1,0:T(8,128)S(1)} %get-tuple-element.37.refs_0_.far_ref), channel_id=1, source_target_pairs={{1,2},{2,1},{3,4},{4,3},{5,6},{6,5},{7,8},{8,7},{9,10},{10,9},{11,... | collective-permute-start | bytes 393224 | tf_op jit(solution)/shard_map/ppermute | solution.py:498
  94.2 5.7 %inner.3 = (f32[8,32,768]{2,1,0:T(8,128)S(1)}, f32[32,1024]{1,0:T(8,128)S(1)}, f32[16,128]{1,0:T(8,128)S(1)}, f32[16,128]{1,0:T(8,128)S(1)}) custom-call(s32[2]{0:T(128)S(1)} %copy-done.10, s32[8]{0:T(128)S(1)} %copy-done.11, bf16[8,32,1024]{2,1,0:T(8,128)(2,1)S(1)} %get-tuple-element.35.scaled_ref, s32[8,1024]{1,0:T(8,128)S(1)} %copy-done.5, ...), custom_call_target="tpu_custom_call" | custom-call | flops 805306368 | bytes 12582912 | tf_op jit(solution)/shard_map/inner/pallas_call | solution.py:49
  99.9 0.1 collective-permute-start.7
  100.0 0.5 collective-permute-start.6
  100.5 0.8 collective-permute-done.6.got_ref
  101.3 1.1 collective-permute-done.8.refs_1_.from_far_ref
  102.4 0.0 collective-permute-done.7.refs_0_.from_mate_ref
  102.4 1.1 dense.3
  103.5 20.6 %all_to_all.33.after_ref.parts_ref = f32[64,16,128]{2,1,0:T(8,128)S(1)} all-to-all(f32[64,16,128]{2,1,0:T(8,128)S(1)} %dense.3), channel_id=1, replica_groups=mesh['y'=4,'z'=4,'x'=4,'c'=2] {'y','z','x'}, dimensions={0} | all-to-all | bytes 1048576 | tf_op jit(solution)/shard_map/all_to_all | solution.py:502
  124.1 2.1 %head.3.refs_0_.head_ref = f32[32,2048]{1,0:T(8,128)S(1)} custom-call(s32[2]{0:T(128)S(1)} %copy-done.10, s32[8]{0:T(128)S(1)} %copy-done.11, f32[32,2048]{1,0:T(8,128)S(1)} %get-tuple-element.36.edge_ref, f32[32,1024]{1,0:T(8,128)S(1)} %get-tuple-element.40.mate_ref, f32[32,1024]{1,0:T(8,128)S(1)} %get-tuple-element.37.refs_0_.far_ref, ...), custom_call_target="tpu_custom_call" | custom-call | flops 805306368 | bytes 1048576 | tf_op jit(solution)/shard_map/head/pallas_call | solution.py:49
  126.2 0.1 sum.3
  126.3 16.8 %all_to_all.34.rhs_ref = f32[64,16,128]{2,1,0:T(8,128)S(1)} all-to-all(f32[64,16,128]{2,1,0:T(8,128)S(1)} %sum.3), channel_id=1, replica_groups=mesh['y'=4,'z'=4,'x'=4,'c'=2] {'y','z','x'}, dimensions={0} | all-to-all | bytes 1048576 | tf_op jit(solution)/shard_map/all_to_all | solution.py:502
  143.1 1.4 solve.3
  144.5 16.5 %all_to_all.35.mine_ref = f32[64,16,128]{2,1,0:T(8,128)S(1)} all-to-all(f32[64,16,128]{2,1,0:T(8,128)S(1)} %solve.3), channel_id=1, replica_groups=mesh['y'=4,'z'=4,'x'=4,'c'=2] {'y','z','x'}, dimensions={0} | all-to-all | bytes 1048576 | tf_op jit(solution)/shard_map/all_to_all | solution.py:502
  161.0 0.0 collective-permute-start.9
  161.0 1.9 %collective-permute-done.9.other_ref = f32[64,16,128]{2,1,0:T(8,128)S(1)} collective-permute-done((f32[64,16,128]{2,1,0:T(8,128)S(1)}, f32[64,16,128]{2,1,0:T(8,128)S(1)}, u32[]{:S(2)}, u32[]{:S(2)}) %collective-permute-start.9) | collective-permute-done | bytes 524320 | tf_op jit(solution)/shard_map/ppermute | solution.py:489
  162.9 3.9 %correct.3 = f32[8,32,1024]{2,1,0:T(8,128)} custom-call(s32[2]{0:T(128)S(1)} %copy-done.10, s32[8,16]{1,0:T(8,128)S(1)} %copy-done.8, s32[8,16]{1,0:T(8,128)S(1)} %collective-permute-done.mate_ref, f32[1,128]{1,0:T(1,128)S(1)} %get-tuple-element.30.far_map_ref, f32[64,16,128]{2,1,0:T(8,128)S(1)} %all_to_all.35.mine_ref, ...), custom_call_target="tpu_custom_call" | custom-call | flops 1000000 | bytes 1048576 | tf_op jit(solution)/shard_map/correct/pallas_call | solution.py:49
  (24 shorter events, 0.0 us)
Async XLA Ops:
  0.6 66.2 %collective-permute-start.4 = (f32[64,8192]{1,0:T(8,128)}, f32[64,8192]{1,0:T(8,128)S(1)}, u32[]{:S(2)}, u32[]{:S(2)}) collective-permute-start(f32[64,8192]{1,0:T(8,128)} %mine_ref.3), channel_id=1, source_target_pairs={{0,1},{1,0},{2,3},{3,2},{4,5},{5,4},{6,7},{7,6},{8,9},{9,8},{10,11... | collective-permute-start | bytes 6291464 | tf_op jit(solution)/shard_map/ppermute | solution.py:489
  7.2 18.1 %collective-permute-start.2 = (f32[64,1024]{1,0:T(8,128)}, f32[64,1024]{1,0:T(8,128)S(1)}, u32[]{:S(2)}, u32[]{:S(2)}) collective-permute-start(f32[64,1024]{1,0:T(8,128)} %get-tuple-element.24.refs_1_.far_ref), channel_id=1, source_target_pairs={{1,2},{2,1},{3,4},{4,3},{5,6},{6,5},{7,8},{8,7},{9,10},{10,9},{11,... | collective-permute-start | bytes 786440 | tf_op jit(solution)/shard_map/ppermute | solution.py:498
  16.2 8.0 %copy-start.8 = (s32[8,16]{1,0:T(8,128)S(1)}, s32[8,16]{1,0:T(8,128)}, u32[]{:S(2)}) copy-start(s32[8,16]{1,0:T(8,128)} %own_ref.7) | copy-start | bytes 1540
  16.2 29.3 %copy-start.13 = (bf16[128,1024]{1,0:T(8,128)(2,1)S(1)}, bf16[128,1024]{1,0:T(8,128)(2,1)}, u32[]{:S(2)}) copy-start(bf16[128,1024]{1,0:T(8,128)(2,1)} %get-tuple-element.29.refs_2_) | copy-start | bytes 786436
  23.5 22.0 %copy-start.1 = (bf16[8,16,1024]{2,1,0:T(8,128)(2,1)S(1)}, bf16[8,16,1024]{2,1,0:T(8,128)(2,1)}, u32[]{:S(2)}) copy-start(bf16[8,16,1024]{2,1,0:T(8,128)(2,1)} %basis_ref.7) | copy-start | bytes 786436
  23.5 22.0 %copy-start.6 = (f32[32,2048]{1,0:T(8,128)S(1)}, f32[32,2048]{1,0:T(8,128)}, u32[]{:S(2)}) copy-start(f32[32,2048]{1,0:T(8,128)} %get-tuple-element.22.edge_ref) | copy-start | bytes 786436
  23.5 22.0 %copy-start.7 = (f32[64,1024]{1,0:T(8,128)S(1)}, f32[64,1024]{1,0:T(8,128)}, u32[]{:S(2)}) copy-start(f32[64,1024]{1,0:T(8,128)} %get-tuple-element.24.refs_1_.far_ref) | copy-start | bytes 786436
  23.5 22.0 %copy-start.9 = (s32[8,256]{1,0:T(8,128)S(1)}, s32[8,256]{1,0:T(8,128)}, u32[]{:S(2)}) copy-start(s32[8,256]{1,0:T(8,128)} %dof_ref.7) | copy-start | bytes 24580
  23.5 22.0 %copy-start.10 = (s32[2]{0:T(128)S(1)}, s32[2]{0:T(128)}, u32[]{:S(2)}) copy-start(s32[2]{0:T(128)} %pad_add_fusion.place_ref) | copy-start | bytes 28
  23.5 22.0 %copy-start.11 = (s32[8]{0:T(128)S(1)}, s32[8]{0:T(128)}, u32[]{:S(2)}) copy-start(s32[8]{0:T(128)} %len_ref.9) | copy-start | bytes 100
  23.5 1.8 %collective-permute-start.1 = (f32[64,1024]{1,0:T(8,128)}, f32[64,1024]{1,0:T(8,128)S(1)}, u32[]{:S(2)}, u32[]{:S(2)}) collective-permute-start(f32[64,1024]{1,0:T(8,128)} %get-tuple-element.25.mate_ref), channel_id=1, source_target_pairs={{0,1},{1,0},{2,3},{3,2},{4,5},{5,4},{6,7},{7,6},{8,9},{9,8},{10,11... | collective-permute-start | bytes 786440 | tf_op jit(solution)/shard_map/ppermute | solution.py:489
  23.6 1.7 %collective-permute-start.3 = (f32[16,128]{1,0:T(8,128)}, f32[16,128]{1,0:T(8,128)S(1)}, u32[]{:S(2)}, u32[]{:S(2)}) collective-permute-start(f32[16,128]{1,0:T(8,128)} %get-tuple-element.27), channel_id=1, source_target_pairs={{0,1},{1,0},{2,3},{3,2},{4,5},{5,4},{6,7},{7,6},{8,9},{9,8},{10,11... | collective-permute-start | bytes 24584 | tf_op jit(solution)/shard_map/ppermute | solution.py:489
  24.1 1.2 collective-permute-start
  25.4 0.7 copy-start.12
  26.1 19.4 %copy-start.14 = (f32[64,1024]{1,0:T(8,128)S(1)}, f32[64,1024]{1,0:T(8,128)}, u32[]{:S(2)}) copy-start(f32[64,1024]{1,0:T(8,128)} %get-tuple-element.25.mate_ref) | copy-start | bytes 786436
  26.1 19.4 %copy-start.15 = (bf16[128,1024]{1,0:T(8,128)(2,1)S(1)}, bf16[128,1024]{1,0:T(8,128)(2,1)}, u32[]{:S(2)}) copy-start(bf16[128,1024]{1,0:T(8,128)(2,1)} %get-tuple-element.28.refs_1_) | copy-start | bytes 786436
  45.5 21.3 %copy-start = (f32[64,8192]{1,0:T(8,128)S(1)}, f32[64,8192]{1,0:T(8,128)}, u32[]{:S(2)}) copy-start(f32[64,8192]{1,0:T(8,128)} %mine_ref.3) | copy-start | bytes 6291460
  49.3 19.0 %copy-start.2 = (bf16[384,2048]{1,0:T(8,128)(2,1)}, bf16[384,2048]{1,0:T(8,128)(2,1)S(1)}, u32[]{:S(2)}) copy-start(bf16[384,2048]{1,0:T(8,128)(2,1)S(1)} %get-tuple-element.32.shared_ref) | copy-start | bytes 4718596
  66.8 19.9 %copy-start.4 = (f32[8,32,768]{2,1,0:T(8,128)S(1)}, f32[8,32,768]{2,1,0:T(8,128)}, u32[]{:S(2)}) copy-start(f32[8,32,768]{2,1,0:T(8,128)} %get-tuple-element.33.inner_ref) | copy-start | bytes 2359300
  66.8 19.9 %copy-start.5 = (s32[8,1024]{1,0:T(8,128)S(1)}, s32[8,1024]{1,0:T(8,128)}, u32[]{:S(2)}) copy-start(s32[8,1024]{1,0:T(8,128)} %mult_ref.3) | copy-start | bytes 98308
  84.7 1.9 %collective-permute-start.5 = (f32[64,16,128]{2,1,0:T(8,128)S(1)}, f32[64,16,128]{2,1,0:T(8,128)S(1)}, u32[]{:S(2)}, u32[]{:S(2)}) collective-permute-start(f32[64,16,128]{2,1,0:T(8,128)S(1)} %all_to_all.32.mine_ref), channel_id=1, source_target_pairs={{0,1},{1,0},{2,3},{3,2},{4,5},{5,4},{6,7},{7,6},{8,9},{9,8},{10,11... | collective-permute-start | bytes 1572872 | tf_op jit(solution)/shard_map/ppermute | solution.py:489
  92.5 9.9 %collective-permute-start.8 = (f32[32,1024]{1,0:T(8,128)S(1)}, f32[32,1024]{1,0:T(8,128)S(1)}, u32[]{:S(2)}, u32[]{:S(2)}) collective-permute-start(f32[32,1024]{1,0:T(8,128)S(1)} %get-tuple-element.37.refs_0_.far_ref), channel_id=1, source_target_pairs={{1,2},{2,1},{3,4},{4,3},{5,6},{6,5},{7,8},{8,7},{9,10},{10,9},{11,... | collective-permute-start | bytes 393224 | tf_op jit(solution)/shard_map/ppermute | solution.py:498
  99.9 2.5 %collective-permute-start.7 = (f32[32,1024]{1,0:T(8,128)S(1)}, f32[32,1024]{1,0:T(8,128)S(1)}, u32[]{:S(2)}, u32[]{:S(2)}) collective-permute-start(f32[32,1024]{1,0:T(8,128)S(1)} %get-tuple-element.40.mate_ref), channel_id=1, source_target_pairs={{0,1},{1,0},{2,3},{3,2},{4,5},{5,4},{6,7},{7,6},{8,9},{9,8},{10,11... | collective-permute-start | bytes 393224 | tf_op jit(solution)/shard_map/ppermute | solution.py:489
  100.0 1.3 collective-permute-start.6
  143.1 19.8 %copy-start.3 = (bf16[384,2048]{1,0:T(8,128)(2,1)S(1)}, bf16[384,2048]{1,0:T(8,128)(2,1)}, u32[]{:S(2)}) copy-start(bf16[384,2048]{1,0:T(8,128)(2,1)} %copy-done.2) | copy-start | bytes 4718596
  161.0 1.9 %collective-permute-start.9 = (f32[64,16,128]{2,1,0:T(8,128)S(1)}, f32[64,16,128]{2,1,0:T(8,128)S(1)}, u32[]{:S(2)}, u32[]{:S(2)}) collective-permute-start(f32[64,16,128]{2,1,0:T(8,128)S(1)} %all_to_all.35.mine_ref), channel_id=1, source_target_pairs={{0,1},{1,0},{2,3},{3,2},{4,5},{5,4},{6,7},{7,6},{8,9},{9,8},{10,11... | collective-permute-start | bytes 1572872 | tf_op jit(solution)/shard_map/ppermute | solution.py:489

commit v5 on v4

--- a/solution.py
+++ b/solution.py
@@ -71,14 +71,14 @@
     return 1.0 / multiplicity.astype(jnp.float32)
 
 
-def part_out(place_ref, scaled_ref, basis_ref, keep_ref, send_ref):
+def parts_of(place_ref, scaled_ref, basis_ref):
     parts = mul_rows(scaled_ref[0], basis_ref[0])
     for sub in range(1, basis_ref.shape[0]):
         parts = parts + mul_rows(scaled_ref[sub], basis_ref[sub])
-    half = keep_ref.shape[0]
-    first = place_ref[1] == 0
-    keep_ref[...] = jnp.where(first, parts[:half], parts[half:])
-    send_ref[...] = jnp.where(first, parts[half:], parts[:half])
+    half = parts.shape[0] // 2
+    first = lax.rem(place_ref[0], 2) == 0
+    keep = jnp.where(first, parts[:half], parts[half:])
+    return keep, jnp.where(first, parts[half:], parts[:half])
 
 
 def widen(basis_ref, wide_ref):
@@ -115,10 +115,12 @@
     return rows.astype(jnp.float32).T
 
 
-def dense_kernel(own_ref, mate_ref, keep_ref, got_ref, *refs):
+def dense_kernel(own_ref, mate_ref, keep_ref, arrived_ref, *refs):
     out_ref = refs[-1]
     cases, width = keep_ref.shape
-    value = halves(jnp.concatenate([keep_ref[...], got_ref[...]], axis=1))
+    got = arrived_ref[arrived_ref.shape[0] - cases // 2 :, : 2 * width]
+    got = jnp.concatenate([got[:, :width], got[:, width:]], axis=0)
+    value = halves(jnp.concatenate([keep_ref[...], got], axis=1))
     maps = jnp.concatenate([flat_map(own_ref), flat_map(mate_ref)], axis=1)
     maps = columns_of(maps)[:, :1]
     wide = 2 * out_ref.shape[2]
@@ -139,7 +141,7 @@
         out_ref[chip] = total
 
 
-def solve_kernel(core_ref, rhs_ref, mine_ref, other_ref, out_ref):
+def solve_kernel(place_ref, rhs_ref, mine_ref, other_ref, out_ref):
     cases, width = rhs_ref.shape[1:]
     total = jnp.zeros((2 * cases, 4 * mine_ref.shape[0]), jnp.float32)
     for pair in range(rhs_ref.shape[0] // 2):
@@ -151,7 +153,7 @@
     own = total[:, :width] + total[:, width:]
     half = width // 2
     turned = jnp.concatenate([own[:, half:], own[:, :half]], axis=1)
-    own = jnp.where(core_ref[0] == 0, own, turned)
+    own = jnp.where(lax.rem(place_ref[0], 2) == 0, own, turned)
     for chip in range(out_ref.shape[0]):
         out_ref[chip] = own
 
@@ -165,7 +167,7 @@
     dof = dof_ref[sub : sub + 1]
     owner = lax.div(dof, owned)
     away = (owner != place_ref[0]).astype(jnp.int32)
-    far = jnp.where(place_ref[1] == 0, away, 1 - away)
+    far = jnp.where(lax.rem(place_ref[0], 2) == 0, away, 1 - away)
     live = live_of(len_ref, sub, dof.shape[1])
     return jnp.where(live, far * owned + (dof - owner * owned), -1)
 
@@ -230,9 +232,9 @@
         total = moved if total is None else total + moved
     count = total.shape[0]
     sums_ref[:count] = total
+    sums_ref[count:] = jnp.zeros_like(sums_ref[count:])
     if basis_ref is not None:
         flat = flat_map(map_ref)
-        sums_ref[count:] = jnp.zeros_like(sums_ref[count:])
         sums_ref[count : count + 1, : flat.shape[1]] = flat
 
 
@@ -325,17 +327,22 @@
         inverse_ref, buffer_ref, sems, inverse_ref.shape[2] - buffer_ref.shape[2]
     )
     if len(inputs) == 7:
-        map_ref, after_ref, inner_ref, mate_ref, keep_ref, send_ref, own_ref = inputs
+        map_ref, after_ref, _, inner_ref, mate_ref, keep_ref, own_ref = inputs
         more = (basis_ref, map_ref, own_ref)
     else:
-        after_ref, inner_ref, mate_ref, keep_ref, send_ref = inputs
+        after_ref, _, inner_ref, mate_ref, keep_ref = inputs
         more = (None, None, None)
 
     @pl.when(started(place_ref))
     def _():
         widen(basis_ref, wide_ref)
-        part_out(place_ref, scaled_ref, wide_ref, keep_ref, send_ref)
+        keep, send = parts_of(place_ref, scaled_ref, wide_ref)
+        half, entries = keep.shape
+        keep_ref[...] = keep
         slot_sums(place_ref, len_ref, mult_ref, dof_ref, 0, edge_ref, mate_ref, *more)
+        last = mate_ref.shape[0] - half // 2
+        mate_ref[last:, :entries] = send[: half // 2]
+        mate_ref[last:, entries : 2 * entries] = send[half // 2 :]
 
     for sub in range(scaled_ref.shape[0]):
         copies[sub].wait()
@@ -450,7 +457,7 @@
             looked = looked + mul(both, hot_pair(maps, pair))
         looked = folded(looked, cases)
         turned = jnp.concatenate([looked[half:], looked[:half]], axis=0)
-        looked = jnp.where(place_ref[1] == 0, looked, turned)
+        looked = jnp.where(lax.rem(place_ref[0], 2) == 0, looked, turned)
         own = thirds(looked[:, :entries])
         looked = thirds(looked)
         for sub in range(subs):
@@ -521,10 +528,10 @@
     entries = subs * coarse
     spots = subs * width
     owned = spots // 2
-    place = jnp.stack([lax.axis_index(DOM), lax.axis_index("c")]).astype(jnp.int32)
-    core = place[1:]
+    place = lax.axis_index(DOM).astype(jnp.int32).reshape(1)
     slot_flops = 2 * 3 * cases * spots * spots
-    sent = cases + coarse + 16
+    kept = cases + half // 2
+    sent = kept + coarse + 16
     blocks = f32(chips, half, order // chips)
     inverse_bytes = 2 * local_inverse.size
 
@@ -539,19 +546,19 @@
     wide = pltpu.VMEM((subs, entries, length), jnp.bfloat16)
     opened = (bf16(subs, cases, length), f32(cases, spots))
 
-    def dense(keep, got, *after):
+    def dense(keep, arrived, *after):
         parts = call(
             dense_kernel,
             "dense",
             blocks,
-            (coarse_map, mate_map, keep, got, *after),
+            (coarse_map, mate_map, keep, arrived, *after),
             [VMEM] * 4 + [ANY] * len(after),
         )
         return by_chip(parts)
 
     def inner_solve(scaled, edge, far, *more):
-        outs = [f32(subs, cases, length - width), f32(sent if more else cases, owned)]
-        outs += [f32(half, entries)] * 2
+        outs = [f32(subs, cases, length - width), f32(sent if more else kept, owned)]
+        outs.append(f32(half, entries))
         if more:
             outs.append(bf16(entries, owned))
         return call(
@@ -569,8 +576,9 @@
                 local_inverse,
                 *more,
                 far,
+                mate_map,
             ),
-            [SMEM] * 2 + [VMEM] * 5 + [HBM] + [VMEM] * len(more) + [ANY],
+            [SMEM] * 2 + [VMEM] * 5 + [HBM] + [VMEM] * len(more) + [ANY] * 2,
             flops=2 * scaled.size * (length - width) + slot_flops // 2,
             moved=inverse_bytes * 3 // 4,
             mib=60 if more else 50,
@@ -586,7 +594,7 @@
             solve_kernel,
             "solve",
             blocks,
-            (core, rhs, coarse_inverse, other_rows),
+            (place, rhs, coarse_inverse, other_rows),
             [SMEM] + [VMEM] * 3,
         )
         return by_chip(own)
@@ -609,7 +617,7 @@
     def correct(mine, head, shared, inner, *more):
         outs, out_specs, specs, scratch = [f32(subs, cases, length)], [HBM], [], []
         if more:
-            outs += [*opened, f32(cases, owned)]
+            outs += [*opened, f32(kept, owned)]
             out_specs += [VMEM] * 3
             specs = [SMEM, VMEM, VMEM, HBM]
             scratch = buffers(width)
@@ -669,9 +677,9 @@
         ],
     )
     from_far = far_swap(far)
-    inner, mate, keep, send, own_mate = inner_solve(scaled, edge, far, coarse_map)
-    got, from_mate = swap(send), swap(mate)
-    parts = dense(keep, got, from_mate, from_far)
+    inner, mate, keep, own_mate = inner_solve(scaled, edge, far, coarse_map)
+    from_mate = swap(mate)
+    parts = dense(keep, from_mate, from_far)
     head, shared, far_map = assemble(
         edge, mate, far, from_mate, from_far, parts, coarse_basis, own_mate, own_far
     )
@@ -681,9 +689,9 @@
     )
 
     from_far = far_swap(far)
-    inner, mate, keep, send = inner_solve(scaled, edge, far)
-    got, from_mate = swap(send), swap(mate)
-    parts = dense(keep, got, from_mate, from_far)
+    inner, mate, keep = inner_solve(scaled, edge, far)
+    from_mate = swap(mate)
+    parts = dense(keep, from_mate, from_far)
     (head,) = assemble(edge, mate, far, from_mate, from_far, parts)
     mine = coarse_solve(parts, (head,))
     (second_apply,) = correct(mine, head, shared, inner)

time: 169 us -> 169 us (level)
    ppermute x2, waiting for transfers between devices: 1.06 us -> 2.77 us  [far_swap(): return lax.ppermute(value, DOM, pairs)]
    ppermute x8 -> x6, waiting for transfers between devices: 5.82 us -> 5.59 us  [swap(): return lax.ppermute(value, 'c', [(0, 1), (1, 0)])]
  transfers between devices with their start and end apart: 10 -> 8, of which waited for: 6 -> 4; matrix products, arithmetic and copies ran while one was open for 0% -> 0% of each run, Pallas kernels for 14% -> 14%
where the time goes in v5:
time: 169 us; the launch traced here: 167 us
  blocking collectives  106 us (63%)
  Pallas kernels  39.1 us (23%)
  starting transfers between devices  11 us (7%)
  waiting for transfers between devices  8.36 us (5%)
  local copies, waits for them, and re-layouts  2.02 us (1%)
    all_to_all x6, blocking collectives, by_chip(): return lax.all_to_all(value, CHIPS, 0, 0, tiled=True)  106 us
    pallas_call x13, Pallas kernels, call(): pl.pallas_call(kernel, out_shape=out_shape, in_specs=specs, compiler_para...  39.1 us
    ppermute x2, starting transfers between devices, far_swap(): return lax.ppermute(value, DOM, pairs)  10.2 us
    ppermute x6, waiting for transfers between devices, swap(): return lax.ppermute(value, 'c', [(0, 1), (1, 0)])  5.59 us
  transfers between devices with their start and end apart: 8, of which 4 were waited for; matrix products, arithmetic and copies ran while one was open for 0% of the time, Pallas kernels for 14%

profile of v5, /device:TPU:0, one launch (start us, length us, event | category | flops | bytes accessed | tf_op | source)
XLA Modules:
  0.0 167.1 jit_solution(4411197657129393740)
XLA Ops:
  0.6 0.1 collective-permute-start.3
  0.7 0.5 collective-permute-start
  1.2 5.8 %first.1 = (bf16[8,32,1024]{2,1,0:T(8,128)(2,1)}, f32[32,2048]{1,0:T(8,128)}, f32[72,1024]{1,0:T(8,128)}, bf16[128,1024]{1,0:T(8,128)(2,1)}) custom-call(s32[1]{0:T(128)} %bitcast.place_ref, s32[8]{0:T(128)} %len_ref.9, bf16[8,32,1024]{2,1,0:T(8,128)(2,1)} %values_hbm.1, s32[8,1024]{1,0:T(8,128)} %mult_ref.3, s32[8,256]{1,0:T(8,128)} %dof_ref.7, ...), custom_call_target="tpu_custom_call" | custom-call | flops 1000000 | bytes 1048576 | tf_op jit(solution)/shard_map/first/pallas_call | solution.py:49
  7.0 8.6 %collective-permute-start.2 = (f32[72,1024]{1,0:T(8,128)}, f32[72,1024]{1,0:T(8,128)S(1)}, u32[]{:S(2)}, u32[]{:S(2)}) collective-permute-start(f32[72,1024]{1,0:T(8,128)} %get-tuple-element.22.refs_1_.far_ref), channel_id=1, source_target_pairs={{1,2},{2,1},{3,4},{4,3},{5,6},{6,5},{7,8},{8,7},{9,10},{10,9},{11,... | collective-permute-start | bytes 884744 | tf_op jit(solution)/shard_map/ppermute | solution.py:505
  15.6 0.0 collective-permute-done.refs_2_.mate_ref.refs_1_
  15.6 0.6 copy-done.9
  16.2 7.3 %inner.2 = (f32[8,32,768]{2,1,0:T(8,128)}, f32[72,1024]{1,0:T(8,128)}, f32[16,128]{1,0:T(8,128)}, bf16[128,1024]{1,0:T(8,128)(2,1)}) custom-call(s32[1]{0:T(128)} %bitcast.place_ref, s32[8]{0:T(128)} %len_ref.9, bf16[8,32,1024]{2,1,0:T(8,128)(2,1)} %get-tuple-element.21.scaled_ref, s32[8,1024]{1,0:T(8,128)} %mult_ref.3, s32[8,256]{1,0:T(8,128)} %dof_ref.7, ...), custom_call_target="tpu_custom_call" | custom-call | flops 805306368 | bytes 12582912 | tf_op jit(solution)/shard_map/inner/pallas_call | solution.py:49
  23.5 0.0 copy-start.1
  23.5 0.0 copy-start.6
  23.5 0.0 copy-start.7
  23.5 0.1 collective-permute-start.1
  23.6 0.0 collective-permute-done.2.refs_0_.from_far_ref
  23.6 1.8 %collective-permute-done.1.arrived_ref.from_mate_ref = f32[72,1024]{1,0:T(8,128)S(1)} collective-permute-done((f32[72,1024]{1,0:T(8,128)}, f32[72,1024]{1,0:T(8,128)S(1)}, u32[]{:S(2)}, u32[]{:S(2)}) %collective-permute-start.1) | collective-permute-done | bytes 294944 | tf_op jit(solution)/shard_map/ppermute | solution.py:496
  25.4 0.0 copy-done.8
  25.4 0.7 copy-done.10
  26.1 0.7 copy-done.14
  26.8 1.1 dense.2
  27.9 18.1 %all_to_all.30.after_ref.parts_ref = f32[64,16,128]{2,1,0:T(8,128)S(1)} all-to-all(f32[64,16,128]{2,1,0:T(8,128)S(1)} %dense.2), channel_id=1, replica_groups=mesh['y'=4,'z'=4,'x'=4,'c'=2] {'y','z','x'}, dimensions={0} | all-to-all | bytes 1048576 | tf_op jit(solution)/shard_map/all_to_all | solution.py:509
  46.0 0.0 copy-done.12
  46.0 0.0 copy-done.13
  46.0 0.0 copy-done.16
  46.0 0.0 copy-start
  46.1 3.7 %head.2 = (f32[32,2048]{1,0:T(8,128)S(1)}, bf16[384,2048]{1,0:T(8,128)(2,1)S(1)}, f32[1,128]{1,0:T(1,128)S(1)}) custom-call(s32[1]{0:T(128)} %bitcast.place_ref, s32[8]{0:T(128)S(1)} %copy-done.13, f32[32,2048]{1,0:T(8,128)S(1)} %copy-done.7, f32[72,1024]{1,0:T(8,128)S(1)} %copy-done.15, f32[72,1024]{1,0:T(8,128)S(1)} %copy-done.6, ...), custom_call_target="tpu_custom_call" | custom-call | flops 805306368 | bytes 1048576 | tf_op jit(solution)/shard_map/head/pallas_call | solution.py:49
  49.8 0.1 sum.2
  49.9 17.3 %all_to_all.31.rhs_ref = f32[64,16,128]{2,1,0:T(8,128)S(1)} all-to-all(f32[64,16,128]{2,1,0:T(8,128)S(1)} %sum.2), channel_id=1, replica_groups=mesh['y'=4,'z'=4,'x'=4,'c'=2] {'y','z','x'}, dimensions={0} | all-to-all | bytes 1048576 | tf_op jit(solution)/shard_map/all_to_all | solution.py:509
  67.2 0.0 collective-permute-done.3.other_ref
  67.2 0.0 copy-done
  67.2 1.4 solve.2
  68.6 0.0 copy-done.2
  68.6 16.5 %all_to_all.32.mine_ref = f32[64,16,128]{2,1,0:T(8,128)S(1)} all-to-all(f32[64,16,128]{2,1,0:T(8,128)S(1)} %solve.2), channel_id=1, replica_groups=mesh['y'=4,'z'=4,'x'=4,'c'=2] {'y','z','x'}, dimensions={0} | all-to-all | bytes 1048576 | tf_op jit(solution)/shard_map/all_to_all | solution.py:509
  85.1 0.0 collective-permute-start.4
  85.1 1.9 %collective-permute-done.4.other_ref = f32[64,16,128]{2,1,0:T(8,128)S(1)} collective-permute-done((f32[64,16,128]{2,1,0:T(8,128)S(1)}, f32[64,16,128]{2,1,0:T(8,128)S(1)}, u32[]{:S(2)}, u32[]{:S(2)}) %collective-permute-start.4) | collective-permute-done | bytes 524320 | tf_op jit(solution)/shard_map/ppermute | solution.py:496
  87.1 5.8 %correct.2 = (f32[8,32,1024]{2,1,0:T(8,128)}, bf16[8,32,1024]{2,1,0:T(8,128)(2,1)S(1)}, f32[32,2048]{1,0:T(8,128)S(1)}, f32[40,1024]{1,0:T(8,128)S(1)}) custom-call(s32[1]{0:T(128)} %bitcast.place_ref, s32[8,16]{1,0:T(8,128)S(1)} %copy-done.8, s32[8,16]{1,0:T(8,128)S(1)} %copy-done.11, f32[1,128]{1,0:T(1,128)S(1)} %get-tuple-element.27.far_map_ref, ...), custom_call_target="tpu_custom_call" | custom-call | flops 1000000 | bytes 1048576 | tf_op jit(solution)/shard_map/correct/pallas_call | solution.py:49
  92.9 1.7 %collective-permute-start.6 = (f32[40,1024]{1,0:T(8,128)S(1)}, f32[40,1024]{1,0:T(8,128)S(1)}, u32[]{:S(2)}, u32[]{:S(2)}) collective-permute-start(f32[40,1024]{1,0:T(8,128)S(1)} %get-tuple-element.34.refs_0_.far_ref), channel_id=1, source_target_pairs={{1,2},{2,1},{3,4},{4,3},{5,6},{6,5},{7,8},{8,7},{9,10},{10,9},{11,... | collective-permute-start | bytes 491528 | tf_op jit(solution)/shard_map/ppermute | solution.py:505
  94.6 5.7 %inner.3 = (f32[8,32,768]{2,1,0:T(8,128)S(1)}, f32[40,1024]{1,0:T(8,128)S(1)}, f32[16,128]{1,0:T(8,128)S(1)}) custom-call(s32[1]{0:T(128)} %bitcast.place_ref, s32[8]{0:T(128)S(1)} %copy-done.13, bf16[8,32,1024]{2,1,0:T(8,128)(2,1)S(1)} %get-tuple-element.32.scaled_ref, s32[8,1024]{1,0:T(8,128)S(1)} %copy-done.5, s32[8,256]{1,0:T(8,128)S(1)} %copy-done.12, ...), custom_call_target="tpu_custom_call" | custom-call | flops 805306368 | bytes 12582912 | tf_op jit(solution)/shard_map/inner/pallas_call | solution.py:49
  100.3 0.1 collective-permute-start.5
  100.4 2.8 %collective-permute-done.6.refs_0_.from_far_ref = f32[40,1024]{1,0:T(8,128)S(1)} collective-permute-done((f32[40,1024]{1,0:T(8,128)S(1)}, f32[40,1024]{1,0:T(8,128)S(1)}, u32[]{:S(2)}, u32[]{:S(2)}) %collective-permute-start.6) | collective-permute-done | bytes 163872 | tf_op jit(solution)/shard_map/ppermute | solution.py:505
  103.1 0.0 collective-permute-done.5.arrived_ref.from_mate_ref
  103.1 1.1 dense.3
  104.3 20.3 %all_to_all.33.after_ref.parts_ref = f32[64,16,128]{2,1,0:T(8,128)S(1)} all-to-all(f32[64,16,128]{2,1,0:T(8,128)S(1)} %dense.3), channel_id=1, replica_groups=mesh['y'=4,'z'=4,'x'=4,'c'=2] {'y','z','x'}, dimensions={0} | all-to-all | bytes 1048576 | tf_op jit(solution)/shard_map/all_to_all | solution.py:509
  124.6 2.0 %head.3.refs_0_.head_ref = f32[32,2048]{1,0:T(8,128)S(1)} custom-call(s32[1]{0:T(128)} %bitcast.place_ref, s32[8]{0:T(128)S(1)} %copy-done.13, f32[32,2048]{1,0:T(8,128)S(1)} %get-tuple-element.33.edge_ref, f32[40,1024]{1,0:T(8,128)S(1)} %get-tuple-element.36.mate_ref, f32[40,1024]{1,0:T(8,128)S(1)} %get-tuple-element.34.refs_0_.far_ref, ...), custom_call_target="tpu_custom_call" | custom-call | flops 805306368 | bytes 1048576 | tf_op jit(solution)/shard_map/head/pallas_call | solution.py:49
  126.6 0.1 sum.3
  126.7 17.0 %all_to_all.34.rhs_ref = f32[64,16,128]{2,1,0:T(8,128)S(1)} all-to-all(f32[64,16,128]{2,1,0:T(8,128)S(1)} %sum.3), channel_id=1, replica_groups=mesh['y'=4,'z'=4,'x'=4,'c'=2] {'y','z','x'}, dimensions={0} | all-to-all | bytes 1048576 | tf_op jit(solution)/shard_map/all_to_all | solution.py:509
  143.7 1.4 solve.3
  145.1 16.5 %all_to_all.35.mine_ref = f32[64,16,128]{2,1,0:T(8,128)S(1)} all-to-all(f32[64,16,128]{2,1,0:T(8,128)S(1)} %solve.3), channel_id=1, replica_groups=mesh['y'=4,'z'=4,'x'=4,'c'=2] {'y','z','x'}, dimensions={0} | all-to-all | bytes 1048576 | tf_op jit(solution)/shard_map/all_to_all | solution.py:509
  161.6 0.0 collective-permute-start.7
  161.6 1.9 %collective-permute-done.7.other_ref = f32[64,16,128]{2,1,0:T(8,128)S(1)} collective-permute-done((f32[64,16,128]{2,1,0:T(8,128)S(1)}, f32[64,16,128]{2,1,0:T(8,128)S(1)}, u32[]{:S(2)}, u32[]{:S(2)}) %collective-permute-start.7) | collective-permute-done | bytes 524320 | tf_op jit(solution)/shard_map/ppermute | solution.py:496
  163.6 3.4 %correct.3 = f32[8,32,1024]{2,1,0:T(8,128)} custom-call(s32[1]{0:T(128)} %bitcast.place_ref, s32[8,16]{1,0:T(8,128)S(1)} %copy-done.8, s32[8,16]{1,0:T(8,128)S(1)} %copy-done.11, f32[1,128]{1,0:T(1,128)S(1)} %get-tuple-element.27.far_map_ref, f32[64,16,128]{2,1,0:T(8,128)S(1)} %all_to_all.35.mine_ref, f32[64,16,128]{2,1,0:T(8,128)S(1)} %collective-permute-done.7.other_ref, ...), custom_call_target="tpu_custom_call" | custom-call | flops 1000000 | bytes 1048576 | tf_op jit(solution)/shard_map/correct/pallas_call | solution.py:49
  (23 shorter events, 0.0 us)
Async XLA Ops:
  0.6 66.6 %collective-permute-start.3 = (f32[64,8192]{1,0:T(8,128)}, f32[64,8192]{1,0:T(8,128)S(1)}, u32[]{:S(2)}, u32[]{:S(2)}) collective-permute-start(f32[64,8192]{1,0:T(8,128)} %mine_ref.3), channel_id=1, source_target_pairs={{0,1},{1,0},{2,3},{3,2},{4,5},{5,4},{6,7},{7,6},{8,9},{9,8},{10,11... | collective-permute-start | bytes 6291464 | tf_op jit(solution)/shard_map/ppermute | solution.py:496
  0.7 14.9 %collective-permute-start = (s32[8,16]{1,0:T(8,128)}, s32[8,16]{1,0:T(8,128)S(1)}, u32[]{:S(2)}, u32[]{:S(2)}) collective-permute-start(s32[8,16]{1,0:T(8,128)} %own_ref.7), channel_id=1, source_target_pairs={{0,1},{1,0},{2,3},{3,2},{4,5},{5,4},{6,7},{7,6},{8,9},{9,8},{10,11... | collective-permute-start | bytes 1544 | tf_op jit(solution)/shard_map/ppermute | solution.py:496
  7.0 16.6 %collective-permute-start.2 = (f32[72,1024]{1,0:T(8,128)}, f32[72,1024]{1,0:T(8,128)S(1)}, u32[]{:S(2)}, u32[]{:S(2)}) collective-permute-start(f32[72,1024]{1,0:T(8,128)} %get-tuple-element.22.refs_1_.far_ref), channel_id=1, source_target_pairs={{1,2},{2,1},{3,4},{4,3},{5,6},{6,5},{7,8},{8,7},{9,10},{10,9},{11,... | collective-permute-start | bytes 884744 | tf_op jit(solution)/shard_map/ppermute | solution.py:505
  15.6 0.6 copy-start.9
  16.2 9.2 %copy-start.8 = (s32[8,16]{1,0:T(8,128)S(1)}, s32[8,16]{1,0:T(8,128)}, u32[]{:S(2)}) copy-start(s32[8,16]{1,0:T(8,128)} %own_ref.7) | copy-start | bytes 1540
  16.2 29.8 %copy-start.12 = (s32[8,256]{1,0:T(8,128)S(1)}, s32[8,256]{1,0:T(8,128)}, u32[]{:S(2)}) copy-start(s32[8,256]{1,0:T(8,128)} %dof_ref.7) | copy-start | bytes 24580
  16.2 29.8 %copy-start.13 = (s32[8]{0:T(128)S(1)}, s32[8]{0:T(128)}, u32[]{:S(2)}) copy-start(s32[8]{0:T(128)} %len_ref.9) | copy-start | bytes 100
  16.2 29.8 %copy-start.16 = (bf16[128,1024]{1,0:T(8,128)(2,1)S(1)}, bf16[128,1024]{1,0:T(8,128)(2,1)}, u32[]{:S(2)}) copy-start(bf16[128,1024]{1,0:T(8,128)(2,1)} %get-tuple-element.26.refs_2_) | copy-start | bytes 786436
  23.5 22.5 %copy-start.1 = (bf16[8,16,1024]{2,1,0:T(8,128)(2,1)S(1)}, bf16[8,16,1024]{2,1,0:T(8,128)(2,1)}, u32[]{:S(2)}) copy-start(bf16[8,16,1024]{2,1,0:T(8,128)(2,1)} %basis_ref.7) | copy-start | bytes 786436
  23.5 22.5 %copy-start.6 = (f32[72,1024]{1,0:T(8,128)S(1)}, f32[72,1024]{1,0:T(8,128)}, u32[]{:S(2)}) copy-start(f32[72,1024]{1,0:T(8,128)} %get-tuple-element.22.refs_1_.far_ref) | copy-start | bytes 884740
  23.5 22.5 %copy-start.7 = (f32[32,2048]{1,0:T(8,128)S(1)}, f32[32,2048]{1,0:T(8,128)}, u32[]{:S(2)}) copy-start(f32[32,2048]{1,0:T(8,128)} %get-tuple-element.20.edge_ref) | copy-start | bytes 786436
  23.5 1.9 %collective-permute-start.1 = (f32[72,1024]{1,0:T(8,128)}, f32[72,1024]{1,0:T(8,128)S(1)}, u32[]{:S(2)}, u32[]{:S(2)}) collective-permute-start(f32[72,1024]{1,0:T(8,128)} %get-tuple-element.23.mate_ref), channel_id=1, source_target_pairs={{0,1},{1,0},{2,3},{3,2},{4,5},{5,4},{6,7},{7,6},{8,9},{9,8},{10,11... | collective-permute-start | bytes 884744 | tf_op jit(solution)/shard_map/ppermute | solution.py:496
  25.4 0.7 copy-start.10
  26.1 0.7 copy-start.14
  26.8 19.3 %copy-start.15 = (f32[72,1024]{1,0:T(8,128)S(1)}, f32[72,1024]{1,0:T(8,128)}, u32[]{:S(2)}) copy-start(f32[72,1024]{1,0:T(8,128)} %get-tuple-element.23.mate_ref) | copy-start | bytes 884740
  26.8 19.3 %copy-start.17 = (bf16[128,1024]{1,0:T(8,128)(2,1)S(1)}, bf16[128,1024]{1,0:T(8,128)(2,1)}, u32[]{:S(2)}) copy-start(bf16[128,1024]{1,0:T(8,128)(2,1)} %get-tuple-element.25.refs_1_) | copy-start | bytes 786436
  46.0 21.1 %copy-start = (f32[64,8192]{1,0:T(8,128)S(1)}, f32[64,8192]{1,0:T(8,128)}, u32[]{:S(2)}) copy-start(f32[64,8192]{1,0:T(8,128)} %mine_ref.3) | copy-start | bytes 6291460
  49.8 18.8 %copy-start.2 = (bf16[384,2048]{1,0:T(8,128)(2,1)}, bf16[384,2048]{1,0:T(8,128)(2,1)S(1)}, u32[]{:S(2)}) copy-start(bf16[384,2048]{1,0:T(8,128)(2,1)S(1)} %get-tuple-element.29.shared_ref) | copy-start | bytes 4718596
  67.2 19.9 %copy-start.4 = (f32[8,32,768]{2,1,0:T(8,128)S(1)}, f32[8,32,768]{2,1,0:T(8,128)}, u32[]{:S(2)}) copy-start(f32[8,32,768]{2,1,0:T(8,128)} %get-tuple-element.30.inner_ref) | copy-start | bytes 2359300
  67.2 19.9 %copy-start.5 = (s32[8,1024]{1,0:T(8,128)S(1)}, s32[8,1024]{1,0:T(8,128)}, u32[]{:S(2)}) copy-start(s32[8,1024]{1,0:T(8,128)} %mult_ref.3) | copy-start | bytes 98308
  67.2 19.9 %copy-start.11 = (s32[8,16]{1,0:T(8,128)S(1)}, s32[8,16]{1,0:T(8,128)}, u32[]{:S(2)}) copy-start(s32[8,16]{1,0:T(8,128)} %copy-done.9) | copy-start | bytes 1540
  85.1 1.9 %collective-permute-start.4 = (f32[64,16,128]{2,1,0:T(8,128)S(1)}, f32[64,16,128]{2,1,0:T(8,128)S(1)}, u32[]{:S(2)}, u32[]{:S(2)}) collective-permute-start(f32[64,16,128]{2,1,0:T(8,128)S(1)} %all_to_all.32.mine_ref), channel_id=1, source_target_pairs={{0,1},{1,0},{2,3},{3,2},{4,5},{5,4},{6,7},{7,6},{8,9},{9,8},{10,11... | collective-permute-start | bytes 1572872 | tf_op jit(solution)/shard_map/ppermute | solution.py:496
  92.9 10.3 %collective-permute-start.6 = (f32[40,1024]{1,0:T(8,128)S(1)}, f32[40,1024]{1,0:T(8,128)S(1)}, u32[]{:S(2)}, u32[]{:S(2)}) collective-permute-start(f32[40,1024]{1,0:T(8,128)S(1)} %get-tuple-element.34.refs_0_.far_ref), channel_id=1, source_target_pairs={{1,2},{2,1},{3,4},{4,3},{5,6},{6,5},{7,8},{8,7},{9,10},{10,9},{11,... | collective-permute-start | bytes 491528 | tf_op jit(solution)/shard_map/ppermute | solution.py:505
  100.3 2.9 %collective-permute-start.5 = (f32[40,1024]{1,0:T(8,128)S(1)}, f32[40,1024]{1,0:T(8,128)S(1)}, u32[]{:S(2)}, u32[]{:S(2)}) collective-permute-start(f32[40,1024]{1,0:T(8,128)S(1)} %get-tuple-element.36.mate_ref), channel_id=1, source_target_pairs={{0,1},{1,0},{2,3},{3,2},{4,5},{5,4},{6,7},{7,6},{8,9},{9,8},{10,11... | collective-permute-start | bytes 491528 | tf_op jit(solution)/shard_map/ppermute | solution.py:496
  143.7 19.8 %copy-start.3 = (bf16[384,2048]{1,0:T(8,128)(2,1)S(1)}, bf16[384,2048]{1,0:T(8,128)(2,1)}, u32[]{:S(2)}) copy-start(bf16[384,2048]{1,0:T(8,128)(2,1)} %copy-done.2) | copy-start | bytes 4718596
  161.6 1.9 %collective-permute-start.7 = (f32[64,16,128]{2,1,0:T(8,128)S(1)}, f32[64,16,128]{2,1,0:T(8,128)S(1)}, u32[]{:S(2)}, u32[]{:S(2)}) collective-permute-start(f32[64,16,128]{2,1,0:T(8,128)S(1)} %all_to_all.35.mine_ref), channel_id=1, source_target_pairs={{0,1},{1,0},{2,3},{3,2},{4,5},{5,4},{6,7},{7,6},{8,9},{9,8},{10,11... | collective-permute-start | bytes 1572872 | tf_op jit(solution)/shard_map/ppermute | solution.py:496

commit v6 on v5

--- a/solution.py
+++ b/solution.py
@@ -1,3 +1,5 @@
+import functools
+
 import jax
 import jax.numpy as jnp
 from jax import lax
@@ -115,13 +117,14 @@
     return rows.astype(jnp.float32).T
 
 
-def dense_kernel(own_ref, mate_ref, keep_ref, arrived_ref, *refs):
+def dense_kernel(row, own_ref, near_ref, keep_ref, arrived_ref, *refs):
     out_ref = refs[-1]
     cases, width = keep_ref.shape
     got = arrived_ref[arrived_ref.shape[0] - cases // 2 :, : 2 * width]
     got = jnp.concatenate([got[:, :width], got[:, width:]], axis=0)
     value = halves(jnp.concatenate([keep_ref[...], got], axis=1))
-    maps = jnp.concatenate([flat_map(own_ref), flat_map(mate_ref)], axis=1)
+    mate = near_ref[row : row + 1, :width]
+    maps = jnp.concatenate([flat_map(own_ref), mate], axis=1)
     maps = columns_of(maps)[:, :1]
     wide = 2 * out_ref.shape[2]
     for pair in range(out_ref.shape[0] // 2):
@@ -326,11 +329,11 @@
     copies = column_copies(
         inverse_ref, buffer_ref, sems, inverse_ref.shape[2] - buffer_ref.shape[2]
     )
-    if len(inputs) == 7:
-        map_ref, after_ref, _, inner_ref, mate_ref, keep_ref, own_ref = inputs
+    if len(inputs) == 6:
+        map_ref, after_ref, inner_ref, mate_ref, keep_ref, own_ref = inputs
         more = (basis_ref, map_ref, own_ref)
     else:
-        after_ref, _, inner_ref, mate_ref, keep_ref = inputs
+        after_ref, inner_ref, mate_ref, keep_ref = inputs
         more = (None, None, None)
 
     @pl.when(started(place_ref))
@@ -387,7 +390,9 @@
                     jnp.bfloat16
                 )
         near, far = near_ref[...], wide_ref[...]
-        map_ref[...] = from_far_ref[cases + coarse + 8 : cases + coarse + 9, :entries]
+        row = cases + coarse + 8
+        map_ref[0:1] = from_mate_ref[row : row + 1, :entries]
+        map_ref[1:2] = from_far_ref[row : row + 1, :entries]
     for sub in range(subs):
         columns = slice(sub * width, (sub + 1) * width)
         hot = slots_of(place_ref, len_ref, dof_ref, sub, 2 * owned)
@@ -409,8 +414,7 @@
 def correct_kernel(
     place_ref,
     own_ref,
-    mate_ref,
-    far_map_ref,
+    near_ref,
     mine_ref,
     other_ref,
     basis_ref,
@@ -438,7 +442,7 @@
         copies = column_copies(inverse_hbm, columns_ref, sems, 0)
     subs, cases, _ = values_ref.shape
     chips, half, _ = mine_ref.shape
-    entries = far_map_ref.shape[1]
+    entries = near_ref.shape[1]
     width = head_ref.shape[1] // subs
     leave = [
         pltpu.make_async_copy(values_ref.at[sub], out_hbm.at[sub], leave_sems.at[sub])
@@ -448,7 +452,7 @@
     @pl.when(started(place_ref))
     def _():
         widen(basis_ref, wide_ref)
-        maps = jnp.concatenate([flat_map(own_ref), flat_map(mate_ref), far_map_ref[...]], axis=1)
+        maps = jnp.concatenate([flat_map(own_ref), near_ref[0:1], near_ref[1:2]], axis=1)
         looked = jnp.zeros((4 * half, 3 * entries), jnp.float32)
         for pair in range(chips // 2):
             mine = jnp.concatenate([mine_ref[2 * pair], mine_ref[2 * pair + 1]], axis=1)
@@ -541,17 +545,16 @@
             pltpu.SemaphoreType.DMA((subs,)),
         ]
 
-    mate_map = swap(coarse_map)
     other_rows = swap(coarse_inverse)
     wide = pltpu.VMEM((subs, entries, length), jnp.bfloat16)
     opened = (bf16(subs, cases, length), f32(cases, spots))
 
-    def dense(keep, arrived, *after):
+    def dense(row, near, keep, arrived, *after):
         parts = call(
-            dense_kernel,
+            functools.partial(dense_kernel, row),
             "dense",
             blocks,
-            (coarse_map, mate_map, keep, arrived, *after),
+            (coarse_map, near, keep, arrived, *after),
             [VMEM] * 4 + [ANY] * len(after),
         )
         return by_chip(parts)
@@ -576,9 +579,8 @@
                 local_inverse,
                 *more,
                 far,
-                mate_map,
             ),
-            [SMEM] * 2 + [VMEM] * 5 + [HBM] + [VMEM] * len(more) + [ANY] * 2,
+            [SMEM] * 2 + [VMEM] * 5 + [HBM] + [VMEM] * len(more) + [ANY],
             flops=2 * scaled.size * (length - width) + slot_flops // 2,
             moved=inverse_bytes * 3 // 4,
             mib=60 if more else 50,
@@ -602,7 +604,7 @@
     def assemble(edge, mate, far, from_mate, from_far, after, *more):
         outs, scratch = [f32(cases, spots)], []
         if more:
-            outs += [bf16(3 * entries, spots), f32(1, entries)]
+            outs += [bf16(3 * entries, spots), f32(2, entries)]
             scratch = [pltpu.VMEM((3 * cases + 2 * entries, owned), jnp.bfloat16)] * 2
         return call(
             head_kernel,
@@ -628,8 +630,7 @@
             (
                 place,
                 coarse_map,
-                mate_map,
-                far_map,
+                near_maps,
                 mine,
                 swap(mine),
                 coarse_basis,
@@ -638,7 +639,7 @@
                 inner,
                 *more,
             ),
-            [SMEM] + [VMEM] * 9 + specs,
+            [SMEM] + [VMEM] * 8 + specs,
             mib=50 if more else 16,
             out_specs=tuple(out_specs),
             scratch_shapes=[
@@ -679,8 +680,8 @@
     from_far = far_swap(far)
     inner, mate, keep, own_mate = inner_solve(scaled, edge, far, coarse_map)
     from_mate = swap(mate)
-    parts = dense(keep, from_mate, from_far)
-    head, shared, far_map = assemble(
+    parts = dense(cases + coarse + 8, from_mate, keep, from_mate, from_far)
+    head, shared, near_maps = assemble(
         edge, mate, far, from_mate, from_far, parts, coarse_basis, own_mate, own_far
     )
     mine = coarse_solve(parts, (head,))
@@ -691,7 +692,7 @@
     from_far = far_swap(far)
     inner, mate, keep = inner_solve(scaled, edge, far)
     from_mate = swap(mate)
-    parts = dense(keep, from_mate, from_far)
+    parts = dense(0, near_maps, keep, from_mate, from_far)
     (head,) = assemble(edge, mate, far, from_mate, from_far, parts)
     mine = coarse_solve(parts, (head,))
     (second_apply,) = correct(mine, head, shared, inner)

time: 169 us -> 168 us (level)
    ppermute x6 -> x5, waiting for transfers between devices: 5.59 us -> 5.59 us  [swap(): return lax.ppermute(value, 'c', [(0, 1), (1, 0)])]
  transfers between devices with their start and end apart: 8 -> 7, of which waited for: 4 -> 4; matrix products, arithmetic and copies ran while one was open for 0% -> 0% of each run, Pallas kernels for 14% -> 14%
where the time goes in v6:
time: 168 us; the launch traced here: 167 us
  blocking collectives  107 us (64%)
  Pallas kernels  39 us (23%)
  starting transfers between devices  10.9 us (6%)
  waiting for transfers between devices  8.35 us (5%)
    all_to_all x6, blocking collectives, by_chip(): return lax.all_to_all(value, CHIPS, 0, 0, tiled=True)  107 us
    pallas_call x13, Pallas kernels, call(): pl.pallas_call(kernel, out_shape=out_shape, in_specs=specs, compiler_para...  39 us
    ppermute x2, starting transfers between devices, far_swap(): return lax.ppermute(value, DOM, pairs)  10.6 us
    ppermute x5, waiting for transfers between devices, swap(): return lax.ppermute(value, 'c', [(0, 1), (1, 0)])  5.59 us
  transfers between devices with their start and end apart: 7, of which 4 were waited for; matrix products, arithmetic and copies ran while one was open for 0% of the time, Pallas kernels for 14%

profile of v6, /device:TPU:0, one launch (start us, length us, event | category | flops | bytes accessed | tf_op | source)
XLA Modules:
  0.0 167.0 jit_solution(7194519236694351242)
XLA Ops:
  0.6 0.1 collective-permute-start.2
  0.7 5.8 %first.1 = (bf16[8,32,1024]{2,1,0:T(8,128)(2,1)}, f32[32,2048]{1,0:T(8,128)}, f32[72,1024]{1,0:T(8,128)}, bf16[128,1024]{1,0:T(8,128)(2,1)}) custom-call(s32[1]{0:T(128)} %bitcast.place_ref, s32[8]{0:T(128)} %len_ref.9, bf16[8,32,1024]{2,1,0:T(8,128)(2,1)} %values_hbm.1, s32[8,1024]{1,0:T(8,128)} %mult_ref.3, s32[8,256]{1,0:T(8,128)} %dof_ref.7, ...), custom_call_target="tpu_custom_call" | custom-call | flops 1000000 | bytes 1048576 | tf_op jit(solution)/shard_map/first/pallas_call | solution.py:51
  6.6 8.9 %collective-permute-start.1 = (f32[72,1024]{1,0:T(8,128)}, f32[72,1024]{1,0:T(8,128)S(1)}, u32[]{:S(2)}, u32[]{:S(2)}) collective-permute-start(f32[72,1024]{1,0:T(8,128)} %get-tuple-element.22.refs_1_.far_ref), channel_id=1, source_target_pairs={{1,2},{2,1},{3,4},{4,3},{5,6},{6,5},{7,8},{8,7},{9,10},{10,9},{11,... | collective-permute-start | bytes 884744 | tf_op jit(solution)/shard_map/ppermute | solution.py:509
  15.5 7.3 %inner.2 = (f32[8,32,768]{2,1,0:T(8,128)}, f32[72,1024]{1,0:T(8,128)}, f32[16,128]{1,0:T(8,128)}, bf16[128,1024]{1,0:T(8,128)(2,1)}) custom-call(s32[1]{0:T(128)} %bitcast.place_ref, s32[8]{0:T(128)} %len_ref.9, bf16[8,32,1024]{2,1,0:T(8,128)(2,1)} %get-tuple-element.21.scaled_ref, s32[8,1024]{1,0:T(8,128)} %mult_ref.3, s32[8,256]{1,0:T(8,128)} %dof_ref.7, ...), custom_call_target="tpu_custom_call" | custom-call | flops 805306368 | bytes 12582912 | tf_op jit(solution)/shard_map/inner/pallas_call | solution.py:51
  22.8 0.0 copy-start.1
  22.8 0.0 copy-start.6
  22.8 0.0 copy-start.7
  22.8 0.0 copy-start.9
  22.8 0.0 copy-start.10
  22.8 0.1 collective-permute-start
  22.9 0.0 collective-permute-done.1.refs_0_.from_far_ref
  22.9 1.8 %collective-permute-done.near_ref.arrived_ref.from_mate_ref = f32[72,1024]{1,0:T(8,128)S(1)} collective-permute-done((f32[72,1024]{1,0:T(8,128)}, f32[72,1024]{1,0:T(8,128)S(1)}, u32[]{:S(2)}, u32[]{:S(2)}) %collective-permute-start) | collective-permute-done | bytes 294944 | tf_op jit(solution)/shard_map/ppermute | solution.py:500
  24.7 0.0 copy-done.8
  24.7 0.7 copy-done.11
  25.4 1.1 dense.2
  26.5 18.5 %all_to_all.30.after_ref.parts_ref = f32[64,16,128]{2,1,0:T(8,128)S(1)} all-to-all(f32[64,16,128]{2,1,0:T(8,128)S(1)} %dense.2), channel_id=1, replica_groups=mesh['y'=4,'z'=4,'x'=4,'c'=2] {'y','z','x'}, dimensions={0} | all-to-all | bytes 1048576 | tf_op jit(solution)/shard_map/all_to_all | solution.py:513
  45.0 0.0 copy-done.13
  45.0 0.0 copy-done.1
  45.0 0.0 copy-done.6
  45.0 0.0 copy-done.7
  45.0 0.0 copy-done.9
  45.1 0.0 copy-start
  45.1 3.7 %head.2 = (f32[32,2048]{1,0:T(8,128)S(1)}, bf16[384,2048]{1,0:T(8,128)(2,1)S(1)}, f32[2,128]{1,0:T(2,128)S(1)}) custom-call(s32[1]{0:T(128)} %bitcast.place_ref, s32[8]{0:T(128)S(1)} %copy-done.10, f32[32,2048]{1,0:T(8,128)S(1)} %copy-done.7, f32[72,1024]{1,0:T(8,128)S(1)} %copy-done.12, f32[72,1024]{1,0:T(8,128)S(1)} %copy-done.6, ...), custom_call_target="tpu_custom_call" | custom-call | flops 805306368 | bytes 1048576 | tf_op jit(solution)/shard_map/head/pallas_call | solution.py:51
  48.8 0.0 copy-start.2
  48.8 0.1 sum.2
  48.9 18.0 %all_to_all.31.rhs_ref = f32[64,16,128]{2,1,0:T(8,128)S(1)} all-to-all(f32[64,16,128]{2,1,0:T(8,128)S(1)} %sum.2), channel_id=1, replica_groups=mesh['y'=4,'z'=4,'x'=4,'c'=2] {'y','z','x'}, dimensions={0} | all-to-all | bytes 1048576 | tf_op jit(solution)/shard_map/all_to_all | solution.py:513
  66.9 0.0 collective-permute-done.2.other_ref
  66.9 1.4 solve.2
  68.4 16.8 %all_to_all.32.mine_ref = f32[64,16,128]{2,1,0:T(8,128)S(1)} all-to-all(f32[64,16,128]{2,1,0:T(8,128)S(1)} %solve.2), channel_id=1, replica_groups=mesh['y'=4,'z'=4,'x'=4,'c'=2] {'y','z','x'}, dimensions={0} | all-to-all | bytes 1048576 | tf_op jit(solution)/shard_map/all_to_all | solution.py:513
  85.1 0.0 collective-permute-start.3
  85.1 1.9 %collective-permute-done.3.other_ref = f32[64,16,128]{2,1,0:T(8,128)S(1)} collective-permute-done((f32[64,16,128]{2,1,0:T(8,128)S(1)}, f32[64,16,128]{2,1,0:T(8,128)S(1)}, u32[]{:S(2)}, u32[]{:S(2)}) %collective-permute-start.3) | collective-permute-done | bytes 524320 | tf_op jit(solution)/shard_map/ppermute | solution.py:500
  87.0 0.0 copy-done.5
  87.0 5.8 %correct.2 = (f32[8,32,1024]{2,1,0:T(8,128)}, bf16[8,32,1024]{2,1,0:T(8,128)(2,1)S(1)}, f32[32,2048]{1,0:T(8,128)S(1)}, f32[40,1024]{1,0:T(8,128)S(1)}) custom-call(s32[1]{0:T(128)} %bitcast.place_ref, s32[8,16]{1,0:T(8,128)S(1)} %copy-done.8, f32[2,128]{1,0:T(2,128)S(1)} %get-tuple-element.27.near_ref, f32[64,16,128]{2,1,0:T(8,128)S(1)} %all_to_all.32.mine_ref, ...), custom_call_target="tpu_custom_call" | custom-call | flops 1000000 | bytes 1048576 | tf_op jit(solution)/shard_map/correct/pallas_call | solution.py:51
  92.8 1.7 %collective-permute-start.5 = (f32[40,1024]{1,0:T(8,128)S(1)}, f32[40,1024]{1,0:T(8,128)S(1)}, u32[]{:S(2)}, u32[]{:S(2)}) collective-permute-start(f32[40,1024]{1,0:T(8,128)S(1)} %get-tuple-element.34.refs_0_.far_ref), channel_id=1, source_target_pairs={{1,2},{2,1},{3,4},{4,3},{5,6},{6,5},{7,8},{8,7},{9,10},{10,9},{11,... | collective-permute-start | bytes 491528 | tf_op jit(solution)/shard_map/ppermute | solution.py:509
  94.5 5.7 %inner.3 = (f32[8,32,768]{2,1,0:T(8,128)S(1)}, f32[40,1024]{1,0:T(8,128)S(1)}, f32[16,128]{1,0:T(8,128)S(1)}) custom-call(s32[1]{0:T(128)} %bitcast.place_ref, s32[8]{0:T(128)S(1)} %copy-done.10, bf16[8,32,1024]{2,1,0:T(8,128)(2,1)S(1)} %get-tuple-element.32.scaled_ref, s32[8,1024]{1,0:T(8,128)S(1)} %copy-done.5, s32[8,256]{1,0:T(8,128)S(1)} %copy-done.9, ...), custom_call_target="tpu_custom_call" | custom-call | flops 805306368 | bytes 12582912 | tf_op jit(solution)/shard_map/inner/pallas_call | solution.py:51
  100.2 0.1 collective-permute-start.4
  100.3 2.8 %collective-permute-done.5.refs_0_.from_far_ref = f32[40,1024]{1,0:T(8,128)S(1)} collective-permute-done((f32[40,1024]{1,0:T(8,128)S(1)}, f32[40,1024]{1,0:T(8,128)S(1)}, u32[]{:S(2)}, u32[]{:S(2)}) %collective-permute-start.5) | collective-permute-done | bytes 163872 | tf_op jit(solution)/shard_map/ppermute | solution.py:509
  103.1 0.0 collective-permute-done.4.arrived_ref.from_mate_ref
  103.1 1.1 dense.3
  104.2 20.3 %all_to_all.33.after_ref.parts_ref = f32[64,16,128]{2,1,0:T(8,128)S(1)} all-to-all(f32[64,16,128]{2,1,0:T(8,128)S(1)} %dense.3), channel_id=1, replica_groups=mesh['y'=4,'z'=4,'x'=4,'c'=2] {'y','z','x'}, dimensions={0} | all-to-all | bytes 1048576 | tf_op jit(solution)/shard_map/all_to_all | solution.py:513
  124.5 2.0 %head.3.refs_0_.head_ref = f32[32,2048]{1,0:T(8,128)S(1)} custom-call(s32[1]{0:T(128)} %bitcast.place_ref, s32[8]{0:T(128)S(1)} %copy-done.10, f32[32,2048]{1,0:T(8,128)S(1)} %get-tuple-element.33.edge_ref, f32[40,1024]{1,0:T(8,128)S(1)} %get-tuple-element.36.mate_ref, f32[40,1024]{1,0:T(8,128)S(1)} %get-tuple-element.34.refs_0_.far_ref, ...), custom_call_target="tpu_custom_call" | custom-call | flops 805306368 | bytes 1048576 | tf_op jit(solution)/shard_map/head/pallas_call | solution.py:51
  126.5 0.1 sum.3
  126.6 17.0 %all_to_all.34.rhs_ref = f32[64,16,128]{2,1,0:T(8,128)S(1)} all-to-all(f32[64,16,128]{2,1,0:T(8,128)S(1)} %sum.3), channel_id=1, replica_groups=mesh['y'=4,'z'=4,'x'=4,'c'=2] {'y','z','x'}, dimensions={0} | all-to-all | bytes 1048576 | tf_op jit(solution)/shard_map/all_to_all | solution.py:513
  143.6 1.4 solve.3
  145.0 16.5 %all_to_all.35.mine_ref = f32[64,16,128]{2,1,0:T(8,128)S(1)} all-to-all(f32[64,16,128]{2,1,0:T(8,128)S(1)} %solve.3), channel_id=1, replica_groups=mesh['y'=4,'z'=4,'x'=4,'c'=2] {'y','z','x'}, dimensions={0} | all-to-all | bytes 1048576 | tf_op jit(solution)/shard_map/all_to_all | solution.py:513
  161.5 0.0 collective-permute-start.6
  161.5 1.9 %collective-permute-done.6.other_ref = f32[64,16,128]{2,1,0:T(8,128)S(1)} collective-permute-done((f32[64,16,128]{2,1,0:T(8,128)S(1)}, f32[64,16,128]{2,1,0:T(8,128)S(1)}, u32[]{:S(2)}, u32[]{:S(2)}) %collective-permute-start.6) | collective-permute-done | bytes 524320 | tf_op jit(solution)/shard_map/ppermute | solution.py:500
  163.4 3.4 %correct.3 = f32[8,32,1024]{2,1,0:T(8,128)} custom-call(s32[1]{0:T(128)} %bitcast.place_ref, s32[8,16]{1,0:T(8,128)S(1)} %copy-done.8, f32[2,128]{1,0:T(2,128)S(1)} %get-tuple-element.27.near_ref, f32[64,16,128]{2,1,0:T(8,128)S(1)} %all_to_all.35.mine_ref, f32[64,16,128]{2,1,0:T(8,128)S(1)} %collective-permute-done.6.other_ref, ...), custom_call_target="tpu_custom_call" | custom-call | flops 1000000 | bytes 1048576 | tf_op jit(solution)/shard_map/correct/pallas_call | solution.py:51
  (15 shorter events, 0.0 us)
Async XLA Ops:
  0.6 66.3 %collective-permute-start.2 = (f32[64,8192]{1,0:T(8,128)}, f32[64,8192]{1,0:T(8,128)S(1)}, u32[]{:S(2)}, u32[]{:S(2)}) collective-permute-start(f32[64,8192]{1,0:T(8,128)} %mine_ref.3), channel_id=1, source_target_pairs={{0,1},{1,0},{2,3},{3,2},{4,5},{5,4},{6,7},{7,6},{8,9},{9,8},{10,11... | collective-permute-start | bytes 6291464 | tf_op jit(solution)/shard_map/ppermute | solution.py:500
  6.6 16.4 %collective-permute-start.1 = (f32[72,1024]{1,0:T(8,128)}, f32[72,1024]{1,0:T(8,128)S(1)}, u32[]{:S(2)}, u32[]{:S(2)}) collective-permute-start(f32[72,1024]{1,0:T(8,128)} %get-tuple-element.22.refs_1_.far_ref), channel_id=1, source_target_pairs={{1,2},{2,1},{3,4},{4,3},{5,6},{6,5},{7,8},{8,7},{9,10},{10,9},{11,... | collective-permute-start | bytes 884744 | tf_op jit(solution)/shard_map/ppermute | solution.py:509
  15.5 9.2 %copy-start.8 = (s32[8,16]{1,0:T(8,128)S(1)}, s32[8,16]{1,0:T(8,128)}, u32[]{:S(2)}) copy-start(s32[8,16]{1,0:T(8,128)} %own_ref.7) | copy-start | bytes 1540
  15.5 29.5 %copy-start.13 = (bf16[128,1024]{1,0:T(8,128)(2,1)S(1)}, bf16[128,1024]{1,0:T(8,128)(2,1)}, u32[]{:S(2)}) copy-start(bf16[128,1024]{1,0:T(8,128)(2,1)} %get-tuple-element.26.refs_2_) | copy-start | bytes 786436
  22.8 22.2 %copy-start.1 = (bf16[8,16,1024]{2,1,0:T(8,128)(2,1)S(1)}, bf16[8,16,1024]{2,1,0:T(8,128)(2,1)}, u32[]{:S(2)}) copy-start(bf16[8,16,1024]{2,1,0:T(8,128)(2,1)} %basis_ref.7) | copy-start | bytes 786436
  22.8 22.2 %copy-start.6 = (f32[72,1024]{1,0:T(8,128)S(1)}, f32[72,1024]{1,0:T(8,128)}, u32[]{:S(2)}) copy-start(f32[72,1024]{1,0:T(8,128)} %get-tuple-element.22.refs_1_.far_ref) | copy-start | bytes 884740
  22.8 22.2 %copy-start.7 = (f32[32,2048]{1,0:T(8,128)S(1)}, f32[32,2048]{1,0:T(8,128)}, u32[]{:S(2)}) copy-start(f32[32,2048]{1,0:T(8,128)} %get-tuple-element.20.edge_ref) | copy-start | bytes 786436
  22.8 22.2 %copy-start.9 = (s32[8,256]{1,0:T(8,128)S(1)}, s32[8,256]{1,0:T(8,128)}, u32[]{:S(2)}) copy-start(s32[8,256]{1,0:T(8,128)} %dof_ref.7) | copy-start | bytes 24580
  22.8 22.2 %copy-start.10 = (s32[8]{0:T(128)S(1)}, s32[8]{0:T(128)}, u32[]{:S(2)}) copy-start(s32[8]{0:T(128)} %len_ref.9) | copy-start | bytes 100
  22.8 1.9 %collective-permute-start = (f32[72,1024]{1,0:T(8,128)}, f32[72,1024]{1,0:T(8,128)S(1)}, u32[]{:S(2)}, u32[]{:S(2)}) collective-permute-start(f32[72,1024]{1,0:T(8,128)} %get-tuple-element.23.mate_ref), channel_id=1, source_target_pairs={{0,1},{1,0},{2,3},{3,2},{4,5},{5,4},{6,7},{7,6},{8,9},{9,8},{10,11... | collective-permute-start | bytes 884744 | tf_op jit(solution)/shard_map/ppermute | solution.py:500
  24.7 0.7 copy-start.11
  25.4 19.6 %copy-start.12 = (f32[72,1024]{1,0:T(8,128)S(1)}, f32[72,1024]{1,0:T(8,128)}, u32[]{:S(2)}) copy-start(f32[72,1024]{1,0:T(8,128)} %get-tuple-element.23.mate_ref) | copy-start | bytes 884740
  25.4 19.7 %copy-start.14 = (bf16[128,1024]{1,0:T(8,128)(2,1)S(1)}, bf16[128,1024]{1,0:T(8,128)(2,1)}, u32[]{:S(2)}) copy-start(bf16[128,1024]{1,0:T(8,128)(2,1)} %get-tuple-element.25.refs_1_) | copy-start | bytes 786436
  45.1 21.8 %copy-start = (f32[64,8192]{1,0:T(8,128)S(1)}, f32[64,8192]{1,0:T(8,128)}, u32[]{:S(2)}) copy-start(f32[64,8192]{1,0:T(8,128)} %mine_ref.3) | copy-start | bytes 6291460
  48.8 19.5 %copy-start.2 = (bf16[384,2048]{1,0:T(8,128)(2,1)}, bf16[384,2048]{1,0:T(8,128)(2,1)S(1)}, u32[]{:S(2)}) copy-start(bf16[384,2048]{1,0:T(8,128)(2,1)S(1)} %get-tuple-element.29.shared_ref) | copy-start | bytes 4718596
  66.9 20.1 %copy-start.4 = (f32[8,32,768]{2,1,0:T(8,128)S(1)}, f32[8,32,768]{2,1,0:T(8,128)}, u32[]{:S(2)}) copy-start(f32[8,32,768]{2,1,0:T(8,128)} %get-tuple-element.30.inner_ref) | copy-start | bytes 2359300
  66.9 20.1 %copy-start.5 = (s32[8,1024]{1,0:T(8,128)S(1)}, s32[8,1024]{1,0:T(8,128)}, u32[]{:S(2)}) copy-start(s32[8,1024]{1,0:T(8,128)} %mult_ref.3) | copy-start | bytes 98308
  85.1 1.9 %collective-permute-start.3 = (f32[64,16,128]{2,1,0:T(8,128)S(1)}, f32[64,16,128]{2,1,0:T(8,128)S(1)}, u32[]{:S(2)}, u32[]{:S(2)}) collective-permute-start(f32[64,16,128]{2,1,0:T(8,128)S(1)} %all_to_all.32.mine_ref), channel_id=1, source_target_pairs={{0,1},{1,0},{2,3},{3,2},{4,5},{5,4},{6,7},{7,6},{8,9},{9,8},{10,11... | collective-permute-start | bytes 1572872 | tf_op jit(solution)/shard_map/ppermute | solution.py:500
  92.8 10.3 %collective-permute-start.5 = (f32[40,1024]{1,0:T(8,128)S(1)}, f32[40,1024]{1,0:T(8,128)S(1)}, u32[]{:S(2)}, u32[]{:S(2)}) collective-permute-start(f32[40,1024]{1,0:T(8,128)S(1)} %get-tuple-element.34.refs_0_.far_ref), channel_id=1, source_target_pairs={{1,2},{2,1},{3,4},{4,3},{5,6},{6,5},{7,8},{8,7},{9,10},{10,9},{11,... | collective-permute-start | bytes 491528 | tf_op jit(solution)/shard_map/ppermute | solution.py:509
  100.2 2.9 %collective-permute-start.4 = (f32[40,1024]{1,0:T(8,128)S(1)}, f32[40,1024]{1,0:T(8,128)S(1)}, u32[]{:S(2)}, u32[]{:S(2)}) collective-permute-start(f32[40,1024]{1,0:T(8,128)S(1)} %get-tuple-element.36.mate_ref), channel_id=1, source_target_pairs={{0,1},{1,0},{2,3},{3,2},{4,5},{5,4},{6,7},{7,6},{8,9},{9,8},{10,11... | collective-permute-start | bytes 491528 | tf_op jit(solution)/shard_map/ppermute | solution.py:500
  143.6 19.8 %copy-start.3 = (bf16[384,2048]{1,0:T(8,128)(2,1)S(1)}, bf16[384,2048]{1,0:T(8,128)(2,1)}, u32[]{:S(2)}) copy-start(bf16[384,2048]{1,0:T(8,128)(2,1)} %copy-done.2) | copy-start | bytes 4718596
  161.5 1.9 %collective-permute-start.6 = (f32[64,16,128]{2,1,0:T(8,128)S(1)}, f32[64,16,128]{2,1,0:T(8,128)S(1)}, u32[]{:S(2)}, u32[]{:S(2)}) collective-permute-start(f32[64,16,128]{2,1,0:T(8,128)S(1)} %all_to_all.35.mine_ref), channel_id=1, source_target_pairs={{0,1},{1,0},{2,3},{3,2},{4,5},{5,4},{6,7},{7,6},{8,9},{9,8},{10,11... | collective-permute-start | bytes 1572872 | tf_op jit(solution)/shard_map/ppermute | solution.py:500

commit v7 on v6

--- a/solution.py
+++ b/solution.py
@@ -326,18 +326,29 @@
     *refs,
 ):
     *inputs, wide_ref, buffer_ref, sems = refs
-    copies = column_copies(
-        inverse_ref, buffer_ref, sems, inverse_ref.shape[2] - buffer_ref.shape[2]
-    )
-    if len(inputs) == 6:
-        map_ref, after_ref, inner_ref, mate_ref, keep_ref, own_ref = inputs
+    small = []
+    if len(inputs) == 13:
+        map_ref, after_ref, inner_ref, mate_ref, keep_ref, own_ref, *held, small_sems = inputs
+        given = (scaled_ref, mult_ref, dof_ref, edge_ref, basis_ref, map_ref)
+        small = [
+            pltpu.make_async_copy(source, target, small_sems.at[place])
+            for place, (source, target) in enumerate(zip(given, held))
+        ]
+        for copy in small:
+            copy.start()
+        scaled_ref, mult_ref, dof_ref, edge_ref, basis_ref, map_ref = held
         more = (basis_ref, map_ref, own_ref)
     else:
         after_ref, inner_ref, mate_ref, keep_ref = inputs
         more = (None, None, None)
+    copies = column_copies(
+        inverse_ref, buffer_ref, sems, inverse_ref.shape[2] - buffer_ref.shape[2]
+    )
 
     @pl.when(started(place_ref))
     def _():
+        for copy in small:
+            copy.wait()
         widen(basis_ref, wide_ref)
         keep, send = parts_of(place_ref, scaled_ref, wide_ref)
         half, entries = keep.shape
@@ -562,6 +573,11 @@
     def inner_solve(scaled, edge, far, *more):
         outs = [f32(subs, cases, length - width), f32(sent if more else kept, owned)]
         outs.append(f32(half, entries))
+        held = []
+        if more:
+            arrays = (scaled, multiplicity, iface_dof, edge, coarse_basis, coarse_map)
+            held = [pltpu.VMEM(array.shape, array.dtype) for array in arrays]
+            held.append(pltpu.SemaphoreType.DMA((len(arrays),)))
         if more:
             outs.append(bf16(entries, owned))
         return call(
@@ -580,11 +596,11 @@
                 *more,
                 far,
             ),
-            [SMEM] * 2 + [VMEM] * 5 + [HBM] + [VMEM] * len(more) + [ANY],
+            [SMEM] * 2 + [HBM if more else VMEM] * 5 + [HBM] * (1 + len(more)) + [ANY],
             flops=2 * scaled.size * (length - width) + slot_flops // 2,
             moved=inverse_bytes * 3 // 4,
             mib=60 if more else 50,
-            scratch_shapes=[wide, *buffers(length - width)],
+            scratch_shapes=[*held, wide, *buffers(length - width)],
         )
 
     def coarse_solve(parts, after):

time: 168 us -> 170 us (1.012)
  Pallas kernels: 39 us -> 42.6 us
  blocking collectives: 107 us -> 105 us
    pallas_call x13, Pallas kernels: 39 us -> 42.6 us  [call(): pl.pallas_call(kernel, out_shape=out_shape, in_specs=specs, compiler_para...]
    all_to_all x6, blocking collectives: 107 us -> 105 us  [by_chip(): return lax.all_to_all(value, CHIPS, 0, 0, tiled=True)]
  transfers between devices with their start and end apart: 7 -> 7, of which waited for: 4 -> 4; matrix products, arithmetic and copies ran while one was open for 0% -> 0% of each run, Pallas kernels for 14% -> 16%
where the time goes in v7:
time: 170 us; the launch traced here: 169 us
  blocking collectives  105 us (62%)
  Pallas kernels  42.6 us (25%)
  starting transfers between devices  10.9 us (6%)
  waiting for transfers between devices  8.34 us (5%)
    all_to_all x6, blocking collectives, by_chip(): return lax.all_to_all(value, CHIPS, 0, 0, tiled=True)  105 us
    pallas_call x13, Pallas kernels, call(): pl.pallas_call(kernel, out_shape=out_shape, in_specs=specs, compiler_para...  42.6 us
    ppermute x2, starting transfers between devices, far_swap(): return lax.ppermute(value, DOM, pairs)  10.6 us
    ppermute x5, waiting for transfers between devices, swap(): return lax.ppermute(value, 'c', [(0, 1), (1, 0)])  5.59 us
  transfers between devices with their start and end apart: 7, of which 4 were waited for; matrix products, arithmetic and copies ran while one was open for 0% of the time, Pallas kernels for 16%

profile of v7, /device:TPU:0, one launch (start us, length us, event | category | flops | bytes accessed | tf_op | source)
XLA Modules:
  0.0 168.9 jit_solution(5648066223265294806)
XLA Ops:
  0.6 0.1 collective-permute-start.2
  0.7 5.8 %first.1 = (bf16[8,32,1024]{2,1,0:T(8,128)(2,1)}, f32[32,2048]{1,0:T(8,128)}, f32[72,1024]{1,0:T(8,128)}, bf16[128,1024]{1,0:T(8,128)(2,1)}) custom-call(s32[1]{0:T(128)} %bitcast.place_ref, s32[8]{0:T(128)} %len_ref.9, bf16[8,32,1024]{2,1,0:T(8,128)(2,1)} %values_hbm.1, s32[8,1024]{1,0:T(8,128)} %mult_ref.3, s32[8,256]{1,0:T(8,128)} %dof_ref.7, ...), custom_call_target="tpu_custom_call" | custom-call | flops 1000000 | bytes 1048576 | tf_op jit(solution)/shard_map/first/pallas_call | solution.py:51
  6.6 8.9 %collective-permute-start.1 = (f32[72,1024]{1,0:T(8,128)}, f32[72,1024]{1,0:T(8,128)S(1)}, u32[]{:S(2)}, u32[]{:S(2)}) collective-permute-start(f32[72,1024]{1,0:T(8,128)} %get-tuple-element.22.refs_1_.far_ref), channel_id=1, source_target_pairs={{1,2},{2,1},{3,4},{4,3},{5,6},{6,5},{7,8},{8,7},{9,10},{10,9},{11,... | collective-permute-start | bytes 884744 | tf_op jit(solution)/shard_map/ppermute | solution.py:520
  15.5 10.9 %inner.2 = (f32[8,32,768]{2,1,0:T(8,128)}, f32[72,1024]{1,0:T(8,128)}, f32[16,128]{1,0:T(8,128)}, bf16[128,1024]{1,0:T(8,128)(2,1)}) custom-call(s32[1]{0:T(128)} %bitcast.place_ref, s32[8]{0:T(128)} %len_ref.9, bf16[8,32,1024]{2,1,0:T(8,128)(2,1)} %get-tuple-element.21.scaled_ref, s32[8,1024]{1,0:T(8,128)} %mult_ref.3, s32[8,256]{1,0:T(8,128)} %dof_ref.7, ...), custom_call_target="tpu_custom_call" | custom-call | flops 805306368 | bytes 12582912 | tf_op jit(solution)/shard_map/inner/pallas_call | solution.py:51
  26.4 0.0 copy-start.1
  26.5 0.0 copy-start.6
  26.5 0.0 copy-start.7
  26.5 0.0 copy-start.9
  26.5 0.0 copy-start.10
  26.5 0.1 collective-permute-start
  26.6 0.0 collective-permute-done.1.refs_0_.from_far_ref
  26.6 1.8 %collective-permute-done.near_ref.arrived_ref.from_mate_ref = f32[72,1024]{1,0:T(8,128)S(1)} collective-permute-done((f32[72,1024]{1,0:T(8,128)}, f32[72,1024]{1,0:T(8,128)S(1)}, u32[]{:S(2)}, u32[]{:S(2)}) %collective-permute-start) | collective-permute-done | bytes 294944 | tf_op jit(solution)/shard_map/ppermute | solution.py:511
  28.4 0.0 copy-done.8
  28.4 0.7 copy-done.11
  29.1 1.1 dense.2
  30.2 17.8 %all_to_all.30.after_ref.parts_ref = f32[64,16,128]{2,1,0:T(8,128)S(1)} all-to-all(f32[64,16,128]{2,1,0:T(8,128)S(1)} %dense.2), channel_id=1, replica_groups=mesh['y'=4,'z'=4,'x'=4,'c'=2] {'y','z','x'}, dimensions={0} | all-to-all | bytes 1048576 | tf_op jit(solution)/shard_map/all_to_all | solution.py:524
  48.0 0.0 copy-done.13
  48.0 0.0 copy-done.7
  48.0 0.0 copy-done.9
  48.0 0.0 copy-done.10
  48.0 0.0 copy-done.12
  48.0 0.0 copy-done.14
  48.1 0.0 copy-start
  48.1 3.7 %head.2 = (f32[32,2048]{1,0:T(8,128)S(1)}, bf16[384,2048]{1,0:T(8,128)(2,1)S(1)}, f32[2,128]{1,0:T(2,128)S(1)}) custom-call(s32[1]{0:T(128)} %bitcast.place_ref, s32[8]{0:T(128)S(1)} %copy-done.10, f32[32,2048]{1,0:T(8,128)S(1)} %copy-done.7, f32[72,1024]{1,0:T(8,128)S(1)} %copy-done.12, f32[72,1024]{1,0:T(8,128)S(1)} %copy-done.6, ...), custom_call_target="tpu_custom_call" | custom-call | flops 805306368 | bytes 1048576 | tf_op jit(solution)/shard_map/head/pallas_call | solution.py:51
  51.8 0.1 sum.2
  51.9 17.0 %all_to_all.31.rhs_ref = f32[64,16,128]{2,1,0:T(8,128)S(1)} all-to-all(f32[64,16,128]{2,1,0:T(8,128)S(1)} %sum.2), channel_id=1, replica_groups=mesh['y'=4,'z'=4,'x'=4,'c'=2] {'y','z','x'}, dimensions={0} | all-to-all | bytes 1048576 | tf_op jit(solution)/shard_map/all_to_all | solution.py:524
  68.9 0.0 collective-permute-done.2.other_ref
  68.9 1.4 solve.2
  70.4 16.7 %all_to_all.32.mine_ref = f32[64,16,128]{2,1,0:T(8,128)S(1)} all-to-all(f32[64,16,128]{2,1,0:T(8,128)S(1)} %solve.2), channel_id=1, replica_groups=mesh['y'=4,'z'=4,'x'=4,'c'=2] {'y','z','x'}, dimensions={0} | all-to-all | bytes 1048576 | tf_op jit(solution)/shard_map/all_to_all | solution.py:524
  87.1 0.0 collective-permute-start.3
  87.1 1.9 %collective-permute-done.3.other_ref = f32[64,16,128]{2,1,0:T(8,128)S(1)} collective-permute-done((f32[64,16,128]{2,1,0:T(8,128)S(1)}, f32[64,16,128]{2,1,0:T(8,128)S(1)}, u32[]{:S(2)}, u32[]{:S(2)}) %collective-permute-start.3) | collective-permute-done | bytes 524320 | tf_op jit(solution)/shard_map/ppermute | solution.py:511
  89.0 0.0 copy-done.5
  89.0 5.8 %correct.2 = (f32[8,32,1024]{2,1,0:T(8,128)}, bf16[8,32,1024]{2,1,0:T(8,128)(2,1)S(1)}, f32[32,2048]{1,0:T(8,128)S(1)}, f32[40,1024]{1,0:T(8,128)S(1)}) custom-call(s32[1]{0:T(128)} %bitcast.place_ref, s32[8,16]{1,0:T(8,128)S(1)} %copy-done.8, f32[2,128]{1,0:T(2,128)S(1)} %get-tuple-element.27.near_ref, f32[64,16,128]{2,1,0:T(8,128)S(1)} %all_to_all.32.mine_ref, ...), custom_call_target="tpu_custom_call" | custom-call | flops 1000000 | bytes 1048576 | tf_op jit(solution)/shard_map/correct/pallas_call | solution.py:51
  94.8 1.7 %collective-permute-start.5 = (f32[40,1024]{1,0:T(8,128)S(1)}, f32[40,1024]{1,0:T(8,128)S(1)}, u32[]{:S(2)}, u32[]{:S(2)}) collective-permute-start(f32[40,1024]{1,0:T(8,128)S(1)} %get-tuple-element.34.refs_0_.far_ref), channel_id=1, source_target_pairs={{1,2},{2,1},{3,4},{4,3},{5,6},{6,5},{7,8},{8,7},{9,10},{10,9},{11,... | collective-permute-start | bytes 491528 | tf_op jit(solution)/shard_map/ppermute | solution.py:520
  96.5 5.7 %inner.3 = (f32[8,32,768]{2,1,0:T(8,128)S(1)}, f32[40,1024]{1,0:T(8,128)S(1)}, f32[16,128]{1,0:T(8,128)S(1)}) custom-call(s32[1]{0:T(128)} %bitcast.place_ref, s32[8]{0:T(128)S(1)} %copy-done.10, bf16[8,32,1024]{2,1,0:T(8,128)(2,1)S(1)} %get-tuple-element.32.scaled_ref, s32[8,1024]{1,0:T(8,128)S(1)} %copy-done.5, s32[8,256]{1,0:T(8,128)S(1)} %copy-done.9, ...), custom_call_target="tpu_custom_call" | custom-call | flops 805306368 | bytes 12582912 | tf_op jit(solution)/shard_map/inner/pallas_call | solution.py:51
  102.2 0.1 collective-permute-start.4
  102.3 2.8 %collective-permute-done.5.refs_0_.from_far_ref = f32[40,1024]{1,0:T(8,128)S(1)} collective-permute-done((f32[40,1024]{1,0:T(8,128)S(1)}, f32[40,1024]{1,0:T(8,128)S(1)}, u32[]{:S(2)}, u32[]{:S(2)}) %collective-permute-start.5) | collective-permute-done | bytes 163872 | tf_op jit(solution)/shard_map/ppermute | solution.py:520
  105.0 0.0 collective-permute-done.4.arrived_ref.from_mate_ref
  105.0 1.1 dense.3
  106.1 20.3 %all_to_all.33.after_ref.parts_ref = f32[64,16,128]{2,1,0:T(8,128)S(1)} all-to-all(f32[64,16,128]{2,1,0:T(8,128)S(1)} %dense.3), channel_id=1, replica_groups=mesh['y'=4,'z'=4,'x'=4,'c'=2] {'y','z','x'}, dimensions={0} | all-to-all | bytes 1048576 | tf_op jit(solution)/shard_map/all_to_all | solution.py:524
  126.4 2.0 %head.3.refs_0_.head_ref = f32[32,2048]{1,0:T(8,128)S(1)} custom-call(s32[1]{0:T(128)} %bitcast.place_ref, s32[8]{0:T(128)S(1)} %copy-done.10, f32[32,2048]{1,0:T(8,128)S(1)} %get-tuple-element.33.edge_ref, f32[40,1024]{1,0:T(8,128)S(1)} %get-tuple-element.36.mate_ref, f32[40,1024]{1,0:T(8,128)S(1)} %get-tuple-element.34.refs_0_.far_ref, ...), custom_call_target="tpu_custom_call" | custom-call | flops 805306368 | bytes 1048576 | tf_op jit(solution)/shard_map/head/pallas_call | solution.py:51
  128.4 0.1 sum.3
  128.6 17.0 %all_to_all.34.rhs_ref = f32[64,16,128]{2,1,0:T(8,128)S(1)} all-to-all(f32[64,16,128]{2,1,0:T(8,128)S(1)} %sum.3), channel_id=1, replica_groups=mesh['y'=4,'z'=4,'x'=4,'c'=2] {'y','z','x'}, dimensions={0} | all-to-all | bytes 1048576 | tf_op jit(solution)/shard_map/all_to_all | solution.py:524
  145.5 1.4 solve.3
  147.0 16.5 %all_to_all.35.mine_ref = f32[64,16,128]{2,1,0:T(8,128)S(1)} all-to-all(f32[64,16,128]{2,1,0:T(8,128)S(1)} %solve.3), channel_id=1, replica_groups=mesh['y'=4,'z'=4,'x'=4,'c'=2] {'y','z','x'}, dimensions={0} | all-to-all | bytes 1048576 | tf_op jit(solution)/shard_map/all_to_all | solution.py:524
  163.5 0.0 collective-permute-start.6
  163.5 1.9 %collective-permute-done.6.other_ref = f32[64,16,128]{2,1,0:T(8,128)S(1)} collective-permute-done((f32[64,16,128]{2,1,0:T(8,128)S(1)}, f32[64,16,128]{2,1,0:T(8,128)S(1)}, u32[]{:S(2)}, u32[]{:S(2)}) %collective-permute-start.6) | collective-permute-done | bytes 524320 | tf_op jit(solution)/shard_map/ppermute | solution.py:511
  165.4 3.4 %correct.3 = f32[8,32,1024]{2,1,0:T(8,128)} custom-call(s32[1]{0:T(128)} %bitcast.place_ref, s32[8,16]{1,0:T(8,128)S(1)} %copy-done.8, f32[2,128]{1,0:T(2,128)S(1)} %get-tuple-element.27.near_ref, f32[64,16,128]{2,1,0:T(8,128)S(1)} %all_to_all.35.mine_ref, f32[64,16,128]{2,1,0:T(8,128)S(1)} %collective-permute-done.6.other_ref, ...), custom_call_target="tpu_custom_call" | custom-call | flops 1000000 | bytes 1048576 | tf_op jit(solution)/shard_map/correct/pallas_call | solution.py:51
  (15 shorter events, 0.0 us)
Async XLA Ops:
  0.6 68.3 %collective-permute-start.2 = (f32[64,8192]{1,0:T(8,128)}, f32[64,8192]{1,0:T(8,128)S(1)}, u32[]{:S(2)}, u32[]{:S(2)}) collective-permute-start(f32[64,8192]{1,0:T(8,128)} %mine_ref.3), channel_id=1, source_target_pairs={{0,1},{1,0},{2,3},{3,2},{4,5},{5,4},{6,7},{7,6},{8,9},{9,8},{10,11... | collective-permute-start | bytes 6291464 | tf_op jit(solution)/shard_map/ppermute | solution.py:511
  6.6 20.0 %collective-permute-start.1 = (f32[72,1024]{1,0:T(8,128)}, f32[72,1024]{1,0:T(8,128)S(1)}, u32[]{:S(2)}, u32[]{:S(2)}) collective-permute-start(f32[72,1024]{1,0:T(8,128)} %get-tuple-element.22.refs_1_.far_ref), channel_id=1, source_target_pairs={{1,2},{2,1},{3,4},{4,3},{5,6},{6,5},{7,8},{8,7},{9,10},{10,9},{11,... | collective-permute-start | bytes 884744 | tf_op jit(solution)/shard_map/ppermute | solution.py:520
  15.5 12.9 %copy-start.8 = (s32[8,16]{1,0:T(8,128)S(1)}, s32[8,16]{1,0:T(8,128)}, u32[]{:S(2)}) copy-start(s32[8,16]{1,0:T(8,128)} %own_ref.7) | copy-start | bytes 1540
  15.5 32.5 %copy-start.13 = (bf16[128,1024]{1,0:T(8,128)(2,1)S(1)}, bf16[128,1024]{1,0:T(8,128)(2,1)}, u32[]{:S(2)}) copy-start(bf16[128,1024]{1,0:T(8,128)(2,1)} %get-tuple-element.26.refs_2_) | copy-start | bytes 786436
  26.4 21.6 %copy-start.1 = (bf16[8,16,1024]{2,1,0:T(8,128)(2,1)S(1)}, bf16[8,16,1024]{2,1,0:T(8,128)(2,1)}, u32[]{:S(2)}) copy-start(bf16[8,16,1024]{2,1,0:T(8,128)(2,1)} %basis_ref.7) | copy-start | bytes 786436
  26.5 21.5 %copy-start.6 = (f32[72,1024]{1,0:T(8,128)S(1)}, f32[72,1024]{1,0:T(8,128)}, u32[]{:S(2)}) copy-start(f32[72,1024]{1,0:T(8,128)} %get-tuple-element.22.refs_1_.far_ref) | copy-start | bytes 884740
  26.5 21.5 %copy-start.7 = (f32[32,2048]{1,0:T(8,128)S(1)}, f32[32,2048]{1,0:T(8,128)}, u32[]{:S(2)}) copy-start(f32[32,2048]{1,0:T(8,128)} %get-tuple-element.20.edge_ref) | copy-start | bytes 786436
  26.5 21.5 %copy-start.9 = (s32[8,256]{1,0:T(8,128)S(1)}, s32[8,256]{1,0:T(8,128)}, u32[]{:S(2)}) copy-start(s32[8,256]{1,0:T(8,128)} %dof_ref.7) | copy-start | bytes 24580
  26.5 21.5 %copy-start.10 = (s32[8]{0:T(128)S(1)}, s32[8]{0:T(128)}, u32[]{:S(2)}) copy-start(s32[8]{0:T(128)} %len_ref.9) | copy-start | bytes 100
  26.5 1.9 %collective-permute-start = (f32[72,1024]{1,0:T(8,128)}, f32[72,1024]{1,0:T(8,128)S(1)}, u32[]{:S(2)}, u32[]{:S(2)}) collective-permute-start(f32[72,1024]{1,0:T(8,128)} %get-tuple-element.23.mate_ref), channel_id=1, source_target_pairs={{0,1},{1,0},{2,3},{3,2},{4,5},{5,4},{6,7},{7,6},{8,9},{9,8},{10,11... | collective-permute-start | bytes 884744 | tf_op jit(solution)/shard_map/ppermute | solution.py:511
  28.4 0.7 copy-start.11
  29.1 19.0 %copy-start.12 = (f32[72,1024]{1,0:T(8,128)S(1)}, f32[72,1024]{1,0:T(8,128)}, u32[]{:S(2)}) copy-start(f32[72,1024]{1,0:T(8,128)} %get-tuple-element.23.mate_ref) | copy-start | bytes 884740
  29.1 19.0 %copy-start.14 = (bf16[128,1024]{1,0:T(8,128)(2,1)S(1)}, bf16[128,1024]{1,0:T(8,128)(2,1)}, u32[]{:S(2)}) copy-start(bf16[128,1024]{1,0:T(8,128)(2,1)} %get-tuple-element.25.refs_1_) | copy-start | bytes 786436
  48.1 20.9 %copy-start = (f32[64,8192]{1,0:T(8,128)S(1)}, f32[64,8192]{1,0:T(8,128)}, u32[]{:S(2)}) copy-start(f32[64,8192]{1,0:T(8,128)} %mine_ref.3) | copy-start | bytes 6291460
  51.8 18.6 %copy-start.2 = (bf16[384,2048]{1,0:T(8,128)(2,1)}, bf16[384,2048]{1,0:T(8,128)(2,1)S(1)}, u32[]{:S(2)}) copy-start(bf16[384,2048]{1,0:T(8,128)(2,1)S(1)} %get-tuple-element.29.shared_ref) | copy-start | bytes 4718596
  68.9 20.1 %copy-start.4 = (f32[8,32,768]{2,1,0:T(8,128)S(1)}, f32[8,32,768]{2,1,0:T(8,128)}, u32[]{:S(2)}) copy-start(f32[8,32,768]{2,1,0:T(8,128)} %get-tuple-element.30.inner_ref) | copy-start | bytes 2359300
  68.9 20.1 %copy-start.5 = (s32[8,1024]{1,0:T(8,128)S(1)}, s32[8,1024]{1,0:T(8,128)}, u32[]{:S(2)}) copy-start(s32[8,1024]{1,0:T(8,128)} %mult_ref.3) | copy-start | bytes 98308
  87.1 1.9 %collective-permute-start.3 = (f32[64,16,128]{2,1,0:T(8,128)S(1)}, f32[64,16,128]{2,1,0:T(8,128)S(1)}, u32[]{:S(2)}, u32[]{:S(2)}) collective-permute-start(f32[64,16,128]{2,1,0:T(8,128)S(1)} %all_to_all.32.mine_ref), channel_id=1, source_target_pairs={{0,1},{1,0},{2,3},{3,2},{4,5},{5,4},{6,7},{7,6},{8,9},{9,8},{10,11... | collective-permute-start | bytes 1572872 | tf_op jit(solution)/shard_map/ppermute | solution.py:511
  94.8 10.3 %collective-permute-start.5 = (f32[40,1024]{1,0:T(8,128)S(1)}, f32[40,1024]{1,0:T(8,128)S(1)}, u32[]{:S(2)}, u32[]{:S(2)}) collective-permute-start(f32[40,1024]{1,0:T(8,128)S(1)} %get-tuple-element.34.refs_0_.far_ref), channel_id=1, source_target_pairs={{1,2},{2,1},{3,4},{4,3},{5,6},{6,5},{7,8},{8,7},{9,10},{10,9},{11,... | collective-permute-start | bytes 491528 | tf_op jit(solution)/shard_map/ppermute | solution.py:520
  102.2 2.8 %collective-permute-start.4 = (f32[40,1024]{1,0:T(8,128)S(1)}, f32[40,1024]{1,0:T(8,128)S(1)}, u32[]{:S(2)}, u32[]{:S(2)}) collective-permute-start(f32[40,1024]{1,0:T(8,128)S(1)} %get-tuple-element.36.mate_ref), channel_id=1, source_target_pairs={{0,1},{1,0},{2,3},{3,2},{4,5},{5,4},{6,7},{7,6},{8,9},{9,8},{10,11... | collective-permute-start | bytes 491528 | tf_op jit(solution)/shard_map/ppermute | solution.py:511
  145.5 19.8 %copy-start.3 = (bf16[384,2048]{1,0:T(8,128)(2,1)S(1)}, bf16[384,2048]{1,0:T(8,128)(2,1)}, u32[]{:S(2)}) copy-start(bf16[384,2048]{1,0:T(8,128)(2,1)} %copy-done.2) | copy-start | bytes 4718596
  163.5 1.9 %collective-permute-start.6 = (f32[64,16,128]{2,1,0:T(8,128)S(1)}, f32[64,16,128]{2,1,0:T(8,128)S(1)}, u32[]{:S(2)}, u32[]{:S(2)}) collective-permute-start(f32[64,16,128]{2,1,0:T(8,128)S(1)} %all_to_all.35.mine_ref), channel_id=1, source_target_pairs={{0,1},{1,0},{2,3},{3,2},{4,5},{5,4},{6,7},{7,6},{8,9},{9,8},{10,11... | collective-permute-start | bytes 1572872 | tf_op jit(solution)/shard_map/ppermute | solution.py:511
